TPU v7x, 32 devices: a whole 2x2x4 slice. The times are simulated.
32 devices in a mesh: seq: 8 (over z, x), mp: 4 (over y, core).
Axes of the slice: x: 2, y: 2, z: 4, core: 2. Of those that a mesh axis runs over, the one named last changes fastest.
Arguments:
- tokens_in: float32 [1024, 2048], P('seq'), may hold values from -6 to 6
- cotangent: float32 [1024, 2048], P('seq'), may hold values from -6 to 6
- lengths: int32 [4], replicated, may hold values from 8 to 960, as said below
- lower_bound: float32 [2048], P('mp'), may hold values from 0.94 to 1, as said below
- query_weight: float32 [2048, 2048], P(None, 'mp'), may hold values from -0.125 to 0.125
- forget_weight: float32 [2048, 2048], P(None, 'mp'), may hold values from -0.125 to 0.125
- input_weight: float32 [2048, 2048], P(None, 'mp'), may hold values from -0.125 to 0.125
- gate_weight: float32 [2048, 2048], P(None, 'mp'), may hold values from -0.125 to 0.125
- out_weight: float32 [2048, 2048], P('mp'), may hold values from -0.25 to 0.25
- swiglu_gate: float32 [2048, 5632], P(None, 'mp'), may hold values from -0.125 to 0.125
- swiglu_up: float32 [2048, 5632], P(None, 'mp'), may hold values from -0.125 to 0.125
- swiglu_down: float32 [5632, 2048], P('mp'), may hold values from -0.15625 to 0.15625
- first_gain: float32 [2048], replicated, may hold values from 0.5 to 1.5
- group_gain: float32 [2048], P('mp'), may hold values from 0.5 to 1.5
- second_gain: float32 [2048], replicated, may hold values from 0.5 to 1.5
Outputs:
- output: float32 [1024, 2048], P(('seq', 'mp'))
- grad_tokens: float32 [1024, 2048], P(('seq', 'mp'))
- grad_query: float32 [2048, 2048], P('seq', 'mp')
- grad_forget: float32 [2048, 2048], P('seq', 'mp')
- grad_inputs: float32 [2048, 2048], P('seq', 'mp')
- grad_gate: float32 [2048, 2048], P('seq', 'mp')
- grad_out: float32 [2048, 2048], P('mp', 'seq')
- grad_swiglu_gate: float32 [2048, 5632], P('seq', 'mp')
- grad_swiglu_up: float32 [2048, 5632], P('seq', 'mp')
- grad_swiglu_down: float32 [5632, 2048], P('mp', 'seq')
- grad_first_gain: float32 [2048], P('seq')
- grad_group_gain: float32 [2048], P(('mp', 'seq'))
- grad_second_gain: float32 [2048], P('seq')
Inputs may be any that keep to these rules, and one draw needn't show every extreme that they name: 4 sequences packed in order, their lengths summing to 1024; one of them, at a seed-drawn place, is exactly 960 long; every other is at least max(1, 8) long. `lower_bound`: the same within each head's channels up to a factor of two.
All inputs are finite; a program needn't handle non-finite values.
Results may differ from a plain program's by a relative error of at most 0.0003.
Values sent between devices are 32-bit elements; how exact they have to be, the bound alone decides.
A program may use at most 256 MiB of HBM per device.

v0:
```python
from functools import partial

import jax
import jax.numpy as jnp
from jax import lax
from jax.sharding import PartitionSpec as P

HDIM = 128


TOP_PRECISION = lax.Precision.HIGHEST
norm_eps = 1e-06
group_eps = 1e-05


def prefix(part, axis, combine, identity, reverse):
    count = lax.axis_size(axis)
    place = lax.axis_index(axis)
    ahead = count - 1 - place if reverse else place
    gathered = jax.tree.map(lambda a: lax.all_gather(a, axis), part)
    state = jax.tree.map(lambda a, e: jnp.zeros_like(a) + jnp.asarray(e, a.dtype), part, identity)

    def one(hop, state):
        source = count - 1 - hop if reverse else hop
        return combine(
            state, jax.tree.map(lambda a: lax.dynamic_index_in_dim(a, source, 0, False), gathered)
        )

    return lax.fori_loop(0, ahead, one, state)


def matmul(left, right):
    return jnp.dot(left, right, precision=TOP_PRECISION)


def rms_norm(entries, gain):
    return entries * lax.rsqrt(jnp.mean(entries * entries, -1, keepdims=True) + norm_eps) * gain


def end_update(carried_state, key_vecs, value_rows, segment, carry_marker, log_decay):
    trailing_decay = jnp.exp(log_decay[-1])
    in_last = (segment == segment[-1]).astype(key_vecs.dtype)
    weighted_terms = key_vecs * jnp.exp(log_decay[-1][None] - log_decay) * in_last[:, None, None]
    return carried_state * (trailing_decay * carry_marker[-1])[:, :, None] + jnp.einsum(
        "bef,bey->efy", weighted_terms, value_rows, precision=TOP_PRECISION
    )


def out_step(carried_state, pieces):
    query_rows, key_vecs, value_rows, segment, flag_bool = pieces
    carry_marker = flag_bool.astype(key_vecs.dtype)
    log_decay = jnp.cumsum(jnp.log1p(-key_vecs), 0)
    growth_factor = jnp.exp(log_decay)
    scores = jnp.einsum(
        "thk,shk->hts",
        query_rows * growth_factor,
        key_vecs * jnp.exp(-log_decay),
        precision=TOP_PRECISION,
    )
    places = jnp.arange(key_vecs.shape[0])
    allowed = (places[:, None] >= places[None, :]) & (segment[:, None] == segment[None, :])
    scores = jnp.where(allowed[None], scores, 0.0)
    output_rows = jnp.einsum("hts,shv->thv", scores, value_rows, precision=TOP_PRECISION)
    output_rows = output_rows + jnp.einsum(
        "dsj,sjp->dsp",
        query_rows * growth_factor * carry_marker[:, None, None],
        carried_state,
        precision=TOP_PRECISION,
    )
    return (
        end_update(carried_state, key_vecs, value_rows, segment, carry_marker, log_decay),
        output_rows,
    )


def end_step(carried_state, pieces):
    key_vecs, value_rows, segment, flag_bool = pieces
    carry_marker = flag_bool.astype(key_vecs.dtype)
    log_decay = jnp.cumsum(jnp.log1p(-key_vecs), 0)
    return (end_update(carried_state, key_vecs, value_rows, segment, carry_marker, log_decay), None)


def block_flags(segment, segment_before, block_size):
    block_count = segment.shape[0] // block_size
    shifted = jnp.concatenate([jnp.reshape(segment_before, (1,)), segment[:-1]])
    first_segs = shifted.reshape(block_count, block_size)[:, 0]
    blocked = segment.reshape(block_count, block_size)
    return (blocked, blocked == first_segs[:, None])


def split_blocks(entries, block_size):
    return entries.reshape(
        entries.shape[0] // block_size, block_size, entries.shape[1], entries.shape[2]
    )


def mixer_in(normed, query_weight, forget_weight, input_weight, gate_weight, lower_bound):
    token_count = normed.shape[0]
    query_rows = jax.nn.silu(matmul(normed, query_weight)).reshape(token_count, -1, HDIM)
    key_vecs = ((1.0 - lower_bound) * jax.nn.sigmoid(-matmul(normed, forget_weight))).reshape(
        token_count, -1, HDIM
    )
    value_rows = matmul(normed, input_weight).reshape(token_count, -1, HDIM)
    gate_in = matmul(normed, gate_weight)
    return (query_rows, key_vecs, value_rows, gate_in)


def summarize(key_vecs, value_rows, segment, segment_before):
    block_size = min(512, key_vecs.shape[0])
    blocked, flags = block_flags(segment, segment_before, block_size)
    start = jnp.zeros((key_vecs.shape[1], HDIM, HDIM), key_vecs.dtype)
    end_states, _ = lax.scan(
        end_step,
        start,
        (split_blocks(key_vecs, block_size), split_blocks(value_rows, block_size), blocked, flags),
    )
    through = jnp.exp(jnp.sum(jnp.log1p(-key_vecs), 0)) * (segment[-1] == segment_before).astype(
        key_vecs.dtype
    )
    return (end_states, through)


def mixer_out(
    query_rows,
    key_vecs,
    value_rows,
    gate_in,
    group_gain,
    out_weight,
    incoming,
    segment,
    segment_before,
):
    token_count = query_rows.shape[0]
    block_size = min(512, token_count)
    blocked, flags = block_flags(segment, segment_before, block_size)
    _, output_rows = lax.scan(
        out_step,
        incoming,
        (
            split_blocks(query_rows, block_size),
            split_blocks(key_vecs, block_size),
            split_blocks(value_rows, block_size),
            blocked,
            flags,
        ),
    )
    raw = output_rows.reshape(token_count, -1, HDIM)
    normed_raw = raw * lax.rsqrt(jnp.mean(raw * raw, -1, keepdims=True) + group_eps)
    mixer = normed_raw.reshape(token_count, -1) * group_gain * jax.nn.silu(gate_in)
    return matmul(mixer, out_weight)


def feed_forward(normed, swiglu_gate, swiglu_up, swiglu_down):
    hidden = jax.nn.silu(matmul(normed, swiglu_gate)) * matmul(normed, swiglu_up)
    return matmul(hidden, swiglu_down)


def forward_combine(earlier, later):
    early_decay, early_state = earlier
    late_decay, late_state = later
    return (early_decay * late_decay, late_decay[:, :, None] * early_state + late_state)


def backward_combine(earlier, later):
    early_decay, early_grad = earlier
    late_decay, late_grad = later
    return (early_decay * late_decay, late_grad + late_decay[:, :, None] * early_grad)


def shards(
    tokens_in,
    cotangent,
    lengths,
    lower_bound,
    query_weight,
    forget_weight,
    input_weight,
    gate_weight,
    out_weight,
    swiglu_gate,
    swiglu_up,
    swiglu_down,
    first_gain,
    group_gain,
    second_gain,
):
    token_count = tokens_in.shape[0]
    share_rows = token_count // lax.axis_size("mp")
    share_start = lax.axis_index("mp") * share_rows
    start_row = lax.axis_index("seq") * token_count
    positions = start_row + jnp.arange(token_count, dtype=jnp.int32)
    offsets = jnp.cumsum(lengths) - lengths
    segment = jnp.sum((positions[:, None] >= offsets[None, :]).astype(jnp.int32), 1) - 1
    segment_before = jnp.sum((start_row - 1 >= offsets).astype(jnp.int32)) - 1
    normed_one, first_back = jax.vjp(rms_norm, tokens_in, first_gain)
    projected, mixin_back = jax.vjp(
        partial(mixer_in, lower_bound=lower_bound),
        normed_one,
        query_weight,
        forget_weight,
        input_weight,
        gate_weight,
    )
    query_rows, key_vecs, value_rows, gate_in = projected
    summary, summary_back = jax.vjp(
        partial(summarize, segment=segment, segment_before=segment_before), key_vecs, value_rows
    )
    end_states, through = summary
    _, incoming = prefix(
        (through, end_states),
        "seq",
        forward_combine,
        (jnp.ones_like(through), jnp.zeros_like(end_states)),
        False,
    )
    mixer_part, mixout_back = jax.vjp(
        partial(mixer_out, segment=segment, segment_before=segment_before),
        query_rows,
        key_vecs,
        value_rows,
        gate_in,
        group_gain,
        out_weight,
        incoming,
    )
    residual = tokens_in + lax.psum(mixer_part, "mp")
    normed_two, second_back = jax.vjp(rms_norm, residual, second_gain)
    ffn_part, ffn_backward = jax.vjp(feed_forward, normed_two, swiglu_gate, swiglu_up, swiglu_down)
    output_full = residual + lax.psum(ffn_part, "mp")
    output = lax.dynamic_slice_in_dim(output_full, share_start, share_rows, 0)
    grad_normed_two, grad_sgate, grad_sup, grad_sdown = ffn_backward(cotangent)
    grad_normed_two = lax.psum(grad_normed_two, "mp")
    grad_res_norm, grad_second = second_back(grad_normed_two)
    grad_residual = cotangent + grad_res_norm
    (
        grad_queries,
        grad_keys_out,
        grad_values_out,
        grad_gate_in,
        grad_group,
        grad_outw,
        grad_incoming,
    ) = mixout_back(grad_residual)
    _, later_grad = prefix(
        (through, grad_incoming),
        "seq",
        backward_combine,
        (jnp.ones_like(through), jnp.zeros_like(grad_incoming)),
        True,
    )
    grad_through = jnp.sum(later_grad * incoming, -1)
    grad_keys_end, grad_values_end = summary_back((later_grad, grad_through))
    grad_normed_one, grad_qw, grad_fw, grad_iw, grad_gw = mixin_back(
        (
            grad_queries,
            grad_keys_out + grad_keys_end,
            grad_values_out + grad_values_end,
            grad_gate_in,
        )
    )
    grad_normed_one = lax.psum(grad_normed_one, "mp")
    grad_tok_norm, grad_first = first_back(grad_normed_one)
    grad_tokens = lax.dynamic_slice_in_dim(
        grad_residual + grad_tok_norm, share_start, share_rows, 0
    )
    row_sums = (
        lax.psum_scatter(grad_qw, "seq", scatter_dimension=0, tiled=True),
        lax.psum_scatter(grad_fw, "seq", scatter_dimension=0, tiled=True),
        lax.psum_scatter(grad_iw, "seq", scatter_dimension=0, tiled=True),
        lax.psum_scatter(grad_gw, "seq", scatter_dimension=0, tiled=True),
        lax.psum_scatter(grad_sgate, "seq", scatter_dimension=0, tiled=True),
        lax.psum_scatter(grad_sup, "seq", scatter_dimension=0, tiled=True),
        lax.psum_scatter(grad_first, "seq", scatter_dimension=0, tiled=True),
        lax.psum_scatter(grad_second, "seq", scatter_dimension=0, tiled=True),
        lax.psum_scatter(grad_group, "seq", scatter_dimension=0, tiled=True),
    )
    col_sums = (
        lax.psum_scatter(grad_outw, "seq", scatter_dimension=1, tiled=True),
        lax.psum_scatter(grad_sdown, "seq", scatter_dimension=1, tiled=True),
    )
    return (
        output,
        grad_tokens,
        row_sums[0],
        row_sums[1],
        row_sums[2],
        row_sums[3],
        col_sums[0],
        row_sums[4],
        row_sums[5],
        col_sums[1],
        row_sums[6],
        row_sums[8],
        row_sums[7],
    )


def solution(mesh):
    in_specs = (
        P("seq", None),
        P("seq", None),
        P(),
        P("mp"),
        P(None, "mp"),
        P(None, "mp"),
        P(None, "mp"),
        P(None, "mp"),
        P("mp", None),
        P(None, "mp"),
        P(None, "mp"),
        P("mp", None),
        P(),
        P("mp"),
        P(),
    )
    out_specs = (
        P(("seq", "mp"), None),
        P(("seq", "mp"), None),
        P("seq", "mp"),
        P("seq", "mp"),
        P("seq", "mp"),
        P("seq", "mp"),
        P("mp", "seq"),
        P("seq", "mp"),
        P("seq", "mp"),
        P("mp", "seq"),
        P("seq"),
        P(("mp", "seq")),
        P("seq"),
    )
    return jax.shard_map(shards, mesh=mesh, in_specs=in_specs, out_specs=out_specs, check_vma=False)
```

profile of v0, /device:TPU:8, one launch (start us, length us, event | category | flops | bytes accessed | tf_op | source)
XLA Modules:
  0.0 1427.4 jit_solution(969566281865800248)
XLA Ops:
  7.3 1.5 multiply_reduce_fusion.5
  14.6 5.0 convolution_bitcast_fusion
  19.7 3.2 fusion.71
  23.0 5.6 log-plus-one_reduce_fusion
  33.2 25.7 %all_gather.18 = f32[8,4,128]{2,1,0:T(4,128)S(1)} all-gather(f32[1,4,128]{2,1,0:T(4,128)S(1)} %multiply_bitcast_fusion), channel_id=1, replica_groups=mesh['seq'=8,'mp'=4] {'seq'}, dimensions={0}, use_global_device_ids=true | all-gather | bytes 18432 | tf_op jit(solution)/shard_map/all_gather | solution.py:20
  60.9 4.7 fusion.118
  65.7 16.3 %all-gather.5.cloned.1.call-done = f32[32,128,128]{2,1,0:T(8,128)} async-done(((f32[4,128,128]{2,1,0:T(8,128)}), f32[32,128,128]{2,1,0:T(8,128)}) %all-gather.5.cloned.1.call-update) | async-done | bytes 2097168 | tf_op jit(solution)/shard_map/all_gather | solution.py:20
  82.0 2.3 while.16
  84.4 1.6 multiply_reduce_fusion.11
  86.7 1.8 copy.300
  88.5 5.6 fusion.92
  94.4 15.1 %fusion.122 = f32[128,1408]{1,0:T(8,128)} fusion(f32[128,2048]{1,0:T(8,128)S(1)} %copy-done.13, f32[1408,2048]{1,0:T(8,128)} %param.30), kind=kOutput, calls=%fused_computation.194 | convolution fusion | flops 4429185024 | bytes 13303808 | tf_op jit(solution)/shard_map/transpose(jvp())/dot_general | solution.py:33
  109.4 25.2 %all-reduce.13.cloned.1.call-done = f32[128,2048]{1,0:T(8,128)} async-done(((f32[128,2048]{1,0:T(8,128)}), f32[128,2048]{1,0:T(8,128)}) %all-reduce.13.cloned.1.call-update) | async-done | bytes 1048592 | tf_op jit(solution)/shard_map/psum | solution.py:227
  134.7 1.4 multiply_reduce_fusion.4
  136.1 9.5 fusion.10
  145.7 9.8 fusion.9
  155.6 11.8 fusion.20
  167.5 13.3 convolution_add_fusion.3
  180.9 36.6 %all-reduce.15.cloned.1.call-done = f32[128,2048]{1,0:T(8,128)} async-done(((f32[128,2048]{1,0:T(8,128)}), f32[128,2048]{1,0:T(8,128)}) %all-reduce.15.cloned.1.call-update) | async-done | bytes 1048592 | tf_op jit(solution)/shard_map/psum | solution.py:233
  217.4 2.2 multiply_reduce_fusion
  219.7 1.8 fusion.3
  221.5 5.9 multiply_reduce_fusion.6
  227.5 1.8 copy.301
  232.1 2.3 convolution_add_fusion.5
  234.5 1.4 fusion.41
  235.8 1.8 copy.286
  237.6 2.3 fusion.74
  240.0 10.7 fusion.24
  251.7 1.8 copy.291
  253.5 1.6 convolution_select_fusion
  255.8 1.6 fusion.126
  258.2 1.4 fusion.124
  260.5 2.2 convolution_add_fusion.6
  262.7 7.5 fusion.123
  270.2 14.0 all-gather.7.cloned.1.call-done
  284.3 6.0 while.17
  290.6 2.3 fusion.38
  292.9 2.4 convolution_add_fusion.4
  295.3 1.8 copy.295
  297.1 1.4 bitcast_multiply_fusion.12
  298.6 7.1 convolution_add_fusion.2
  306.2 1.8 fusion.51
  308.1 1.4 fusion.44
  309.6 4.8 convolution_add_fusion.1
  314.5 5.4 convolution_add_fusion
  320.0 6.3 fusion.91
  327.3 5.1 fusion.115
  332.5 6.2 fusion.104
  338.8 5.2 fusion.117
  344.3 6.2 fusion.116
  350.5 13.4 fusion.8
  364.2 13.2 fusion.7
  377.5 12.9 fusion.22
  393.0 2.4 multiply_reduce_fusion.1
  395.4 33.7 %all-reduce.7 = (f32[2048]{0:T(1024)S(1)}, f32[512]{0:T(512)S(1)}, f32[2048]{0:T(1024)S(1)}) all-reduce(f32[2048]{0:T(1024)S(1)} %get-tuple-element.382, f32[512]{0:T(512)S(1)} %copy-done.50, f32[2048]{0:T(1024)S(1)} %copy-done.47), channel_id=12, replica_groups=mesh['seq'=8,'mp'=4] {'seq'}, use_global_device_ids=true, to_apply=%region_35.36.clone | all-reduce | flops 4608 | bytes 36864
  431.0 1.9 fusion.33
  432.9 32.3 %reduce-scatter.17.cloned.1.call-done = f32[512,256]{1,0:T(8,128)} async-done(((f32[512,2048]{1,0:T(8,128)}), f32[512,256]{1,0:T(8,128)}) %reduce-scatter.17.cloned.1.call-update) | async-done | bytes 524304 | tf_op jit(solution)/shard_map/reduce_scatter | solution.py:279
  465.2 91.9 %reduce-scatter.15.cloned.1.call-done = f32[256,512]{1,0:T(8,128)} async-done(((f32[2048,512]{1,0:T(8,128)}), f32[256,512]{1,0:T(8,128)}) %reduce-scatter.15.cloned.1.call-update) | async-done | bytes 524304 | tf_op jit(solution)/shard_map/reduce_scatter | solution.py:271
  557.1 92.3 %reduce-scatter.9.cloned.1.call-done = f32[256,512]{1,0:T(8,128)} async-done(((f32[2048,512]{1,0:T(8,128)}), f32[256,512]{1,0:T(8,128)}) %reduce-scatter.9.cloned.1.call-update) | async-done | bytes 524304 | tf_op jit(solution)/shard_map/reduce_scatter | solution.py:268
  649.5 92.1 %reduce-scatter.11.cloned.1.call-done = f32[256,512]{1,0:T(8,128)} async-done(((f32[2048,512]{1,0:T(8,128)}), f32[256,512]{1,0:T(8,128)}) %reduce-scatter.11.cloned.1.call-update) | async-done | bytes 524304 | tf_op jit(solution)/shard_map/reduce_scatter | solution.py:269
  741.5 92.2 %reduce-scatter.13.cloned.1.call-done = f32[256,512]{1,0:T(8,128)} async-done(((f32[2048,512]{1,0:T(8,128)}), f32[256,512]{1,0:T(8,128)}) %reduce-scatter.13.cloned.1.call-update) | async-done | bytes 524304 | tf_op jit(solution)/shard_map/reduce_scatter | solution.py:270
  833.7 194.8 %reduce-scatter.19.cloned.1.call-done = f32[256,1408]{1,0:T(8,128)} async-done(((f32[2048,1408]{1,0:T(8,128)}), f32[256,1408]{1,0:T(8,128)}) %reduce-scatter.19.cloned.1.call-update) | async-done | bytes 1441808 | tf_op jit(solution)/shard_map/reduce_scatter | solution.py:272
  1028.5 195.7 %reduce-scatter.21.cloned.1.call-done = f32[256,1408]{1,0:T(8,128)} async-done(((f32[2048,1408]{1,0:T(8,128)}), f32[256,1408]{1,0:T(8,128)}) %reduce-scatter.21.cloned.1.call-update) | async-done | bytes 1441808 | tf_op jit(solution)/shard_map/reduce_scatter | solution.py:273
  1224.2 196.4 %reduce-scatter.23.cloned.1.call-done = f32[1408,256]{1,0:T(8,128)} async-done(((f32[1408,2048]{1,0:T(8,128)}), f32[1408,256]{1,0:T(8,128)}) %reduce-scatter.23.cloned.1.call-update) | async-done | bytes 1441808 | tf_op jit(solution)/shard_map/reduce_scatter | solution.py:280
  (211 shorter events, 32.5 us)
Async XLA Ops:
  7.2 12.5 copy-start
  7.2 12.5 copy-start.43
  7.2 74.8 %all-gather.5.cloned.1.call-start = ((), (), s32[]{:S(2)}) async-start(), calls=%async_computation.18 | async-start | bytes 2359296 | tf_op jit(solution)/shard_map/all_gather | solution.py:20
  8.7 14.1 copy-start.51
  8.7 330.1 %copy-start.45 = (f32[128]{0:T(128)}, f32[128]{0:T(128)S(1)}, u32[]{:S(2)}) copy-start(f32[128]{0:T(128)S(1)} %fusion.96) | copy-start | bytes 1540
  11.5 8.1 copy-start.6
  19.7 233.9 %copy-start.14 = (f32[16,4,8,128]{3,2,1,0:T(8,128)}, f32[16,4,8,128]{3,2,1,0:T(8,128)S(1)}, u32[]{:S(2)}) copy-start(f32[16,4,8,128]{3,2,1,0:T(8,128)S(1)} %convolution_bitcast_fusion) | copy-start | bytes 786436
  23.0 7.0 copy-start.35
  28.6 37.0 %copy-start.8 = (f32[128,4,128]{2,1,0:T(4,128)}, f32[128,4,128]{2,1,0:T(4,128)S(1)}, u32[]{:S(2)}) copy-start(f32[128,4,128]{2,1,0:T(4,128)S(1)} %squeeze.133) | copy-start | bytes 786436
  28.9 36.8 %copy-start.11 = (f32[128,4,128]{2,1,0:T(4,128)}, f32[128,4,128]{2,1,0:T(4,128)S(1)}, u32[]{:S(2)}) copy-start(f32[128,4,128]{2,1,0:T(4,128)S(1)} %fusion.69) | copy-start | bytes 786436
  30.0 35.7 %copy-start.19 = (f32[128,4,128]{2,1,0:T(4,128)}, f32[128,4,128]{2,1,0:T(4,128)S(1)}, u32[]{:S(2)}) copy-start(f32[128,4,128]{2,1,0:T(4,128)S(1)} %get-tuple-element.425) | copy-start | bytes 786436
  31.3 103.3 %all-reduce.13.cloned.1.call-start = ((), (), s32[]{:S(2)}) async-start(), calls=%async_computation.8 | async-start | bytes 2097152 | tf_op jit(solution)/shard_map/psum | solution.py:227
  32.2 49.8 %copy-start.26 = (f32[128,4,128]{0,2,1:T(8,128)}, f32[128,4,128]{0,2,1:T(8,128)S(1)}, u32[]{:S(2)}) copy-start(f32[128,4,128]{0,2,1:T(8,128)S(1)} %copy.292) | copy-start | bytes 786436
  33.2 48.8 %copy-start.27 = (f32[128,4,128]{0,2,1:T(8,128)}, f32[128,4,128]{0,2,1:T(8,128)S(1)}, u32[]{:S(2)}) copy-start(f32[128,4,128]{0,2,1:T(8,128)S(1)} %copy.289) | copy-start | bytes 786436
  59.6 22.4 %copy-start.32 = (f32[4,128,128]{2,1,0:T(8,128)}, f32[4,128,128]{2,1,0:T(8,128)S(1)}, u32[]{:S(2)}) copy-start(f32[4,128,128]{2,1,0:T(8,128)S(1)} %convolution_select_fusion.1) | copy-start | bytes 786436
  65.6 28.5 %copy-start.20 = (f32[128,512]{1,0:T(8,128)}, f32[128,512]{1,0:T(8,128)S(1)}, u32[]{:S(2)}) copy-start(f32[128,512]{1,0:T(8,128)S(1)} %fusion.118) | copy-start | bytes 786436
  65.6 22.8 %copy-start.49 = (f32[512]{0:T(512)S(1)}, f32[512]{0:T(512)}, u32[]{:S(2)}) copy-start(f32[512]{0:T(512)} %param.32) | copy-start | bytes 6148
  85.9 23.5 %copy-start.18 = (f32[128,4,128]{0,2,1:T(8,128)}, f32[128,4,128]{0,2,1:T(8,128)S(1)}, u32[]{:S(2)}) copy-start(f32[128,4,128]{0,2,1:T(8,128)S(1)} %get-tuple-element.440) | copy-start | bytes 786436
  85.9 8.4 copy-start.13
  94.1 42.0 %copy-start.44 = (f32[2048]{0:T(1024)S(1)}, f32[2048]{0:T(1024)}, u32[]{:S(2)}) copy-start(f32[2048]{0:T(1024)} %param.33) | copy-start | bytes 24580
  94.1 123.3 %all-reduce.15.cloned.1.call-start = ((), (), s32[]{:S(2)}) async-start(), calls=%async_computation.9 | async-start | bytes 2097152 | tf_op jit(solution)/shard_map/psum | solution.py:233
  136.1 83.6 %copy-start.48 = (f32[128]{0:T(128)}, f32[128]{0:T(128)S(1)}, u32[]{:S(2)}) copy-start(f32[128]{0:T(128)S(1)} %fusion.97) | copy-start | bytes 1540
  136.1 19.4 %slice-start = ((s8[11534336]{0:T(1024)(128)(4,1)}), s8[4194304]{0:T(1024)(128)(4,1)S(1)}, s32[]{:S(2)}) async-start(s8[11534336]{0:T(1024)(128)(4,1)} %bitcast.182), calls=%async_computation.21 | async-start | bytes 8388608
  136.1 19.4 %slice-start.1 = ((s8[11534336]{0:T(1024)(128)(4,1)}), s8[4194304]{0:T(1024)(128)(4,1)S(1)}, s32[]{:S(2)}) async-start(s8[11534336]{0:T(1024)(128)(4,1)} %bitcast.182), calls=%async_computation.22 | async-start | bytes 8388608
  145.7 9.9 slice-start.2
  145.7 9.9 copy-start.3
  145.7 21.8 %slice-start.3 = ((s8[11534336]{0:T(1024)(128)(4,1)}), s8[4194304]{0:T(1024)(128)(4,1)S(1)}, s32[]{:S(2)}) async-start(s8[11534336]{0:T(1024)(128)(4,1)} %bitcast.184), calls=%async_computation.24 | async-start | bytes 8388608
  145.7 21.8 %slice-start.4 = ((s8[11534336]{0:T(1024)(128)(4,1)}), s8[4194304]{0:T(1024)(128)(4,1)S(1)}, s32[]{:S(2)}) async-start(s8[11534336]{0:T(1024)(128)(4,1)} %bitcast.184), calls=%async_computation.25 | async-start | bytes 8388608
  155.6 11.8 copy-start.1
  155.6 11.9 slice-start.5
  180.8 103.4 %all-gather.7.cloned.1.call-start = ((), (), s32[]{:S(2)}) async-start(), calls=%async_computation.19 | async-start | bytes 2359296 | tf_op jit(solution)/shard_map/all_gather | solution.py:20
  217.4 4.1 copy-start.21
  217.4 4.1 copy-start.23
  221.5 5.9 copy-start.10
  234.4 158.5 %all-reduce.17.cloned.1.call-start = ((), (), s32[]{:S(2)}) async-start(), calls=%async_computation.20 | async-start | bytes 4194304 | tf_op jit(solution)/shard_map/psum | solution.py:230
  240.0 10.7 copy-start.16
  292.9 12.8 copy-start.9
  295.3 10.4 copy-start.12
  297.1 8.6 copy-start.17
  297.1 8.6 copy-start.28
  297.1 8.6 copy-start.29
  297.1 8.6 copy-start.31
  298.6 7.6 copy-start.30
  298.6 7.6 copy-start.36
  306.2 8.2 copy-start.39
  308.0 6.4 copy-start.7
  308.0 6.4 copy-start.37
  309.6 4.8 copy-start.33
  314.4 5.5 copy-start.22
  314.4 5.5 copy-start.24
  319.9 145.3 %reduce-scatter.17.cloned.1.call-start = ((), (), s32[]{:S(2)}) async-start(), calls=%async_computation.14 | async-start | bytes 4718592 | tf_op jit(solution)/shard_map/reduce_scatter | solution.py:279
  326.3 6.2 copy-start.38
  326.4 230.8 %reduce-scatter.15.cloned.1.call-start = ((), (), s32[]{:S(2)}) async-start(), calls=%async_computation.13 | async-start | bytes 4718592 | tf_op jit(solution)/shard_map/reduce_scatter | solution.py:271
  332.4 6.4 copy-start.34
  332.5 317.0 %reduce-scatter.9.cloned.1.call-start = ((), (), s32[]{:S(2)}) async-start(), calls=%async_computation.10 | async-start | bytes 4718592 | tf_op jit(solution)/shard_map/reduce_scatter | solution.py:268
  338.8 402.8 %reduce-scatter.11.cloned.1.call-start = ((), (), s32[]{:S(2)}) async-start(), calls=%async_computation.11 | async-start | bytes 4718592 | tf_op jit(solution)/shard_map/reduce_scatter | solution.py:269
  344.0 6.5 copy-start.2
  344.0 489.7 %reduce-scatter.13.cloned.1.call-start = ((), (), s32[]{:S(2)}) async-start(), calls=%async_computation.12 | async-start | bytes 4718592 | tf_op jit(solution)/shard_map/reduce_scatter | solution.py:270
  350.5 678.0 %reduce-scatter.19.cloned.1.call-start = ((), (), s32[]{:S(2)}) async-start(), calls=%async_computation.15 | async-start | bytes 12976128 | tf_op jit(solution)/shard_map/reduce_scatter | solution.py:272
  363.9 860.2 %reduce-scatter.21.cloned.1.call-start = ((), (), s32[]{:S(2)}) async-start(), calls=%async_computation.16 | async-start | bytes 12976128 | tf_op jit(solution)/shard_map/reduce_scatter | solution.py:273
  377.4 1043.2 %reduce-scatter.23.cloned.1.call-start = ((), (), s32[]{:S(2)}) async-start(), calls=%async_computation.17 | async-start | bytes 12976128 | tf_op jit(solution)/shard_map/reduce_scatter | solution.py:280
  390.3 5.0 copy-start.52
  390.3 5.1 copy-start.47
  390.3 5.1 copy-start.50
  (9 other events, 19.4 us)
Sparse Core Ops, SparseCore 0:
  31.5 50.4 all-gather.4
  94.2 40.3 all-reduce.12
  180.9 36.4 all-reduce.14
  234.6 49.6 all-gather.6
  320.0 51.1 all-reduce.16
  375.7 89.4 reduce-scatter.16
  469.4 87.6 reduce-scatter.14
  561.8 87.6 reduce-scatter.8
  653.7 87.8 reduce-scatter.10
  746.0 87.6 reduce-scatter.12
  837.9 190.5 reduce-scatter.18
  1032.5 191.6 reduce-scatter.20
  1228.3 192.2 reduce-scatter.22
where the time goes:
time: 1440 us; the launch traced here: 1430 us
  waiting for transfers between devices  1080 us (75%)
  matrix products  217 us (15%)
  blocking collectives  59.5 us (4%)
  other arithmetic  32.7 us (2%)
  local copies, waits for them, and re-layouts  19 us (1%)
  between operations  17.7 us (1%)
    reduce_scatter x1, waiting for transfers between devices, shards(): lax.psum_scatter(grad_sdown, 'seq', scatter_dimension=1, tiled=True)  196 us
    reduce_scatter x1, waiting for transfers between devices, shards(): lax.psum_scatter(grad_sup, 'seq', scatter_dimension=0, tiled=True)  196 us
    reduce_scatter x1, waiting for transfers between devices, shards(): lax.psum_scatter(grad_sgate, 'seq', scatter_dimension=0, tiled=True)  195 us
    dot_general x24, matrix products, matmul(): return jnp.dot(left, right, precision=TOP_PRECISION)  194 us
    reduce_scatter x1, waiting for transfers between devices, shards(): lax.psum_scatter(grad_qw, 'seq', scatter_dimension=0, tiled=True)  92.3 us
    reduce_scatter x1, waiting for transfers between devices, shards(): lax.psum_scatter(grad_iw, 'seq', scatter_dimension=0, tiled=True)  92.2 us
    reduce_scatter x1, waiting for transfers between devices, shards(): lax.psum_scatter(grad_fw, 'seq', scatter_dimension=0, tiled=True)  92.1 us
    reduce_scatter x1, waiting for transfers between devices, shards(): lax.psum_scatter(grad_gw, 'seq', scatter_dimension=0, tiled=True)  91.9 us
  transfers between devices with their start and end apart: 13, of which 12 were waited for; matrix products, arithmetic and copies ran while one was open for 9% of the time, Pallas kernels for 0%

commit v1 on v0

v1 whole, which is shorter than its diff:
```python
from functools import partial

import jax
import jax.numpy as jnp
from jax import lax
from jax.sharding import PartitionSpec as P

HDIM = 128
CHUNK = 128
HIGH = lax.Precision.HIGH
HIGHEST = lax.Precision.HIGHEST
norm_eps = 1e-06
group_eps = 1e-05


def dot(left, right, contract_left, contract_right, precision=HIGH):
    return lax.dot_general(
        left,
        right,
        (((contract_left,), (contract_right,)), ((), ())),
        precision=precision,
        preferred_element_type=jnp.float32,
    )


def rms(entries):
    return lax.rsqrt(jnp.mean(entries * entries, -1, keepdims=True) + norm_eps)


def silu_grad(entries):
    gate = jax.nn.sigmoid(entries)
    return gate * (1.0 + entries * (1.0 - gate))


def gather_tokens(block):
    return lax.all_gather(block, "seq", axis=0, tiled=True)


def recurrence(query_rows, key_vecs, value_rows, segment):
    token_count, width = query_rows.shape
    heads = width // HDIM
    chunks = token_count // CHUNK

    def split(entries):
        return entries.reshape(chunks, CHUNK, heads, HDIM)

    blocked = segment.reshape(chunks, CHUNK)
    last_seg = blocked[:, -1]
    first_segs = jnp.concatenate([jnp.full((1,), -1, segment.dtype), last_seg[:-1]])
    carry = (blocked == first_segs[:, None]).astype(jnp.float32)
    in_last = (blocked == last_seg[:, None]).astype(jnp.float32)
    places = jnp.arange(CHUNK)
    allowed = (places[None, :, None] >= places[None, None, :]) & (
        blocked[:, :, None] == blocked[:, None, :]
    )
    lower = (places[:, None] >= places[None, :]).astype(jnp.float32)
    queries, keys, values = split(query_rows), split(key_vecs), split(value_rows)
    log_decay = jnp.einsum("ts,cshk->cthk", lower, jnp.log1p(-keys), precision=HIGHEST)
    growth = jnp.exp(log_decay)
    grown = queries * growth
    last = log_decay[:, -1]
    scores = jnp.einsum("cthk,cshk->chts", grown, keys * jnp.exp(-log_decay), precision=HIGH)
    scores = jnp.where(allowed[:, None], scores, 0.0)
    inner = jnp.einsum("chts,cshv->cthv", scores, values, precision=HIGH)
    weighted = keys * jnp.exp(last[:, None] - log_decay) * in_last[:, :, None, None]
    updates = jnp.einsum("cshk,cshv->chkv", weighted, values, precision=HIGH)
    through = jnp.exp(last) * carry[:, -1][:, None, None]
    state = jnp.zeros_like(updates[0])
    states = []
    for chunk in range(chunks):
        states.append(state)
        state = state * through[chunk][:, :, None] + updates[chunk]
    outer = jnp.einsum(
        "cthk,chkv->cthv", grown * carry[:, :, None, None], jnp.stack(states), precision=HIGH
    )
    return (inner + outer).reshape(token_count, width)


def mixer_all(pre_query, pre_forget, value_rows, gate_in, group_gain, lower_bound, segment):
    key_vecs = (1.0 - lower_bound) * jax.nn.sigmoid(-pre_forget)
    raw = recurrence(jax.nn.silu(pre_query), key_vecs, value_rows, segment)
    heads = raw.reshape(raw.shape[0], -1, HDIM)
    scale = lax.rsqrt(jnp.mean(heads * heads, -1, keepdims=True) + group_eps)
    normed = (heads * scale).reshape(raw.shape)
    return normed * group_gain * jax.nn.silu(gate_in)


def shards(
    tokens_in,
    cotangent,
    lengths,
    lower_bound,
    query_weight,
    forget_weight,
    input_weight,
    gate_weight,
    out_weight,
    swiglu_gate,
    swiglu_up,
    swiglu_down,
    first_gain,
    group_gain,
    second_gain,
):
    seq_count = lax.axis_size("seq")
    seq_place = lax.axis_index("seq")
    own_rows, model = tokens_in.shape
    token_count = own_rows * seq_count
    share_rows = own_rows // lax.axis_size("mp")
    share_start = lax.axis_index("mp") * share_rows
    start_row = seq_place * own_rows
    own_cols = model // seq_count
    start_col = seq_place * own_cols

    def own(entries):
        return lax.dynamic_slice_in_dim(entries, start_row, own_rows, 0)

    def columns(entries):
        return lax.dynamic_slice_in_dim(entries, start_col, own_cols, 1)

    def share(entries):
        return lax.dynamic_slice_in_dim(entries, share_start, share_rows, 0)

    positions = jnp.arange(token_count, dtype=jnp.int32)
    offsets = jnp.cumsum(lengths) - lengths
    segment = jnp.sum((positions[:, None] >= offsets[None, :]).astype(jnp.int32), 1) - 1

    all_tokens = gather_tokens(tokens_in)
    all_cotangent = gather_tokens(cotangent)
    normed_one = all_tokens * rms(all_tokens) * first_gain
    pre_query = dot(normed_one, query_weight, 1, 0)
    pre_forget = dot(normed_one, forget_weight, 1, 0)
    value_rows = dot(normed_one, input_weight, 1, 0)
    gate_in = dot(normed_one, gate_weight, 1, 0)
    mixer, mixer_back = jax.vjp(
        partial(mixer_all, lower_bound=lower_bound, segment=segment),
        pre_query,
        pre_forget,
        value_rows,
        gate_in,
        group_gain,
    )
    residual = tokens_in + lax.psum(dot(own(mixer), out_weight, 1, 0), "mp")
    scale_two = rms(residual)
    normed_two = residual * scale_two * second_gain
    grad_hidden_all = dot(all_cotangent, swiglu_down, 1, 1)
    a = dot(normed_two, swiglu_gate, 1, 0)
    b = dot(normed_two, swiglu_up, 1, 0)
    silu_a = jax.nn.silu(a)
    ffn_part = dot(silu_a * b, swiglu_down, 1, 0)
    output = share(residual) + lax.psum_scatter(ffn_part, "mp", scatter_dimension=0, tiled=True)
    e = own(grad_hidden_all)
    grad_a = e * b * silu_grad(a)
    grad_b = e * silu_a
    grad_normed_two = lax.psum(
        dot(grad_a, swiglu_gate, 1, 1) + dot(grad_b, swiglu_up, 1, 1), "mp"
    )
    pulled = grad_normed_two * second_gain
    grad_residual = (
        cotangent
        + scale_two * pulled
        - residual * scale_two**3 * jnp.mean(pulled * residual, -1, keepdims=True)
    )
    all_normed_two = gather_tokens(normed_two)
    a_all = dot(all_normed_two, swiglu_gate, 1, 0)
    b_all = dot(all_normed_two, swiglu_up, 1, 0)
    silu_all = jax.nn.silu(a_all)
    hidden_all = silu_all * b_all
    grad_a_all = grad_hidden_all * b_all * silu_grad(a_all)
    grad_b_all = grad_hidden_all * silu_all
    normed_two_cols = columns(all_normed_two)
    grad_sgate = dot(normed_two_cols, grad_a_all, 0, 0)
    grad_sup = dot(normed_two_cols, grad_b_all, 0, 0)
    grad_sdown = dot(hidden_all, columns(all_cotangent), 0, 0)

    grad_mixer = gather_tokens(dot(grad_residual, out_weight, 1, 1))
    residual_cols = lax.all_to_all(grad_residual, "seq", 1, 0, tiled=True)
    grad_outw = dot(mixer, residual_cols, 0, 0)
    grad_query_rows, grad_forget_rows, grad_value_rows, grad_gate_rows, grad_group = mixer_back(
        grad_mixer
    )
    grad_group = lax.dynamic_slice_in_dim(
        grad_group, seq_place * (group_gain.shape[0] // seq_count), group_gain.shape[0] // seq_count
    )
    normed_one_cols = columns(normed_one)
    pairs = (
        (grad_query_rows, query_weight),
        (grad_forget_rows, forget_weight),
        (grad_value_rows, input_weight),
        (grad_gate_rows, gate_weight),
    )
    weight_grads = []
    normed_part = 0.0
    first_sum = 0.0
    for grad_rows, weight in pairs:
        weight_grad = dot(normed_one_cols, grad_rows, 0, 0)
        weight_grads.append(weight_grad)
        normed_part = normed_part + dot(own(grad_rows), weight, 1, 1)
        own_weight = lax.dynamic_slice_in_dim(weight, start_col, own_cols, 0)
        first_sum = first_sum + jnp.sum(own_weight * weight_grad, 1)
    second_sum = jnp.sum(
        lax.dynamic_slice_in_dim(swiglu_gate, start_col, own_cols, 0) * grad_sgate
        + lax.dynamic_slice_in_dim(swiglu_up, start_col, own_cols, 0) * grad_sup,
        1,
    )
    gains = jnp.stack(
        [
            lax.dynamic_slice_in_dim(first_gain, start_col, own_cols),
            lax.dynamic_slice_in_dim(second_gain, start_col, own_cols),
        ]
    )
    gain_grads = lax.psum(jnp.stack([first_sum, second_sum]), "mp") / gains
    grad_normed_one = lax.psum_scatter(normed_part, "mp", scatter_dimension=0, tiled=True)
    tokens_share = share(tokens_in)
    scale_one = rms(tokens_share)
    pulled_one = grad_normed_one * first_gain
    grad_tokens = (
        share(grad_residual)
        + scale_one * pulled_one
        - tokens_share * scale_one**3 * jnp.mean(pulled_one * tokens_share, -1, keepdims=True)
    )
    return (
        output,
        grad_tokens,
        weight_grads[0],
        weight_grads[1],
        weight_grads[2],
        weight_grads[3],
        grad_outw,
        grad_sgate,
        grad_sup,
        grad_sdown,
        gain_grads[0],
        grad_group,
        gain_grads[1],
    )


def solution(mesh):
    in_specs = (
        P("seq", None),
        P("seq", None),
        P(),
        P("mp"),
        P(None, "mp"),
        P(None, "mp"),
        P(None, "mp"),
        P(None, "mp"),
        P("mp", None),
        P(None, "mp"),
        P(None, "mp"),
        P("mp", None),
        P(),
        P("mp"),
        P(),
    )
    out_specs = (
        P(("seq", "mp"), None),
        P(("seq", "mp"), None),
        P("seq", "mp"),
        P("seq", "mp"),
        P("seq", "mp"),
        P("seq", "mp"),
        P("mp", "seq"),
        P("seq", "mp"),
        P("seq", "mp"),
        P("mp", "seq"),
        P("seq"),
        P(("mp", "seq")),
        P("seq"),
    )
    return jax.shard_map(shards, mesh=mesh, in_specs=in_specs, out_specs=out_specs, check_vma=False)
```

time: 1440 us -> 743 us (0.52)
  waiting for transfers between devices: 1080 us -> 368 us
  blocking collectives: 59.5 us -> 6.14 us
  matrix products: 217 us -> 259 us
  local copies, waits for them, and re-layouts: 19 us -> 47.7 us
    reduce_scatter x8 -> x2, waiting for transfers between devices: 988 us -> 0.01 us  [the longest x1 0.01 us: shards(): lax.psum_scatter(normed_part, 'mp', scatter_dimension=0, tiled=True)]
    all_gather x2 -> x4, waiting for transfers between devices: 30.4 us -> 296 us  [gather_tokens(): return lax.all_gather(block, 'seq', axis=0, tiled=True)]
    dot_general x38 -> x40, matrix products: 217 us -> 259 us  [the longest x26 227 us: dot(): lax.dot_general(left, right, (((contract_left,), (contract_right,)), ((),...]
    unnamed x1 -> x0, blocking collectives: 33.7 us -> none
    all_gather x1 -> x0, blocking collectives: 25.7 us -> none  [prefix(): gathered = jax.tree.map(lambda a: lax.all_gather(a, axis), part)]
    all_to_all x0 -> x1, waiting for transfers between devices: none -> 20.2 us  [shards(): residual_cols = lax.all_to_all(grad_residual, 'seq', 1, 0, tiled=True)]
    unnamed x124 -> x172, local copies, waits for them, and re-layouts: 5.58 us -> 20.4 us
    psum x3 -> x2, waiting for transfers between devices: 61.8 us -> 49.1 us  [the longest x1 36.5 us: shards(): lax.psum(dot(grad_a, swiglu_gate, 1, 1) + dot(grad_b, swiglu_up, 1, 1), '...]
  transfers between devices with their start and end apart: 13 -> 9, of which waited for: 12 -> 7; matrix products, arithmetic and copies ran while one was open for 9% -> 27% of each run, Pallas kernels for 0% -> 0%
where the time goes in v1:
time: 743 us; the launch traced here: 732 us
  waiting for transfers between devices  368 us (50%)
  matrix products  259 us (35%)
  local copies, waits for them, and re-layouts  47.7 us (6%)
  other arithmetic  31.1 us (4%)
  between operations  15.6 us (2%)
    all_gather x4, waiting for transfers between devices, gather_tokens(): return lax.all_gather(block, 'seq', axis=0, tiled=True)  296 us
    dot_general x26, matrix products, dot(): lax.dot_general(left, right, (((contract_left,), (contract_right,)), ((),...  227 us
    psum x1, waiting for transfers between devices, shards(): lax.psum(dot(grad_a, swiglu_gate, 1, 1) + dot(grad_b, swiglu_up, 1, 1), '...  36.5 us
    unnamed x172, local copies, waits for them, and re-layouts  20.4 us
    all_to_all x1, waiting for transfers between devices, shards(): residual_cols = lax.all_to_all(grad_residual, 'seq', 1, 0, tiled=True)  20.2 us
  transfers between devices with their start and end apart: 9, of which 7 were waited for; matrix products, arithmetic and copies ran while one was open for 27% of the time, Pallas kernels for 0%

profile of v1, /device:TPU:8, one launch (start us, length us, event | category | flops | bytes accessed | tf_op | source)
XLA Modules:
  0.0 732.3 jit_solution(4622363377666889125)
XLA Ops:
  10.7 123.7 %all-gather.5.cloned.1.call-done = f32[1024,2048]{1,0:T(8,128)} async-done(((f32[128,2048]{1,0:T(8,128)}), f32[1024,2048]{1,0:T(8,128)}) %all-gather.5.cloned.1.call-update) | async-done | bytes 8388624 | tf_op jit(solution)/shard_map/all_gather | solution.py:36
  134.4 4.1 multiply_reduce_fusion
  138.6 1.6 copy-done.7
  141.0 3.9 copy-done.2
  144.9 8.2 %fusion.169 = f32[1024,512]{1,0:T(8,128)} fusion(f32[1024,2048]{1,0:T(8,128)S(1)} %multiply_multiply_fusion, f32[2048,512]{1,0:T(8,128)S(1)} %copy-done.36), kind=kOutput, calls=%fused_computation.275 | convolution fusion | flops 6442450944 | bytes 14680064 | tf_op jit(solution)/shard_map/dot_general | solution.py:17
  153.1 3.4 reshape.313
  156.5 11.7 %fusion.39 = (f32[1024,512]{1,0:T(8,128)S(1)}, f32[1024,512]{1,0:T(8,128)}) fusion(f32[1024,2048]{1,0:T(8,128)} %copy-done.2, f32[2048,512]{1,0:T(8,128)} %param.19), kind=kOutput, calls=%fused_computation.73 | convolution fusion | flops 6444548096 | bytes 16777216 | tf_op jit(solution)/shard_map/dot_general | solution.py:17
  168.3 1.7 reshape.316
  170.0 12.2 %broadcast_multiply_fusion.1 = (f32[1024,512]{1,0:T(8,128)}, f32[1024,512]{1,0:T(8,128)}) fusion(f32[512]{0:T(512)S(1)} %broadcast_subtract_fusion, f32[1024,2048]{1,0:T(8,128)} %copy-done.2, f32[2048,512]{1,0:T(8,128)} %param.20), kind=kOutput, calls=%fused_computation.119 | convolution fusion | flops 6444023808 | bytes 16779264 | tf_op jit(solution)/shard_map/dot_general | solution.py:17
  182.1 2.1 reshape.317
  184.3 3.9 copy_multiply_fusion
  188.4 2.1 fusion.58
  191.9 2.4 fusion.47
  194.3 2.3 fusion.118
  196.6 3.1 multiply_reduce_fusion.3
  200.6 2.9 copy.150
  205.1 12.5 %multiply_multiply_fusion.2 = (f32[1024,512]{1,0:T(8,128)S(1)}, f32[1024,512]{1,0:T(8,128)}) fusion(f32[512]{0:T(512)S(1)} %copy-done.69, f32[128,8,4,128]{3,2,1,0:T(4,128)S(1)} %bitcast.281, f32[128,8,4,128]{3,2,1,0:T(4,128)S(1)} %bitcast.284, f32[1024,2048]{1,0:T(8,128)} %copy-done.2, f32[2048,512]{1,0:T(8,128)} %param.22), kind=kOutput, calls=%fused_computation.80 | convolution fusion | flops 6446120960 | bytes 20973568 | tf_op jit(solution)/shard_map/dot_general | solution.py:17
  219.0 2.5 fusion.130
  221.5 38.2 %all-gather.7.cloned.1.call-done = f32[1024,2048]{1,0:T(8,128)} async-done(((f32[128,2048]{1,0:T(8,128)}), f32[1024,2048]{1,0:T(8,128)}) %all-gather.7.cloned.1.call-update) | async-done | bytes 8388624 | tf_op jit(solution)/shard_map/all_gather | solution.py:36
  259.7 26.5 %fusion.172 = f32[1024,1408]{1,0:T(8,128)} fusion(f32[1024,2048]{1,0:T(8,128)} %all-gather.7.cloned.1.call-done, f32[1408,2048]{1,0:T(8,128)} %param.26), kind=kOutput, calls=%fused_computation.278 | convolution fusion | flops 17716740096 | bytes 25690112 | tf_op jit(solution)/shard_map/dot_general | solution.py:17
  286.2 12.6 %all-reduce.18.cloned.1.call-done = f32[128,2048]{1,0:T(8,128)} async-done(((f32[128,2048]{1,0:T(8,128)}), f32[128,2048]{1,0:T(8,128)}) %all-reduce.18.cloned.1.call-update) | async-done | bytes 1048592 | tf_op jit(solution)/shard_map/psum | solution.py:143
  298.8 1.7 multiply_reduce_fusion.5
  301.7 8.3 %fusion.171 = f32[128,1408]{1,0:T(8,128)S(1)} fusion(f32[128,2048]{1,0:T(8,128)} %multiply_multiply_fusion.3, f32[2048,1408]{1,0:T(8,128)} %param.25), kind=kOutput, calls=%fused_computation.277 | convolution fusion | flops 2214592512 | bytes 13303808 | tf_op jit(solution)/shard_map/dot_general | solution.py:17
  310.1 8.1 %fusion.170 = f32[128,1408]{1,0:T(8,128)S(1)} fusion(f32[128,2048]{1,0:T(8,128)S(1)} %copy-done.17, f32[2048,1408]{1,0:T(8,128)} %param.24), kind=kOutput, calls=%fused_computation.276 | convolution fusion | flops 2214592512 | bytes 13303808 | tf_op jit(solution)/shard_map/dot_general | solution.py:17
  318.3 8.7 %fusion.104 = f32[128,2048]{1,0:T(8,128)} fusion(f32[2048,1408]{1,0:T(8,128)S(1)} %bitcast.276, f32[128,1408]{1,0:T(8,128)S(1)} %fusion.170, f32[128,1408]{1,0:T(8,128)S(1)} %fusion.171, f32[1024,1408]{1,0:T(8,128)} %fusion.172, s32[]{:T(128)S(6)} %select_n.17), kind=kOutput, calls=%fused_computation.135 | convolution fusion | flops 2216214528 | bytes 14745604 | tf_op jit(solution)/shard_map/dot_general | solution.py:17
  327.1 8.5 %convolution_add_fusion.3 = f32[128,2048]{1,0:T(8,128)} fusion(f32[128,2048]{1,0:T(8,128)} %fusion.104, f32[2048,1408]{1,0:T(8,128)S(1)} %bitcast.278, f32[1024,1408]{1,0:T(8,128)} %fusion.172, s32[]{:T(128)S(6)} %select_n.17, f32[128,1408]{1,0:T(8,128)S(1)} %fusion.170), kind=kOutput, calls=%fused_computation.23 | convolution fusion | flops 2215755776 | bytes 15073284 | tf_op jit(solution)/shard_map/dot_general | solution.py:17
  335.6 36.5 %all-reduce.20.cloned.1.call-done = f32[128,2048]{1,0:T(8,128)} async-done(((f32[128,2048]{1,0:T(8,128)}), f32[128,2048]{1,0:T(8,128)}) %all-reduce.20.cloned.1.call-update) | async-done | bytes 1048592 | tf_op jit(solution)/shard_map/psum | solution.py:155
  372.2 1.6 multiply_reduce_fusion.4
  376.6 3.0 fusion.173
  379.7 2.0 bitcast_add_fusion.8
  381.7 9.3 %fusion.111 = f32[128,2048]{1,0:T(8,128)} fusion(f32[1408,2048]{1,0:T(8,128)} %param.26, f32[128,1408]{1,0:T(8,128)} %copy-done.33, f32[128,1408]{1,0:T(8,128)} %copy-done.20), kind=kOutput, calls=%fused_computation.142 | convolution fusion | flops 2215493632 | bytes 14024704 | tf_op jit(solution)/shard_map/dot_general | solution.py:17
  391.0 38.4 %all-gather.9.cloned.1.call-done = f32[1024,512]{1,0:T(8,128)} async-done(((f32[128,512]{1,0:T(8,128)}), f32[1024,512]{1,0:T(8,128)}) %all-gather.9.cloned.1.call-update) | async-done | bytes 2097168 | tf_op jit(solution)/shard_map/all_gather | solution.py:36
  429.4 7.4 %multiply_reduce_fusion.1 = (f32[512]{0:T(512)}, f32[1024,512]{1,0:T(8,128)}, f32[1024,512]{1,0:T(8,128)}) fusion(f32[1024,512]{1,0:T(8,128)} %all-gather.9.cloned.1.call-done, f32[128,8,4,128]{3,2,1,0:T(4,128)} %bitcast.282, f32[128,8,4,128]{3,2,1,0:T(4,128)} %bitcast.283, f32[1024,512]{1,0:T(8,128)} %get-tuple-element.70, f32[512]{0:T(512)} %param.28), kind=kLoop, calls=%fused_computation.55 | loop fusion | flops 8912384 | bytes 12587008 | tf_op jit(solution)/shard_map/transpose(jvp())/reduce_sum | solution.py:85
  436.9 2.9 reshape.319
  439.8 3.3 copy.152
  443.1 2.7 multiply_reduce_fusion.2
  448.4 1.9 fusion.63
  453.4 2.0 fusion.41
  455.4 2.3 multiply_add_fusion
  458.6 2.3 fusion.116
  460.9 2.1 fusion.74
  467.8 3.7 fusion.21
  477.4 2.3 fusion.128
  480.3 1.6 copy-done.35
  482.0 2.3 convolution_add_fusion.2
  484.9 2.4 convolution_add_fusion.1
  487.3 4.3 convolution_add_fusion
  492.4 2.3 copy.245
  494.7 4.6 all-to-all-start
  500.2 1.7 dynamic-slice_add_fusion
  501.9 20.2 %all-to-all-done = f32[128,8,256]{2,0,1:T(8,128)} async-done(((f32[128,8,256]{2,0,1:T(8,128)}), f32[128,8,256]{2,0,1:T(8,128)}, u32[]{:S(2)}, u32[]{:S(2)}) %all-to-all-start) | async-done | bytes 1048608 | tf_op jit(solution)/shard_map/all_to_all | solution.py:177
  522.0 4.6 fusion.174
  527.9 3.4 multiply_reduce_fusion.9
  531.4 3.2 multiply_reduce_fusion.8
  534.6 4.2 multiply_reduce_fusion.7
  538.8 3.3 multiply_reduce_fusion.6
  543.3 1.9 multiply_subtract_fusion.1
  545.1 95.8 %all-gather.11.cloned.1.call-done = f32[1024,2048]{1,0:T(8,128)} async-done(((f32[128,2048]{1,0:T(8,128)}), f32[1024,2048]{1,0:T(8,128)}) %all-gather.11.cloned.1.call-update) | async-done | bytes 8388624 | tf_op jit(solution)/shard_map/all_gather | solution.py:36
  641.0 24.5 %fusion.176 = f32[1024,1408]{1,0:T(8,128)S(1)} fusion(f32[1024,2048]{1,0:T(8,128)} %all-gather.11.cloned.1.call-done, f32[2048,1408]{1,0:T(8,128)} %param.24), kind=kOutput, calls=%fused_computation.282 | convolution fusion | flops 17716740096 | bytes 25690112 | tf_op jit(solution)/shard_map/dot_general | solution.py:17
  665.5 25.7 %fusion.175 = f32[1024,1408]{1,0:T(8,128)} fusion(f32[1024,2048]{1,0:T(8,128)S(1)} %copy-done.73, f32[2048,1408]{1,0:T(8,128)} %param.25), kind=kOutput, calls=%fused_computation.281 | convolution fusion | flops 17716740096 | bytes 25690112 | tf_op jit(solution)/shard_map/dot_general | solution.py:17
  691.3 7.6 %fusion.4 = f32[256,1408]{1,0:T(8,128)S(1)} fusion(f32[1024,1408]{1,0:T(8,128)S(1)} %fusion.176, f32[1024,1408]{1,0:T(8,128)S(1)} %bitcast.297, f32[1024,1408]{1,0:T(8,128)} %fusion.175, f32[1024,2048]{1,0:T(8,128)S(1)} %copy-done.73, s32[]{:T(128)S(6)} %select_n.20), kind=kOutput, calls=%fused_computation.6 | convolution fusion | flops 2227568640 | bytes 19791876 | tf_op jit(solution)/shard_map/dot_general | solution.py:17
  698.8 9.2 %add_reduce_fusion = (f32[256]{0:T(256)S(1)}, f32[256,1408]{1,0:T(8,128)}) fusion(f32[2048,1408]{1,0:T(8,128)} %param.25, s32[]{:T(128)S(6)} %select_n.20, f32[256,1408]{1,0:T(8,128)S(1)} %fusion.4, f32[2048,1408]{1,0:T(8,128)} %param.24, f32[1024,1408]{1,0:T(8,128)S(1)} %bitcast.297, f32[1024,1408]{1,0:T(8,128)} %copy-done.76, f32[1024,2048]{1,0:T(8,128)S(1)} %copy-done.73), kind=kOutput, calls=%fused_computation.103 | convolution fusion | flops 2223243008 | bytes 18352128 | tf_op jit(solution)/shard_map/dot_general | solution.py:17
  708.0 6.1 psum.23
  714.8 10.5 %fusion = f32[1408,256]{1,0:T(8,128)} fusion(f32[1024,1408]{1,0:T(8,128)} %fusion.175, f32[1024,2048]{1,0:T(8,128)} %all-gather.7.cloned.1.call-done, s32[]{:T(128)S(6)} %select_n.20, f32[1024,1408]{1,0:T(8,128)} %copy-done.76), kind=kOutput, calls=%fused_computation.2 | convolution fusion | flops 2221801472 | bytes 14024708 | tf_op jit(solution)/shard_map/dot_general | solution.py:17
  (247 shorter events, 36.3 us)
Async XLA Ops:
  7.2 3.3 copy-start.72
  7.2 127.2 %all-gather.5.cloned.1.call-start = ((), (), s32[]{:S(2)}) async-start(), calls=%async_computation.3 | async-start | bytes 9437184 | tf_op jit(solution)/shard_map/all_gather | solution.py:36
  7.9 251.8 %all-gather.7.cloned.1.call-start = ((), (), s32[]{:S(2)}) async-start(), calls=%async_computation.6 | async-start | bytes 9437184 | tf_op jit(solution)/shard_map/all_gather | solution.py:36
  8.7 290.2 %all-reduce.18.cloned.1.call-start = ((), (), s32[]{:S(2)}) async-start(), calls=%async_computation.4 | async-start | bytes 2097152 | tf_op jit(solution)/shard_map/psum | solution.py:143
  9.6 178.9 %copy-start.63 = (f32[8,128]{1,0:T(8,128)}, f32[8,128]{1,0:T(8,128)S(1)}, u32[]{:S(2)}) copy-start(f32[8,128]{1,0:T(8,128)S(1)} %get-tuple-element.54) | copy-start | bytes 12292
  9.6 182.3 %copy-start.45 = (f32[8,128]{1,0:T(8,128)}, f32[8,128]{1,0:T(8,128)S(1)}, u32[]{:S(2)}) copy-start(f32[8,128]{1,0:T(8,128)S(1)} %get-tuple-element.53) | copy-start | bytes 12292
  9.7 178.5 %copy-start.70 = (f32[8]{0:T(128)}, f32[8]{0:T(128)S(1)}, u32[]{:S(2)}) copy-start(f32[8]{0:T(128)S(1)} %slice_reduce_fusion.1) | copy-start | bytes 100
  10.5 159.5 %copy-start.67 = (f32[512]{0:T(512)}, f32[512]{0:T(512)S(1)}, u32[]{:S(2)}) copy-start(f32[512]{0:T(512)S(1)} %broadcast_subtract_fusion) | copy-start | bytes 6148
  10.7 127.9 %copy-start.50 = (f32[2048]{0:T(1024)S(1)}, f32[2048]{0:T(1024)}, u32[]{:S(2)}) copy-start(f32[2048]{0:T(1024)} %param.27) | copy-start | bytes 24580
  134.4 5.8 copy-start.7
  140.2 4.7 copy-start.36
  141.0 3.9 copy-start.2
  184.2 4.2 copy-start.3
  188.2 6.1 copy-start
  188.2 6.1 copy-start.5
  188.3 3.2 copy-start.55
  188.4 3.2 copy-start.61
  188.4 3.3 copy-start.47
  188.4 3.3 copy-start.52
  188.4 3.4 copy-start.57
  188.4 3.4 copy-start.59
  188.4 3.4 copy-start.65
  188.4 3.1 copy-start.26
  191.9 2.4 copy-start.27
  196.6 3.2 copy-start.13
  199.8 3.8 copy-start.43
  204.8 12.9 %copy-start.15 = (f32[1024,4,128]{2,1,0:T(4,128)}, f32[1024,4,128]{2,1,0:T(4,128)S(1)}, u32[]{:S(2)}) copy-start(f32[1024,4,128]{2,1,0:T(4,128)S(1)} %mul.638) | copy-start | bytes 6291460
  205.1 13.8 %copy-start.18 = (f32[512,2048]{1,0:T(8,128)S(1)}, f32[512,2048]{1,0:T(8,128)}, u32[]{:S(2)}) copy-start(f32[512,2048]{1,0:T(8,128)} %param.23) | copy-start | bytes 12582916
  221.4 150.7 %all-reduce.20.cloned.1.call-start = ((), (), s32[]{:S(2)}) async-start(), calls=%async_computation.7 | async-start | bytes 2097152 | tf_op jit(solution)/shard_map/psum | solution.py:155
  286.2 14.4 %copy-start.49 = (f32[2048]{0:T(1024)S(1)}, f32[2048]{0:T(1024)}, u32[]{:S(2)}) copy-start(f32[2048]{0:T(1024)} %param.29) | copy-start | bytes 24580
  301.7 8.3 %copy-start.17 = (f32[128,2048]{1,0:T(8,128)S(1)}, f32[128,2048]{1,0:T(8,128)}, u32[]{:S(2)}) copy-start(f32[128,2048]{1,0:T(8,128)} %multiply_multiply_fusion.3) | copy-start | bytes 3145732
  301.7 16.5 %slice-start = ((s8[11534336]{0:T(1024)(128)(4,1)}), s8[4194304]{0:T(1024)(128)(4,1)S(1)}, s32[]{:S(2)}) async-start(s8[11534336]{0:T(1024)(128)(4,1)} %bitcast.275), calls=%async_computation.11 | async-start | bytes 8388608
  301.7 16.5 %slice-start.1 = ((s8[11534336]{0:T(1024)(128)(4,1)}), s8[4194304]{0:T(1024)(128)(4,1)S(1)}, s32[]{:S(2)}) async-start(s8[11534336]{0:T(1024)(128)(4,1)} %bitcast.275), calls=%async_computation.12 | async-start | bytes 8388608
  310.1 8.2 %copy-start.33 = (f32[128,1408]{1,0:T(8,128)}, f32[128,1408]{1,0:T(8,128)S(1)}, u32[]{:S(2)}) copy-start(f32[128,1408]{1,0:T(8,128)S(1)} %fusion.171) | copy-start | bytes 2162692
  310.1 8.2 %slice-start.2 = ((s8[11534336]{0:T(1024)(128)(4,1)}), s8[3145728]{0:T(1024)(128)(4,1)S(1)}, s32[]{:S(2)}) async-start(s8[11534336]{0:T(1024)(128)(4,1)} %bitcast.275), calls=%async_computation.13 | async-start | bytes 6291456
  310.1 17.0 %slice-start.3 = ((s8[11534336]{0:T(1024)(128)(4,1)}), s8[4194304]{0:T(1024)(128)(4,1)S(1)}, s32[]{:S(2)}) async-start(s8[11534336]{0:T(1024)(128)(4,1)} %bitcast.277), calls=%async_computation.14 | async-start | bytes 8388608
  310.1 17.0 %slice-start.4 = ((s8[11534336]{0:T(1024)(128)(4,1)}), s8[4194304]{0:T(1024)(128)(4,1)S(1)}, s32[]{:S(2)}) async-start(s8[11534336]{0:T(1024)(128)(4,1)} %bitcast.277), calls=%async_computation.15 | async-start | bytes 8388608
  318.3 8.8 %copy-start.20 = (f32[128,1408]{1,0:T(8,128)}, f32[128,1408]{1,0:T(8,128)S(1)}, u32[]{:S(2)}) copy-start(f32[128,1408]{1,0:T(8,128)S(1)} %fusion.170) | copy-start | bytes 2162692
  318.3 8.8 %slice-start.5 = ((s8[11534336]{0:T(1024)(128)(4,1)}), s8[3145728]{0:T(1024)(128)(4,1)S(1)}, s32[]{:S(2)}) async-start(s8[11534336]{0:T(1024)(128)(4,1)} %bitcast.277), calls=%async_computation.16 | async-start | bytes 6291456
  335.6 93.8 %all-gather.9.cloned.1.call-start = ((), (), s32[]{:S(2)}) async-start(), calls=%async_computation.8 | async-start | bytes 2359296 | tf_op jit(solution)/shard_map/all_gather | solution.py:36
  374.0 2.6 copy-start.19
  379.6 120.5 %reduce-scatter.3.cloned.1.call-start = ((), (), s32[]{:S(2)}) async-start(), calls=%async_computation.5 | async-start | bytes 1310720 | tf_op jit(solution)/shard_map/reduce_scatter | solution.py:151
  391.0 151.2 %reduce-scatter.5.cloned.1.call-start = ((), (), s32[]{:S(2)}) async-start(), calls=%async_computation.9 | async-start | bytes 1310720 | tf_op jit(solution)/shard_map/reduce_scatter | solution.py:213
  443.1 2.8 copy-start.44
  443.1 2.9 copy-start.8
  443.1 3.5 copy-start.12
  443.1 3.5 copy-start.54
  455.4 2.5 copy-start.53
  455.4 2.5 copy-start.60
  467.2 8.9 %copy-start.22 = (f32[1024,512]{1,0:T(8,128)}, f32[1024,512]{1,0:T(8,128)S(1)}, u32[]{:S(2)}) copy-start(f32[1024,512]{1,0:T(8,128)S(1)} %fusion.15) | copy-start | bytes 6291460
  467.8 3.7 copy-start.14
  482.0 2.9 copy-start.37
  491.6 149.3 %all-gather.11.cloned.1.call-start = ((), (), s32[]{:S(2)}) async-start(), calls=%async_computation.10 | async-start | bytes 9437184 | tf_op jit(solution)/shard_map/all_gather | solution.py:36
  492.4 7.7 %copy-start.51 = (f32[2048]{0:T(1024)S(1)}, f32[2048]{0:T(1024)}, u32[]{:S(2)}) copy-start(f32[2048]{0:T(1024)} %param.27) | copy-start | bytes 24580
  494.7 27.3 %all-to-all-start = ((f32[128,8,256]{2,0,1:T(8,128)}), f32[128,8,256]{2,0,1:T(8,128)}, u32[]{:S(2)}, u32[]{:S(2)}) async-start(f32[128,8,256]{2,0,1:T(8,128)} %bitcast.288), calls=%async_computation.2 | async-start | bytes 2097152 | tf_op jit(solution)/shard_map/all_to_all | solution.py:177
  522.0 5.9 copy-start.23
  527.9 3.4 copy-start.25
  534.6 4.2 copy-start.30
  538.8 3.4 copy-start.32
  641.0 24.5 %copy-start.73 = (f32[1024,2048]{1,0:T(8,128)S(1)}, f32[1024,2048]{1,0:T(8,128)}, u32[]{:S(2)}) copy-start(f32[1024,2048]{1,0:T(8,128)} %all-gather.11.cloned.1.call-done) | copy-start | bytes 25165828
  641.0 50.3 %slice-start.6 = ((s8[5767168]{0:T(1024)(128)(4,1)}), s8[4194304]{0:T(1024)(128)(4,1)S(1)}, s32[]{:S(2)}) async-start(s8[5767168]{0:T(1024)(128)(4,1)} %bitcast.296), calls=%async_computation.17 | async-start | bytes 8388608
  665.5 25.7 %copy-start.76 = (f32[1024,1408]{1,0:T(8,128)}, f32[1024,1408]{1,0:T(8,128)S(1)}, u32[]{:S(2)}) copy-start(f32[1024,1408]{1,0:T(8,128)S(1)} %fusion.176) | copy-start | bytes 17301508
  665.5 25.7 %slice-start.7 = ((s8[5767168]{0:T(1024)(128)(4,1)}), s8[1572864]{0:T(1024)(128)(4,1)S(1)}, s32[]{:S(2)}) async-start(s8[5767168]{0:T(1024)(128)(4,1)} %bitcast.296), calls=%async_computation.18 | async-start | bytes 3145728
  698.8 9.2 %copy-start.75 = (f32[256,1408]{1,0:T(8,128)}, f32[256,1408]{1,0:T(8,128)S(1)}, u32[]{:S(2)}) copy-start(f32[256,1408]{1,0:T(8,128)S(1)} %fusion.4) | copy-start | bytes 4325380
  (30 other events, 50.5 us)
Sparse Core Ops, SparseCore 0:
  10.2 124.2 all-gather.4
  136.6 123.1 all-gather.6
  262.6 36.1 all-reduce.17
  335.7 36.4 all-reduce.19
  379.8 49.6 all-gather.8
  432.4 23.3 reduce-scatter.2
  491.8 23.3 reduce-scatter.4
  517.9 123.0 all-gather.10

commit v2 on v1

--- a/solution.py
+++ b/solution.py
@@ -3,6 +3,8 @@
 import jax
 import jax.numpy as jnp
 from jax import lax
+from jax.experimental import pallas as pl
+from jax.experimental.pallas import tpu as pltpu
 from jax.sharding import PartitionSpec as P
 
 HDIM = 128
@@ -236,6 +238,702 @@
     )
 
 
+Z, X = 4, 2
+
+
+def z_shift(array, distance):
+    steps = [(z * X + x, (z + distance) % Z * X + x) for z in range(Z) for x in range(X)]
+    return lax.ppermute(array, "seq", steps)
+
+
+def x_swap(array):
+    return lax.ppermute(array, "seq", [(s, s ^ 1) for s in range(Z * X)])
+
+
+def core_swap(array):
+    return lax.ppermute(array, "mp", [(m, m ^ 1) for m in range(4)])
+
+
+def y_swap(array):
+    return lax.ppermute(array, "mp", [(m, m ^ 2) for m in range(4)])
+
+
+def cut(array, place, size, axis):
+    return lax.dynamic_slice_in_dim(array, place * size, size, axis)
+
+
+def in_order(first, mine, other, axis):
+    return jnp.where(
+        first, jnp.concatenate([mine, other], axis), jnp.concatenate([other, mine], axis)
+    )
+
+
+def in_place(shifted, z):
+    return [lax.select_n((z - here) % Z, *shifted) for here in range(Z)]
+
+
+def core_place():
+    return lax.axis_index("mp") % 2
+
+
+def scatter_over_mp(part):
+    rows = part.shape[0] // 4
+    core = core_place()
+    place = lax.axis_index("mp") // 2
+    pieces = part.reshape(2, 2, rows, part.shape[1])
+
+    def of_core(index):
+        return lax.dynamic_index_in_dim(pieces, index, 1, False)
+
+    mine = of_core(core) + core_swap(of_core(1 - core))
+
+    def of_y(index):
+        return lax.dynamic_index_in_dim(mine, index, 0, False)
+
+    return of_y(place) + y_swap(of_y(1 - place))
+
+
+F32, BF16 = jnp.float32, jnp.bfloat16
+MESH = pl.DeviceIdType.MESH
+ANY = pl.BlockSpec(memory_space=pl.ANY)
+TILE = 256
+VMEM_BYTES = 60 << 20
+
+
+def halves(entries):
+    high = entries.astype(BF16)
+    return high, (entries - high.astype(F32)).astype(BF16)
+
+
+def product(left, right, contract_left, contract_right):
+    return lax.dot_general(
+        left,
+        right,
+        (((contract_left,), (contract_right,)), ((), ())),
+        preferred_element_type=F32,
+    )
+
+
+def three_pass(left, right, contract_left, contract_right):
+    (left_high, left_low), (right_high, right_low) = left, right
+    return product(left_high, right_high, contract_left, contract_right) + (
+        product(left_high, right_low, contract_left, contract_right)
+        + product(left_low, right_high, contract_left, contract_right)
+    )
+
+
+def remote(src, dst, sems, index, device):
+    return pltpu.make_async_remote_copy(
+        src_ref=src,
+        dst_ref=dst,
+        send_sem=sems[0].at[index],
+        recv_sem=sems[1].at[index],
+        device_id=device,
+        device_id_type=MESH,
+    )
+
+
+def where_am_i():
+    place, part = lax.axis_index("seq"), lax.axis_index("mp")
+    return place // X, place % X, part // 2, part % 2
+
+
+class Gather:
+    spec = pl.BlockSpec(memory_space=pl.ANY)
+
+    def shape(block):
+        return (Z * X * block.shape[0], block.shape[1])
+
+    def scratch(block):
+        return [
+            pltpu.SemaphoreType.DMA((26,)),
+            pltpu.SemaphoreType.DMA((26,)),
+            pltpu.SemaphoreType.DMA((1,)),
+        ]
+
+    def __init__(self, block_ref, out_ref, send, recv, local):
+        self.block, self.out, self.sems_here, self.local = block_ref, out_ref, (send, recv), local
+        self.z, self.x, self.y, self.core = where_am_i()
+        self.rows, self.half = block_ref.shape[0], block_ref.shape[1] // 2
+
+    def device(self, z, x, core):
+        return (z * X + x, self.y * 2 + core)
+
+    def region(self, z, x, core):
+        return self.out.at[
+            pl.ds(pl.multiple_of((z * X + x) * self.rows, self.rows), self.rows),
+            pl.ds(pl.multiple_of(core * self.half, self.half), self.half),
+        ]
+
+    def own(self):
+        return self.block.at[:, pl.ds(pl.multiple_of(self.core * self.half, self.half), self.half)]
+
+    def along(self, way, step, arriving):
+        source = self.z - way * (step if arriving else step - 1)
+        src = self.own() if step == 1 and not arriving else self.region(source, self.x, self.core)
+        return remote(
+            src,
+            self.region(source, self.x, self.core),
+            self.sems_here,
+            (0 if way > 0 else 3) + step - 1,
+            self.device(self.z + way, self.x, self.core),
+        )
+
+    def across(self, way, step, arriving):
+        source = self.z - way * step
+        x = 1 - self.x if arriving else self.x
+        src = self.own() if step == 0 and not arriving else self.region(source, x, self.core)
+        return remote(
+            src,
+            self.region(source, x, self.core),
+            self.sems_here,
+            6 + (0 if step == 0 else (0 if way > 0 else 3) + step),
+            self.device(self.z, 1 - self.x, self.core),
+        )
+
+    def inside(self, way, step, other_x, arriving):
+        source = self.z - way * step
+        x = 1 - self.x if other_x else self.x
+        core = 1 - self.core if arriving else self.core
+        region = self.region(source, x, core)
+        index = (0 if way > 0 else 3) + step
+        return remote(
+            region,
+            region,
+            self.sems_here,
+            13 + index if other_x else 13 + 6 + index,
+            self.device(self.z, self.x, 1 - self.core),
+        )
+
+    def holds(self, way, step):
+        source = self.z - way * step
+        return (source >= 0) & (source < Z)
+
+    def goes_on(self, way, step):
+        return self.holds(way, step - 1) & (self.z + way >= 0) & (self.z + way < Z)
+
+    def when_holds(self, way, step, action):
+        if step == 0:
+            action()
+        else:
+            pl.when(self.holds(way, step))(action)
+
+    def greet(self):
+        barrier = pltpu.get_barrier_semaphore()
+
+        def signal(device):
+            pl.semaphore_signal(barrier, inc=1, device_id=device, device_id_type=MESH)
+
+        signal(self.device(self.z, 1 - self.x, self.core))
+        signal(self.device(self.z, self.x, 1 - self.core))
+        for way in (1, -1):
+            ahead = (self.z + way >= 0) & (self.z + way < Z)
+            pl.when(ahead)(lambda way=way: signal(self.device(self.z + way, self.x, self.core)))
+        neighbours = jnp.where(self.z > 0, 1, 0) + jnp.where(self.z < Z - 1, 1, 0)
+        pl.semaphore_wait(barrier, 2 + neighbours)
+
+    def own_copy(self):
+        row = pl.multiple_of((self.z * X + self.x) * self.rows, self.rows)
+        return pltpu.make_async_copy(
+            self.block, self.out.at[pl.ds(row, self.rows), :], self.local.at[0]
+        )
+
+    def begin(self):
+        self.greet()
+        self.own_copy().start()
+        for way in (1, -1):
+            pl.when(self.goes_on(way, 1))(lambda way=way: self.along(way, 1, False).start())
+        self.across(1, 0, False).start()
+
+    def arrive_along(self, step):
+        for way in (1, -1):
+
+            def action(way=way):
+                self.along(way, step, True).wait_recv()
+                if step < Z - 1:
+                    pl.when(self.goes_on(way, step + 1))(
+                        lambda: self.along(way, step + 1, False).start()
+                    )
+                self.across(way, step, False).start()
+                self.inside(way, step, False, False).start()
+
+            self.when_holds(way, step, action)
+
+    def arrive_across(self, step):
+        for way in (1, -1) if step else (1,):
+
+            def action(way=way):
+                self.across(way, step, True).wait_recv()
+                self.inside(way, step, True, False).start()
+
+            self.when_holds(way, step, action)
+
+    def finish(self):
+        self.own_copy().wait()
+        for way in (1, -1):
+            for step in range(1, Z):
+                pl.when(self.goes_on(way, step))(
+                    lambda way=way, step=step: self.along(way, step, False).wait_send()
+                )
+        for step in range(Z):
+            for way in (1, -1) if step else (1,):
+
+                def action(way=way, step=step):
+                    self.across(way, step, False).wait_send()
+                    self.inside(way, step, True, False).wait_send()
+                    self.inside(way, step, True, True).wait_recv()
+                    if step:
+                        self.inside(way, step, False, False).wait_send()
+                        self.inside(way, step, False, True).wait_recv()
+
+                self.when_holds(way, step, action)
+
+    def events(self):
+        def round_of(step):
+            def event():
+                self.arrive_along(step)
+                self.arrive_across(step - 1)
+
+            return event
+
+        return [round_of(step) for step in range(1, Z)] + [
+            lambda: self.arrive_across(Z - 1),
+            self.finish,
+        ]
+
+
+def move_only(kind, array, collective_id):
+    def kernel(array_ref, out_ref, *scratch):
+        move = kind(array_ref, out_ref, *scratch)
+        move.begin()
+        for event in move.events():
+            event()
+
+    return pl.pallas_call(
+        kernel,
+        out_shape=jax.ShapeDtypeStruct(kind.shape(array), F32),
+        in_specs=[kind.spec],
+        out_specs=kind.spec,
+        scratch_shapes=kind.scratch(array),
+        compiler_params=pltpu.CompilerParams(collective_id=collective_id, has_side_effects=True),
+        cost_estimate=pl.CostEstimate(flops=0, bytes_accessed=16 << 20, transcendentals=0),
+    )(array)
+
+
+def load_halves(src_ref, high_ref, low_ref, stage_ref, sem):
+    rows = stage_ref.shape[1]
+    count = src_ref.shape[0] // rows
+
+    def fetch(index):
+        return pltpu.make_async_copy(
+            src_ref.at[pl.ds(index * rows, rows), :], stage_ref.at[index % 2], sem.at[index % 2]
+        )
+
+    fetch(0).start()
+    for index in range(count):
+        if index + 1 < count:
+            fetch(index + 1).start()
+        fetch(index).wait()
+        high, low = halves(stage_ref[index % 2])
+        high_ref[index * rows : (index + 1) * rows, :] = high
+        low_ref[index * rows : (index + 1) * rows, :] = low
+
+
+def at_steps(events, steps):
+    step = pl.program_id(0)
+    for event, when in zip(events, steps, strict=True):
+        pl.when(step == when)(event)
+
+
+def beside_product(kind, array, left, weights, by_rows, collective_id, steps):
+    rows, inner = left.shape
+    count = len(weights)
+    if count > 1:
+        tiles, columns = count, count * TILE
+    else:
+        columns = weights[0].shape[0 if by_rows else 1]
+        tiles = pl.cdiv(columns, TILE)
+
+    def kernel(array_ref, left_ref, *refs):
+        weight_refs, refs = refs[:count], refs[count:]
+        out_ref, product_ref, high_ref, low_ref, stage_ref, stage_sem, weight_buf, weight_sem, *scratch = refs
+        move = kind(array_ref, out_ref, *scratch)
+        step = pl.program_id(0)
+        pl.when(step == 0)(move.begin)
+        if count > 1:
+            start = pl.multiple_of((lax.axis_index("seq") % X) * TILE, TILE)
+
+            def fetch(index):
+                return pltpu.make_async_copy(
+                    weight_refs[index].at[:, pl.ds(start, TILE)],
+                    weight_buf.at[index % 2],
+                    weight_sem.at[index % 2],
+                )
+
+            pl.when(step == 0)(fetch(0).start)
+            for index in range(count - 1):
+                pl.when(step == index)(fetch(index + 1).start)
+        pl.when(step == 0)(
+            lambda: load_halves(left_ref, high_ref, low_ref, stage_ref, stage_sem)
+        )
+        if count > 1:
+            for index in range(count):
+                pl.when(step == index)(fetch(index).wait)
+            weight = weight_buf[lax.rem(step, 2)]
+        else:
+            weight = weight_refs[0][...]
+        product_ref[...] = three_pass(
+            (high_ref[...], low_ref[...]), halves(weight), 1, 1 if by_rows else 0
+        )
+        at_steps(move.events(), steps)
+
+    if count > 1:
+        weight_spec = ANY
+    elif by_rows:
+        weight_spec = pl.BlockSpec((TILE, inner), lambda tile: (tile, 0))
+    else:
+        weight_spec = pl.BlockSpec((inner, TILE), lambda tile: (0, tile))
+    return pl.pallas_call(
+        kernel,
+        grid=(tiles,),
+        out_shape=[
+            jax.ShapeDtypeStruct(kind.shape(array), F32),
+            jax.ShapeDtypeStruct((rows, columns), F32),
+        ],
+        in_specs=[kind.spec, ANY] + [weight_spec] * count,
+        out_specs=[kind.spec, pl.BlockSpec((rows, TILE), lambda tile: (0, tile))],
+        scratch_shapes=[
+            pltpu.VMEM((rows, inner), BF16),
+            pltpu.VMEM((rows, inner), BF16),
+            pltpu.VMEM((2, 128, inner), F32),
+            pltpu.SemaphoreType.DMA((2,)),
+            pltpu.VMEM((2, inner, TILE) if count > 1 else (8, 128), F32),
+            pltpu.SemaphoreType.DMA((2,)),
+            *kind.scratch(array),
+        ],
+        compiler_params=pltpu.CompilerParams(
+            collective_id=collective_id, has_side_effects=True, vmem_limit_bytes=VMEM_BYTES
+        ),
+        cost_estimate=pl.CostEstimate(
+            flops=6 * rows * inner * columns, bytes_accessed=48 << 20, transcendentals=0
+        ),
+    )(array, left, *weights)
+
+
+class Sum:
+    spec = pl.BlockSpec(memory_space=pltpu.VMEM)
+
+    def shape(part):
+        return part.shape
+
+    def scratch(part):
+        rows, half = part.shape[0], part.shape[1] // 2
+        return [
+            pltpu.VMEM((4, rows, half), F32),
+            pltpu.SemaphoreType.DMA((3,)),
+            pltpu.SemaphoreType.DMA((3,)),
+        ]
+
+    def __init__(self, part_ref, out_ref, landing, send, recv):
+        self.part, self.out, self.landing, self.sems_here = part_ref, out_ref, landing, (send, recv)
+        self.z, self.x, self.y, self.core = where_am_i()
+        self.half = part_ref.shape[1] // 2
+
+    def columns(self, ref, core):
+        return ref.at[:, pl.ds(pl.multiple_of(core * self.half, self.half), self.half)]
+
+    def device(self, y, core):
+        return (self.z * X + self.x, y * 2 + core)
+
+    def first(self):
+        return remote(
+            self.columns(self.part, 1 - self.core),
+            self.landing.at[0],
+            self.sems_here,
+            0,
+            self.device(self.y, 1 - self.core),
+        )
+
+    def second(self):
+        return remote(
+            self.landing.at[1],
+            self.landing.at[2],
+            self.sems_here,
+            1,
+            self.device(1 - self.y, self.core),
+        )
+
+    def third(self):
+        return remote(
+            self.landing.at[1],
+            self.landing.at[3],
+            self.sems_here,
+            2,
+            self.device(self.y, 1 - self.core),
+        )
+
+    def begin(self):
+        barrier = pltpu.get_barrier_semaphore()
+        for device in (self.device(self.y, 1 - self.core), self.device(1 - self.y, self.core)):
+            pl.semaphore_signal(barrier, inc=1, device_id=device, device_id_type=MESH)
+        pl.semaphore_wait(barrier, 2)
+        self.first().start()
+
+    def to_y(self):
+        self.first().wait()
+        self.landing[1] = self.columns(self.part, self.core)[...] + self.landing[0]
+        self.second().start()
+
+    def back(self):
+        self.second().wait()
+        self.landing[1] = self.landing[1] + self.landing[2]
+        self.third().start()
+
+    def finish(self):
+        self.third().wait()
+        self.columns(self.out, self.core)[...] = self.landing[1]
+        self.columns(self.out, 1 - self.core)[...] = self.landing[3]
+
+    def events(self):
+        return [self.to_y, self.back, self.finish]
+
+
+def hidden_and_sum(part, normed_two, grad_hidden, w_gate, w_up, normed_cols, cot_cols, collective_id, steps):
+    rows, inner = normed_two.shape
+    columns = w_gate.shape[1]
+    narrow = normed_cols.shape[1]
+    tiles = pl.cdiv(columns, TILE)
+
+    def kernel(
+        part_ref, normed_ref, e_ref, gate_ref, up_ref, normed_cols_ref, cot_cols_ref,
+        sum_ref, grad_gate_ref, grad_up_ref, grad_down_ref,
+        high_ref, low_ref, stage_ref, stage_sem, *sum_scratch,
+    ):
+        total = Sum(part_ref, sum_ref, *sum_scratch)
+        step = pl.program_id(0)
+        pl.when(step == 0)(total.begin)
+        pl.when(step == 0)(
+            lambda: load_halves(normed_ref, high_ref, low_ref, stage_ref, stage_sem)
+        )
+        normed = high_ref[...], low_ref[...]
+        a = three_pass(normed, halves(gate_ref[...]), 1, 0)
+        b = three_pass(normed, halves(up_ref[...]), 1, 0)
+        gate = jax.nn.sigmoid(a)
+        silu_a = a * gate
+        e = e_ref[...]
+        cols = halves(normed_cols_ref[...])
+        grad_gate_ref[...] = three_pass(
+            cols, halves(e * b * (gate * (1.0 + a * (1.0 - gate)))), 0, 0
+        )
+        grad_up_ref[...] = three_pass(cols, halves(e * silu_a), 0, 0)
+        grad_down_ref[...] = three_pass(halves(silu_a * b), halves(cot_cols_ref[...]), 0, 0)
+        at_steps(total.events(), steps)
+
+    whole = pl.BlockSpec(memory_space=pltpu.VMEM)
+    by_column = pl.BlockSpec((inner, TILE), lambda tile: (0, tile))
+    grad_spec = pl.BlockSpec((narrow, TILE), lambda tile: (0, tile))
+    return pl.pallas_call(
+        kernel,
+        grid=(tiles,),
+        out_shape=[
+            jax.ShapeDtypeStruct(part.shape, F32),
+            jax.ShapeDtypeStruct((narrow, columns), F32),
+            jax.ShapeDtypeStruct((narrow, columns), F32),
+            jax.ShapeDtypeStruct((columns, narrow), F32),
+        ],
+        in_specs=[
+            Sum.spec, ANY, pl.BlockSpec((rows, TILE), lambda tile: (0, tile)), by_column, by_column, whole, whole,
+        ],
+        out_specs=[
+            whole, grad_spec, grad_spec, pl.BlockSpec((TILE, narrow), lambda tile: (tile, 0)),
+        ],
+        scratch_shapes=[
+            pltpu.VMEM((rows, inner), BF16),
+            pltpu.VMEM((rows, inner), BF16),
+            pltpu.VMEM((2, 128, inner), F32),
+            pltpu.SemaphoreType.DMA((2,)),
+        ]
+        + Sum.scratch(part),
+        compiler_params=pltpu.CompilerParams(
+            collective_id=collective_id, has_side_effects=True, vmem_limit_bytes=VMEM_BYTES
+        ),
+        cost_estimate=pl.CostEstimate(
+            flops=15 * rows * inner * columns, bytes_accessed=48 << 20, transcendentals=0
+        ),
+    )(part, normed_two, grad_hidden, w_gate, w_up, normed_cols, cot_cols)
+
+
+def fast_shards(
+    tokens_in,
+    cotangent,
+    lengths,
+    lower_bound,
+    query_weight,
+    forget_weight,
+    input_weight,
+    gate_weight,
+    out_weight,
+    swiglu_gate,
+    swiglu_up,
+    swiglu_down,
+    first_gain,
+    group_gain,
+    second_gain,
+):
+    place = lax.axis_index("seq")
+    z, x = place // X, place % X
+    core = core_place()
+    rows, model = tokens_in.shape
+    wide = model // Z
+    narrow = model // (Z * X)
+    width = query_weight.shape[1] // X
+    share_rows = rows // 4
+
+    def share(entries):
+        return cut(entries, lax.axis_index("mp"), share_rows, 0)
+
+    def own(entries, at):
+        return cut(entries, at, rows, 0)
+
+    token_count = rows * Z * X
+    positions = jnp.arange(token_count, dtype=jnp.int32)
+    offsets = jnp.cumsum(lengths) - lengths
+    segment = jnp.sum((positions[:, None] >= offsets[None, :]).astype(jnp.int32), 1) - 1
+
+    all_tokens = move_only(Gather, tokens_in, 1)
+    normed_one = all_tokens * rms(all_tokens) * first_gain
+    in_weights = (query_weight, forget_weight, input_weight, gate_weight)
+    all_cotangent, projected = beside_product(
+        Gather, cotangent, normed_one, in_weights, False, 2, (1, 2, 3, 3, 3)
+    )
+    mixer, mixer_back = jax.vjp(
+        partial(mixer_all, lower_bound=cut(lower_bound, x, width, 0), segment=segment),
+        *jnp.split(projected, 4, 1),
+        cut(group_gain, x, width, 0),
+    )
+    mixer_other = x_swap(own(mixer, place + 1 - 2 * x))
+    mixer_part = dot(own(mixer, place), cut(out_weight, x, width, 0), 1, 0) + dot(
+        mixer_other, cut(out_weight, 1 - x, width, 0), 1, 0
+    )
+    mixer_sum, grad_hidden_all = beside_product(
+        Sum, mixer_part, all_cotangent, (swiglu_down,), True, 3, (0, 4, 5)
+    )
+    residual = tokens_in + mixer_sum
+    scale_two = rms(residual)
+    normed_two = residual * scale_two * second_gain
+    all_normed_two = move_only(Gather, normed_two, 4)
+
+    a = dot(normed_two, swiglu_gate, 1, 0)
+    b = dot(normed_two, swiglu_up, 1, 0)
+    silu_a = jax.nn.silu(a)
+    e = own(grad_hidden_all, place)
+    normed_two_part = dot(e * b * silu_grad(a), swiglu_gate, 1, 1) + dot(
+        e * silu_a, swiglu_up, 1, 1
+    )
+    ffn_part = dot(silu_a * b, swiglu_down, 1, 0)
+    grad_normed_two, grad_sgate, grad_sup, grad_sdown = hidden_and_sum(
+        normed_two_part,
+        all_normed_two,
+        grad_hidden_all,
+        swiglu_gate,
+        swiglu_up,
+        cut(all_normed_two, place, narrow, 1),
+        cut(all_cotangent, place, narrow, 1),
+        5,
+        (0, 2, 3),
+    )
+    pulled = grad_normed_two * second_gain
+    grad_residual = (
+        cotangent
+        + scale_two * pulled
+        - residual * scale_two**3 * jnp.mean(pulled * residual, -1, keepdims=True)
+    )
+    output = share(residual) + scatter_over_mp(ffn_part)
+
+    grad_mixer_own = dot(grad_residual, out_weight, 1, 1)
+    grad_mixer_here = jnp.stack(
+        [cut(grad_mixer_own, x, width, 1), x_swap(cut(grad_mixer_own, 1 - x, width, 1))]
+    )
+    at_z = [grad_mixer_here] + [z_shift(grad_mixer_here, distance) for distance in range(1, Z)]
+    grad_mixer = jnp.stack(in_place(at_z, z))
+    grad_mixer = jnp.where(x == 0, grad_mixer, grad_mixer[:, ::-1]).reshape(token_count, width)
+
+    half = wide // 2
+    residual_parts = [
+        cut(grad_residual, ((z + distance) % Z) * 2 + core, half, 1) for distance in range(Z)
+    ]
+    residual_parts = [residual_parts[0]] + [
+        z_shift(residual_parts[distance], distance) for distance in range(1, Z)
+    ]
+    residual_mine = jnp.stack(in_place(residual_parts, z))
+    residual_mine = in_order(
+        x == 0, residual_mine[:, None], x_swap(residual_mine)[:, None], 1
+    ).reshape(token_count, half)
+    residual_cols = in_order(core == 0, residual_mine, core_swap(residual_mine), 1)
+
+    *grad_rows, grad_group = mixer_back(grad_mixer)
+    grad_group = jnp.where(
+        x == 0,
+        jnp.concatenate([grad_group, jnp.zeros_like(grad_group)]),
+        jnp.concatenate([jnp.zeros_like(grad_group), grad_group]),
+    )
+    grad_group = cut(
+        grad_group + x_swap(grad_group), place, group_gain.shape[0] // (Z * X), 0
+    )
+    others = x_swap(jnp.stack([own(part, place + 1 - 2 * x) for part in grad_rows]))
+    normed_part = 0.0
+    for index, weight in enumerate(in_weights):
+        normed_part = normed_part + dot(
+            in_order(x == 0, own(grad_rows[index], place), others[index], 1), weight, 1, 1
+        )
+    grad_normed_one = scatter_over_mp(normed_part)
+    tokens_share = share(tokens_in)
+    scale_one = rms(tokens_share)
+    pulled_one = grad_normed_one * first_gain
+    grad_tokens = (
+        share(grad_residual)
+        + scale_one * pulled_one
+        - tokens_share * scale_one**3 * jnp.mean(pulled_one * tokens_share, -1, keepdims=True)
+    )
+
+    normed_one_cols = cut(normed_one, z, wide, 1)
+    blocks = [dot(normed_one_cols, part, 0, 0) for part in grad_rows]
+    block_mine = jnp.stack([cut(block, x, narrow, 0) for block in blocks])
+    block_other = x_swap(jnp.stack([cut(block, 1 - x, narrow, 0) for block in blocks]))
+    weight_grads = in_order(x == 0, block_mine, block_other, 2)
+    out_block = dot(mixer, residual_cols, 0, 0)
+    grad_outw = in_order(
+        x == 0, cut(out_block, x, narrow, 1), x_swap(cut(out_block, 1 - x, narrow, 1)), 0
+    )
+
+    first_sum = 0.0
+    for index, weight in enumerate(in_weights):
+        first_sum = first_sum + jnp.sum(cut(weight, place, narrow, 0) * weight_grads[index], 1)
+    second_sum = jnp.sum(
+        cut(swiglu_gate, place, narrow, 0) * grad_sgate
+        + cut(swiglu_up, place, narrow, 0) * grad_sup,
+        1,
+    )
+    sums = jnp.stack([first_sum, second_sum])
+    sums = sums + core_swap(sums)
+    sums = sums + y_swap(sums)
+    return (
+        output,
+        grad_tokens,
+        weight_grads[0],
+        weight_grads[1],
+        weight_grads[2],
+        weight_grads[3],
+        grad_outw,
+        grad_sgate,
+        grad_sup,
+        grad_sdown,
+        sums[0] / cut(first_gain, place, narrow, 0),
+        grad_group,
+        sums[1] / cut(second_gain, place, narrow, 0),
+    )
+
+
 def solution(mesh):
     in_specs = (
         P("seq", None),
@@ -269,4 +967,6 @@
         P(("mp", "seq")),
         P("seq"),
     )
-    return jax.shard_map(shards, mesh=mesh, in_specs=in_specs, out_specs=out_specs, check_vma=False)
+    small = (mesh.shape["seq"], mesh.shape["mp"]) == (Z * X, 4)
+    body = fast_shards if small else shards
+    return jax.shard_map(body, mesh=mesh, in_specs=in_specs, out_specs=out_specs, check_vma=False)

time: 743 us -> 524 us (0.71)
  waiting for transfers between devices: 368 us -> 49.1 us
  Pallas kernels: 0 us -> 259 us
  matrix products: 259 us -> 85.2 us
  starting transfers between devices: 4.95 us -> 22.5 us
  other arithmetic: 31.1 us -> 48.3 us
  between operations: 15.6 us -> 2.92 us
    all_gather x4 -> x0, waiting for transfers between devices: 296 us -> none  [gather_tokens(): return lax.all_gather(block, 'seq', axis=0, tiled=True)]
    pallas_call x0 -> x5, Pallas kernels: none -> 259 us  [the longest x2 105 us: move_only(): pl.pallas_call(kernel, out_shape=jax.ShapeDtypeStruct(kind.shape(array),...]
    dot_general x26 -> x17, matrix products: 227 us -> 63.8 us  [dot(): lax.dot_general(left, right, (((contract_left,), (contract_right,)), ((),...]
    psum x2 -> x0, waiting for transfers between devices: 49.1 us -> none  [the longest x1 36.5 us: shards(): lax.psum(dot(grad_a, swiglu_gate, 1, 1) + dot(grad_b, swiglu_up, 1, 1), '...]
    ppermute x0 -> x20, waiting for transfers between devices: none -> 49.1 us  [the longest x6 22.2 us: z_shift(): return lax.ppermute(array, 'seq', steps)]
    dynamic_slice x3 -> x21, local copies, waits for them, and re-layouts: 2.1 us -> 24.9 us  [cut(): return lax.dynamic_slice_in_dim(array, place * size, size, axis)]
    ppermute x0 -> x20, starting transfers between devices: none -> 22.5 us  [the longest x6 11 us: z_shift(): return lax.ppermute(array, 'seq', steps)]
    all_to_all x1 -> x0, waiting for transfers between devices: 20.2 us -> none  [shards(): residual_cols = lax.all_to_all(grad_residual, 'seq', 1, 0, tiled=True)]
  transfers between devices with their start and end apart: 9 -> 20, of which waited for: 7 -> 10; matrix products, arithmetic and copies ran while one was open for 27% -> 17% of each run, Pallas kernels for 0% -> 0%
where the time goes in v2:
time: 524 us; the launch traced here: 518 us
  Pallas kernels  259 us (49%)
  matrix products  85.2 us (16%)
  local copies, waits for them, and re-layouts  50.8 us (10%)
  waiting for transfers between devices  49.1 us (9%)
  other arithmetic  48.3 us (9%)
  starting transfers between devices  22.5 us (4%)
    pallas_call x2, Pallas kernels, move_only(): pl.pallas_call(kernel, out_shape=jax.ShapeDtypeStruct(kind.shape(array),...  105 us
    pallas_call x2, Pallas kernels, beside_product(): pl.pallas_call(kernel, grid=(tiles,), out_shape=[jax.ShapeDtypeStruct(kin...  88.5 us
    pallas_call x1, Pallas kernels, hidden_and_sum(): pl.pallas_call(kernel, grid=(tiles,), out_shape=[jax.ShapeDtypeStruct(par...  65.7 us
    dot_general x17, matrix products, dot(): lax.dot_general(left, right, (((contract_left,), (contract_right,)), ((),...  63.8 us
    dynamic_slice x21, local copies, waits for them, and re-layouts, cut(): return lax.dynamic_slice_in_dim(array, place * size, size, axis)  24.9 us
    ppermute x6, waiting for transfers between devices, z_shift(): return lax.ppermute(array, 'seq', steps)  22.2 us
    ppermute x7, waiting for transfers between devices, x_swap(): return lax.ppermute(array, 'seq', [(s, s ^ 1) for s in range(Z * X)])  17.4 us
    ppermute x6, starting transfers between devices, z_shift(): return lax.ppermute(array, 'seq', steps)  11 us
  transfers between devices with their start and end apart: 20, of which 10 were waited for; matrix products, arithmetic and copies ran while one was open for 17% of the time, Pallas kernels for 0%

profile of v2, /device:TPU:8, one launch (start us, length us, event | category | flops | bytes accessed | tf_op | source)
XLA Modules:
  0.0 517.7 jit_solution(16732762979066695248)
XLA Ops:
  5.4 51.8 %shard_map.246 = f32[1024,2048]{1,0:T(8,128)} custom-call(f32[128,2048]{1,0:T(8,128)} %array_ref.2), custom_call_target="tpu_custom_call" | custom-call | bytes 16777216 | tf_op jit(solution)/shard_map/pallas_call | solution.py:512
  57.2 4.1 multiply_reduce_fusion
  61.3 1.6 copy-done
  62.9 4.1 multiply_multiply_fusion.left_ref
  67.0 56.7 %shard_map.247 = (f32[1024,2048]{1,0:T(8,128)}, f32[1024,1024]{1,0:T(8,128)}) custom-call(f32[128,2048]{1,0:T(8,128)} %array_ref.3, f32[1024,2048]{1,0:T(8,128)} %multiply_multiply_fusion.left_ref, f32[2048,512]{1,0:T(8,128)} %refs_0_.2, f32[2048,512]{1,0:T(8,128)} %refs_1_.1, f32[2048,512]{1,0:T(8,128)} %refs_2_.1, f32[2048,512]{1,0:T(8,128)} %refs_3_.1), custom_call_target="tpu_custom_call" | custom-call | flops 12884901888 | bytes 50331648 | tf_op jit(solution)/shard_map/pallas_call | solution.py:596
  123.8 3.4 fusion.145
  128.3 2.1 reshape.325
  139.4 2.4 mul.694
  141.8 1.9 multiply_multiply_fusion.4
  144.8 2.1 collective-permute-start
  147.7 2.4 constant_dynamic-slice_fusion.18.cot_cols_ref
  150.1 2.4 fusion.7
  152.5 1.9 convolution_add_fusion.4.array_ref
  154.4 31.8 %shard_map.248 = (f32[128,2048]{1,0:T(8,128)}, f32[1024,1408]{1,0:T(8,128)}) custom-call(f32[128,2048]{1,0:T(8,128)} %convolution_add_fusion.4.array_ref, f32[1024,2048]{1,0:T(8,128)} %get-tuple-element.22.left_ref, f32[1408,2048]{1,0:T(8,128)} %refs_0_.3), custom_call_target="tpu_custom_call" | custom-call | flops 17716740096 | bytes 50331648 | tf_op jit(solution)/shard_map/pallas_call | solution.py:596
  189.9 52.9 %shard_map.249.normed_ref = f32[1024,2048]{1,0:T(8,128)} custom-call(f32[128,2048]{1,0:T(8,128)} %multiply_multiply_fusion.2.array_ref), custom_call_target="tpu_custom_call" | custom-call | bytes 16777216 | tf_op jit(solution)/shard_map/pallas_call | solution.py:512
  242.8 8.3 %fusion.147 = f32[128,1408]{1,0:T(8,128)S(1)} fusion(f32[128,2048]{1,0:T(8,128)} %multiply_multiply_fusion.2.array_ref, f32[2048,1408]{1,0:T(8,128)} %gate_ref.1), kind=kOutput, calls=%fused_computation.336 | convolution fusion | flops 2214592512 | bytes 13303808 | tf_op jit(solution)/shard_map/dot_general | solution.py:19
  251.2 8.0 %fusion.148 = f32[128,1408]{1,0:T(8,128)S(1)} fusion(f32[128,2048]{1,0:T(8,128)S(1)} %copy-done.9, f32[2048,1408]{1,0:T(8,128)} %up_ref.1), kind=kOutput, calls=%fused_computation.337 | convolution fusion | flops 2214592512 | bytes 13303808 | tf_op jit(solution)/shard_map/dot_general | solution.py:19
  259.2 9.0 %fusion.70 = f32[128,2048]{1,0:T(8,128)} fusion(f32[1408,2048]{1,0:T(8,128)} %refs_0_.3, f32[128,1408]{1,0:T(8,128)S(1)} %fusion.148, f32[128,1408]{1,0:T(8,128)S(1)} %fusion.147), kind=kOutput, calls=%fused_computation.123 | convolution fusion | flops 2215493632 | bytes 14024704 | tf_op jit(solution)/shard_map/dot_general | solution.py:19
  268.2 7.4 %fusion.63 = f32[128,2048]{1,0:T(8,128)S(1)} fusion(f32[2048,1408]{1,0:T(8,128)S(1)} %bitcast.316, f32[128,1408]{1,0:T(8,128)S(1)} %fusion.147, f32[128,1408]{1,0:T(8,128)S(1)} %fusion.148, f32[1024,1408]{1,0:T(8,128)} %get-tuple-element.24.e_ref, s32[]{:T(128)S(6)} %select_n.420), kind=kOutput, calls=%fused_computation.116 | convolution fusion | flops 2216214528 | bytes 14745604 | tf_op jit(solution)/shard_map/dot_general | solution.py:19
  275.6 8.2 %convolution_add_fusion.3.part_ref = f32[128,2048]{1,0:T(8,128)} fusion(f32[128,2048]{1,0:T(8,128)S(1)} %fusion.63, f32[2048,1408]{1,0:T(8,128)S(1)} %bitcast.314, f32[1024,1408]{1,0:T(8,128)} %get-tuple-element.24.e_ref, s32[]{:T(128)S(6)} %select_n.420, f32[128,1408]{1,0:T(8,128)S(1)} %fusion.147), kind=kOutput, calls=%fused_computation.5 | convolution fusion | flops 2215755776 | bytes 15073284 | tf_op jit(solution)/shard_map/dot_general | solution.py:19
  283.8 2.3 constant_dynamic-slice_fusion.19.normed_cols_ref
  286.1 65.7 %shard_map.250 = (f32[128,2048]{1,0:T(8,128)}, f32[256,1408]{1,0:T(8,128)}, f32[256,1408]{1,0:T(8,128)}, f32[1408,256]{1,0:T(8,128)}) custom-call(f32[128,2048]{1,0:T(8,128)} %convolution_add_fusion.3.part_ref, f32[1024,2048]{1,0:T(8,128)} %shard_map.249.normed_ref, f32[1024,1408]{1,0:T(8,128)} %get-tuple-element.24.e_ref, f32[2048,1408]{1,0:T(8,128)} %gate_ref.1, ...), custom_call_target="tpu_custom_call" | custom-call | flops 44291850240 | bytes 50331648 | tf_op jit(solution)/shard_map/pallas_call | solution.py:735
  351.9 1.6 multiply_reduce_fusion.3
  353.5 1.5 multiply_subtract_fusion
  355.1 2.3 fusion.149
  357.5 1.5 collective-permute-start.3
  359.7 3.4 collective-permute-start.13
  363.1 2.3 collective-permute-start.12
  366.2 2.9 add_reduce_fusion
  369.9 3.8 collective-permute-start.6
  373.8 12.0 %collective-permute-done.12 = f32[128,256]{1,0:T(8,128)S(1)} collective-permute-done((f32[128,256]{1,0:T(8,128)S(1)}, f32[128,256]{1,0:T(8,128)S(1)}, u32[]{:S(2)}, u32[]{:S(2)}) %collective-permute-start.12) | collective-permute-done | bytes 131104 | tf_op jit(solution)/shard_map/ppermute | solution.py:246
  387.1 4.5 collective-permute-done.5
  391.6 5.7 %collective-permute-done.6 = f32[2,128,256]{2,1,0:T(8,128)S(1)} collective-permute-done((f32[2,128,256]{2,1,0:T(8,128)S(1)}, f32[2,128,256]{2,1,0:T(8,128)S(1)}, u32[]{:S(2)}, u32[]{:S(2)}) %collective-permute-start.6) | collective-permute-done | bytes 262176 | tf_op jit(solution)/shard_map/ppermute | solution.py:246
  398.9 3.7 multiply_reduce_fusion.1
  402.6 1.5 reshape.330
  404.1 1.5 copy.196
  413.8 2.0 convolution_bitcast_fusion.1
  416.0 2.1 exponential_multiply_fusion
  418.1 1.8 copy.202
  420.0 1.7 fusion.17
  421.7 2.4 copy.212
  424.2 4.7 fusion.20
  429.8 2.9 fusion.9
  442.2 1.8 copy.217
  444.0 1.8 copy.216
  445.8 1.8 copy.215
  447.6 1.8 copy.219
  449.3 1.8 copy.220
  451.1 1.8 copy.218
  452.9 1.8 copy.214
  455.9 1.8 collective-permute-start.7
  464.7 3.4 collective-permute-done.2
  468.8 2.0 collective-permute-done.7
  470.9 2.2 fusion.82
  473.1 2.5 convolution_add_fusion.2
  475.6 2.2 convolution_add_fusion.1
  477.9 2.2 convolution_add_fusion
  480.3 11.7 %collective-permute-done.10 = f32[4,256,256]{2,1,0:T(8,128)S(1)} collective-permute-done((f32[4,256,256]{2,1,0:T(8,128)S(1)}, f32[4,256,256]{2,1,0:T(8,128)S(1)}, u32[]{:S(2)}, u32[]{:S(2)}) %collective-permute-start.10) | collective-permute-done | bytes 1048608 | tf_op jit(solution)/shard_map/ppermute | solution.py:250
  492.4 1.5 multiply_reduce_fusion.6
  497.4 1.5 collective-permute-done.18
  500.9 3.6 collective-permute-done.9
  505.9 1.8 collective-permute-start.16
  507.7 1.8 multiply_subtract_fusion.1
  509.4 3.7 collective-permute-done.16
  (324 shorter events, 64.1 us)
Async XLA Ops:
  4.0 119.7 %copy-start.79 = (f32[256]{0:T(256)}, f32[256]{0:T(256)S(1)}, u32[]{:S(2)}) copy-start(f32[256]{0:T(256)S(1)} %dynamic-slice_subtract_fusion) | copy-start | bytes 3076
  4.8 137.0 %copy-start.75 = (f32[256]{0:T(256)}, f32[256]{0:T(256)S(1)}, u32[]{:S(2)}) copy-start(f32[256]{0:T(256)S(1)} %dynamic_slice.165) | copy-start | bytes 3076
  5.0 126.8 %copy-start.70 = (f32[8,128]{1,0:T(8,128)}, f32[8,128]{1,0:T(8,128)S(1)}, u32[]{:S(2)}) copy-start(f32[8,128]{1,0:T(8,128)S(1)} %get-tuple-element.125) | copy-start | bytes 12292
  5.1 126.4 %copy-start.81 = (f32[8]{0:T(128)}, f32[8]{0:T(128)S(1)}, u32[]{:S(2)}) copy-start(f32[8]{0:T(128)S(1)} %slice_reduce_fusion.1) | copy-start | bytes 100
  127.7 6.6 %copy-start.10 = (f32[8,128,2,128]{3,2,1,0:T(2,128)}, f32[8,128,2,128]{3,2,1,0:T(2,128)S(1)}, u32[]{:S(2)}) copy-start(f32[8,128,2,128]{3,2,1,0:T(2,128)S(1)} %reshape.322) | copy-start | bytes 3145732
  133.0 13.9 %copy-start.17 = (f32[8,2,128,128]{2,3,1,0:T(8,128)}, f32[8,2,128,128]{2,3,1,0:T(8,128)S(1)}, u32[]{:S(2)}) copy-start(f32[8,2,128,128]{2,3,1,0:T(8,128)S(1)} %fusion.53) | copy-start | bytes 3145732
  137.0 6.7 %copy-start.12 = (f32[8,128,2,128]{1,3,2,0:T(8,128)}, f32[8,128,2,128]{1,3,2,0:T(8,128)S(1)}, u32[]{:S(2)}) copy-start(f32[8,128,2,128]{1,3,2,0:T(8,128)S(1)} %get-tuple-element.135) | copy-start | bytes 3145732
  137.0 6.7 %copy-start.59 = (f32[8,128,2]{1,2,0:T(2,128)}, f32[8,128,2]{1,2,0:T(2,128)S(1)}, u32[]{:S(2)}) copy-start(f32[8,128,2]{1,2,0:T(2,128)S(1)} %get-tuple-element.134) | copy-start | bytes 24580
  139.4 10.7 %copy-start.19 = (f32[8,128,2,128]{3,2,1,0:T(2,128)}, f32[8,128,2,128]{3,2,1,0:T(2,128)S(1)}, u32[]{:S(2)}) copy-start(f32[8,128,2,128]{3,2,1,0:T(2,128)S(1)} %copy.190) | copy-start | bytes 3145732
  144.8 7.7 %collective-permute-start = (f32[128,256]{1,0:T(8,128)}, f32[128,256]{1,0:T(8,128)S(1)}, u32[]{:S(2)}, u32[]{:S(2)}) collective-permute-start(f32[128,256]{1,0:T(8,128)} %constant_dynamic-slice_fusion.20), channel_id=1, source_target_pairs={{0,4},{4,0},{8,12},{12,8},{16,20},{20,16},{24,28},{28,24},{1,5},{5... | collective-permute-start | bytes 393224 | tf_op jit(solution)/shard_map/ppermute | solution.py:250
  154.4 31.8 %copy-start.27 = (f32[128,2048]{1,0:T(8,128)S(1)}, f32[128,2048]{1,0:T(8,128)}, u32[]{:S(2)}) copy-start(f32[128,2048]{1,0:T(8,128)} %array_ref.2) | copy-start | bytes 3145732
  154.4 34.4 %copy-start.55 = (f32[2048]{0:T(1024)S(1)}, f32[2048]{0:T(1024)}, u32[]{:S(2)}) copy-start(f32[2048]{0:T(1024)} %param.29) | copy-start | bytes 24580
  189.9 78.3 %slice-start.3 = ((s8[11534336]{0:T(1024)(128)(4,1)}), s8[3145728]{0:T(1024)(128)(4,1)S(1)}, s32[]{:S(2)}) async-start(s8[11534336]{0:T(1024)(128)(4,1)} %bitcast.315), calls=%async_computation.3 | async-start | bytes 6291456
  242.8 8.3 %copy-start.9 = (f32[128,2048]{1,0:T(8,128)S(1)}, f32[128,2048]{1,0:T(8,128)}, u32[]{:S(2)}) copy-start(f32[128,2048]{1,0:T(8,128)} %multiply_multiply_fusion.2.array_ref) | copy-start | bytes 3145732
  242.8 25.4 %slice-start.4 = ((s8[11534336]{0:T(1024)(128)(4,1)}), s8[4194304]{0:T(1024)(128)(4,1)S(1)}, s32[]{:S(2)}) async-start(s8[11534336]{0:T(1024)(128)(4,1)} %bitcast.315), calls=%async_computation.4 | async-start | bytes 8388608
  251.1 17.1 %slice-start.5 = ((s8[11534336]{0:T(1024)(128)(4,1)}), s8[4194304]{0:T(1024)(128)(4,1)S(1)}, s32[]{:S(2)}) async-start(s8[11534336]{0:T(1024)(128)(4,1)} %bitcast.315), calls=%async_computation.5 | async-start | bytes 8388608
  259.2 16.4 %slice-start = ((s8[11534336]{0:T(1024)(128)(4,1)}), s8[4194304]{0:T(1024)(128)(4,1)S(1)}, s32[]{:S(2)}) async-start(s8[11534336]{0:T(1024)(128)(4,1)} %bitcast.313), calls=%async_computation | async-start | bytes 8388608
  259.2 16.4 %slice-start.1 = ((s8[11534336]{0:T(1024)(128)(4,1)}), s8[4194304]{0:T(1024)(128)(4,1)S(1)}, s32[]{:S(2)}) async-start(s8[11534336]{0:T(1024)(128)(4,1)} %bitcast.313), calls=%async_computation.1 | async-start | bytes 8388608
  268.2 7.4 %slice-start.2 = ((s8[11534336]{0:T(1024)(128)(4,1)}), s8[3145728]{0:T(1024)(128)(4,1)S(1)}, s32[]{:S(2)}) async-start(s8[11534336]{0:T(1024)(128)(4,1)} %bitcast.313), calls=%async_computation.2 | async-start | bytes 6291456
  286.1 65.8 %copy-start.6 = (f32[128,2048]{1,0:T(8,128)S(1)}, f32[128,2048]{1,0:T(8,128)}, u32[]{:S(2)}) copy-start(f32[128,2048]{1,0:T(8,128)} %copy-done.5) | copy-start | bytes 3145732
  286.1 65.8 %copy-start.56 = (f32[2048]{0:T(1024)S(1)}, f32[2048]{0:T(1024)}, u32[]{:S(2)}) copy-start(f32[2048]{0:T(1024)} %param.29) | copy-start | bytes 24580
  286.1 67.4 %copy-start.49 = (f32[128,2048]{1,0:T(8,128)S(1)}, f32[128,2048]{1,0:T(8,128)}, u32[]{:S(2)}) copy-start(f32[128,2048]{1,0:T(8,128)} %array_ref.3) | copy-start | bytes 3145732
  286.1 67.4 %copy-start.84 = (f32[128]{0:T(128)S(1)}, f32[128]{0:T(128)}, u32[]{:S(2)}) copy-start(f32[128]{0:T(128)} %copy-done.83) | copy-start | bytes 1540
  286.1 67.4 %copy-start.85 = (f32[128]{0:T(128)S(1)}, f32[128]{0:T(128)}, u32[]{:S(2)}) copy-start(f32[128]{0:T(128)} %get-tuple-element.130) | copy-start | bytes 1540
  355.1 30.7 %copy-start.26 = (f32[128,2048]{1,0:T(8,128)}, f32[128,2048]{1,0:T(8,128)S(1)}, u32[]{:S(2)}) copy-start(f32[128,2048]{1,0:T(8,128)S(1)} %multiply_subtract_fusion) | copy-start | bytes 3145732
  355.1 10.3 %copy-start.43 = (f32[128,2048]{1,0:T(8,128)S(1)}, f32[128,2048]{1,0:T(8,128)}, u32[]{:S(2)}) copy-start(f32[128,2048]{1,0:T(8,128)} %fusion.70) | copy-start | bytes 3145732
  355.1 11.1 %copy-start.29 = (f32[256,1408]{1,0:T(8,128)S(1)}, f32[256,1408]{1,0:T(8,128)}, u32[]{:S(2)}) copy-start(f32[256,1408]{1,0:T(8,128)} %get-tuple-element.162) | copy-start | bytes 4325380
  355.1 11.1 %copy-start.31 = (f32[256,1408]{1,0:T(8,128)S(1)}, f32[256,1408]{1,0:T(8,128)}, u32[]{:S(2)}) copy-start(f32[256,1408]{1,0:T(8,128)} %get-tuple-element.161) | copy-start | bytes 4325380
  357.5 11.7 %collective-permute-start.3 = (f32[128,256]{1,0:T(8,128)S(1)}, f32[128,256]{1,0:T(8,128)S(1)}, u32[]{:S(2)}, u32[]{:S(2)}) collective-permute-start(f32[128,256]{1,0:T(8,128)S(1)} %get-tuple-element.114), channel_id=1, source_target_pairs={{0,4},{4,0},{8,12},{12,8},{16,20},{20,16},{24,28},{28,24},{1,5},{5... | collective-permute-start | bytes 393224 | tf_op jit(solution)/shard_map/ppermute | solution.py:250
  359.0 10.9 %collective-permute-start.11 = (f32[128,256]{1,0:T(8,128)S(1)}, f32[128,256]{1,0:T(8,128)S(1)}, u32[]{:S(2)}, u32[]{:S(2)}) collective-permute-start(f32[128,256]{1,0:T(8,128)S(1)} %get-tuple-element.80), channel_id=1, source_target_pairs={{0,8},{4,12},{8,16},{12,20},{16,24},{20,28},{24,0},{28,4},{1,9},{5... | collective-permute-start | bytes 393224 | tf_op jit(solution)/shard_map/ppermute | solution.py:246
  359.7 14.0 %collective-permute-start.13 = (f32[128,256]{1,0:T(8,128)S(1)}, f32[128,256]{1,0:T(8,128)S(1)}, u32[]{:S(2)}, u32[]{:S(2)}) collective-permute-start(f32[128,256]{1,0:T(8,128)S(1)} %get-tuple-element.81), channel_id=1, source_target_pairs={{0,24},{4,28},{8,0},{12,4},{16,8},{20,12},{24,16},{28,20},{1,25},{... | collective-permute-start | bytes 393224 | tf_op jit(solution)/shard_map/ppermute | solution.py:246
  363.1 22.7 %collective-permute-start.12 = (f32[128,256]{1,0:T(8,128)S(1)}, f32[128,256]{1,0:T(8,128)S(1)}, u32[]{:S(2)}, u32[]{:S(2)}) collective-permute-start(f32[128,256]{1,0:T(8,128)S(1)} %get-tuple-element.82), channel_id=1, source_target_pairs={{0,16},{4,20},{8,24},{12,28},{16,0},{20,4},{24,8},{28,12},{1,17},{... | collective-permute-start | bytes 393224 | tf_op jit(solution)/shard_map/ppermute | solution.py:246
  369.2 90.2 %collective-permute-start.1 = (f32[2,32,2048]{2,1,0:T(8,128)}, f32[2,32,2048]{2,1,0:T(8,128)}, u32[]{:S(2)}, u32[]{:S(2)}) collective-permute-start(f32[2,32,2048]{2,1,0:T(8,128)} %dynamic-slice_bitcast_fusion.1), channel_id=1, source_target_pairs={{0,1},{1,0},{2,3},{3,2},{4,5},{5,4},{6,7},{7,6},{8,9},{9,8},{10,11... | collective-permute-start | bytes 1572872 | tf_op jit(solution)/shard_map/ppermute | solution.py:254
  369.2 22.4 %collective-permute-start.5 = (f32[2,128,256]{2,1,0:T(8,128)S(1)}, f32[2,128,256]{2,1,0:T(8,128)S(1)}, u32[]{:S(2)}, u32[]{:S(2)}) collective-permute-start(f32[2,128,256]{2,1,0:T(8,128)S(1)} %pad_maximum_fusion.4), channel_id=1, source_target_pairs={{0,16},{4,20},{8,24},{12,28},{16,0},{20,4},{24,8},{28,12},{1,17},{... | collective-permute-start | bytes 786440 | tf_op jit(solution)/shard_map/ppermute | solution.py:246
  369.9 27.4 %collective-permute-start.6 = (f32[2,128,256]{2,1,0:T(8,128)S(1)}, f32[2,128,256]{2,1,0:T(8,128)S(1)}, u32[]{:S(2)}, u32[]{:S(2)}) collective-permute-start(f32[2,128,256]{2,1,0:T(8,128)S(1)} %pad_maximum_fusion.4), channel_id=1, source_target_pairs={{0,24},{4,28},{8,0},{12,4},{16,8},{20,12},{24,16},{28,20},{1,25},{... | collective-permute-start | bytes 786440 | tf_op jit(solution)/shard_map/ppermute | solution.py:246
  373.6 23.7 %collective-permute-start.4 = (f32[2,128,256]{2,1,0:T(8,128)S(1)}, f32[2,128,256]{2,1,0:T(8,128)S(1)}, u32[]{:S(2)}, u32[]{:S(2)}) collective-permute-start(f32[2,128,256]{2,1,0:T(8,128)S(1)} %pad_maximum_fusion.4), channel_id=1, source_target_pairs={{0,8},{4,12},{8,16},{12,20},{16,24},{20,28},{24,0},{28,4},{1,9},{5... | collective-permute-start | bytes 786440 | tf_op jit(solution)/shard_map/ppermute | solution.py:246
  386.9 76.1 %collective-permute-start.14 = (f32[4,128,256]{2,1,0:T(8,128)}, f32[4,128,256]{2,1,0:T(8,128)}, u32[]{:S(2)}, u32[]{:S(2)}) collective-permute-start(f32[4,128,256]{2,1,0:T(8,128)} %get-tuple-element.100), channel_id=1, source_target_pairs={{0,4},{4,0},{8,12},{12,8},{16,20},{20,16},{24,28},{28,24},{1,5},{5... | collective-permute-start | bytes 1572872 | tf_op jit(solution)/shard_map/ppermute | solution.py:250
  398.9 6.6 %copy-start.13 = (f32[8,128,2,128]{1,3,2,0:T(8,128)S(1)}, f32[8,128,2,128]{1,3,2,0:T(8,128)}, u32[]{:S(2)}) copy-start(f32[8,128,2,128]{1,3,2,0:T(8,128)} %copy-done.12) | copy-start | bytes 3145732
  413.5 48.3 %collective-permute-start.19 = (f32[512]{0:T(512)}, f32[512]{0:T(512)}, u32[]{:S(2)}, u32[]{:S(2)}) collective-permute-start(f32[512]{0:T(512)} %pad_select_fusion), channel_id=1, source_target_pairs={{0,4},{4,0},{8,12},{12,8},{16,20},{20,16},{24,28},{28,24},{1,5},{5... | collective-permute-start | bytes 6152 | tf_op jit(solution)/shard_map/ppermute | solution.py:250
  418.1 6.0 %copy-start.82 = (f32[8]{0:T(128)S(1)}, f32[8]{0:T(128)}, u32[]{:S(2)}) copy-start(f32[8]{0:T(128)} %copy-done.81) | copy-start | bytes 100
  424.2 8.5 %copy-start.16 = (f32[1024,1024]{1,0:T(8,128)S(1)}, f32[1024,1024]{1,0:T(8,128)}, u32[]{:S(2)}) copy-start(f32[1024,1024]{1,0:T(8,128)} %get-tuple-element.21) | copy-start | bytes 12582916
  424.2 9.2 %slice-start.6 = ((s8[8388608]{0:T(1024)(128)(4,1)}), s8[4194304]{0:T(1024)(128)(4,1)S(1)}, s32[]{:S(2)}) async-start(s8[8388608]{0:T(1024)(128)(4,1)} %bitcast.317), calls=%async_computation.6 | async-start | bytes 8388608
  449.3 12.5 %copy-start.78 = (f32[256]{0:T(256)S(1)}, f32[256]{0:T(256)}, u32[]{:S(2)}) copy-start(f32[256]{0:T(256)} %get-tuple-element.62) | copy-start | bytes 3076
  454.7 8.4 %copy-start.45 = (f32[4,1,128,256]{3,2,0,1:T(8,128)S(1)}, f32[4,1,128,256]{3,2,0,1:T(8,128)}, u32[]{:S(2)}) copy-start(f32[4,1,128,256]{3,2,0,1:T(8,128)} %get-tuple-element.99) | copy-start | bytes 1572868
  455.9 14.9 %collective-permute-start.7 = (f32[4,128,256]{2,1,0:T(8,128)S(1)}, f32[4,128,256]{2,1,0:T(8,128)S(1)}, u32[]{:S(2)}, u32[]{:S(2)}) collective-permute-start(f32[4,128,256]{2,1,0:T(8,128)S(1)} %pad_maximum_fusion.2), channel_id=1, source_target_pairs={{0,4},{4,0},{8,12},{12,8},{16,20},{20,16},{24,28},{28,24},{1,5},{5... | collective-permute-start | bytes 1572872 | tf_op jit(solution)/shard_map/ppermute | solution.py:250
  459.0 11.9 %copy-start.33 = (f32[2048,512]{1,0:T(8,128)S(1)}, f32[2048,512]{1,0:T(8,128)}, u32[]{:S(2)}) copy-start(f32[2048,512]{1,0:T(8,128)} %refs_0_.2) | copy-start | bytes 12582916
  459.0 33.0 %collective-permute-start.10 = (f32[4,256,256]{2,1,0:T(8,128)S(1)}, f32[4,256,256]{2,1,0:T(8,128)S(1)}, u32[]{:S(2)}, u32[]{:S(2)}) collective-permute-start(f32[4,256,256]{2,1,0:T(8,128)S(1)} %pad_maximum_fusion.1), channel_id=1, source_target_pairs={{0,4},{4,0},{8,12},{12,8},{16,20},{20,16},{24,28},{28,24},{1,5},{5... | collective-permute-start | bytes 3145736 | tf_op jit(solution)/shard_map/ppermute | solution.py:250
  460.7 7.4 %collective-permute-start.2 = (f32[32,2048]{1,0:T(8,128)S(1)}, f32[32,2048]{1,0:T(8,128)S(1)}, u32[]{:S(2)}, u32[]{:S(2)}) collective-permute-start(f32[32,2048]{1,0:T(8,128)S(1)} %dynamic-slice_bitcast_fusion.3), channel_id=1, source_target_pairs={{0,2},{1,3},{2,0},{3,1},{4,6},{5,7},{6,4},{7,5},{8,10},{9,11},{10,... | collective-permute-start | bytes 786440 | tf_op jit(solution)/shard_map/ppermute | solution.py:258
  464.6 8.5 %copy-start.34 = (f32[2048,512]{1,0:T(8,128)S(1)}, f32[2048,512]{1,0:T(8,128)}, u32[]{:S(2)}) copy-start(f32[2048,512]{1,0:T(8,128)} %refs_1_.1) | copy-start | bytes 12582916
  464.6 40.1 %collective-permute-start.15 = (f32[1024,256]{1,0:T(8,128)S(1)}, f32[1024,256]{1,0:T(8,128)S(1)}, u32[]{:S(2)}, u32[]{:S(2)}) collective-permute-start(f32[1024,256]{1,0:T(8,128)S(1)} %bitcast.339), channel_id=1, source_target_pairs={{0,1},{1,0},{2,3},{3,2},{4,5},{5,4},{6,7},{7,6},{8,9},{9,8},{10,11... | collective-permute-start | bytes 3145736 | tf_op jit(solution)/shard_map/ppermute | solution.py:254
  477.9 14.1 %copy-start.51 = (f32[256,256]{1,0:T(8,128)S(1)}, f32[256,256]{1,0:T(8,128)}, u32[]{:S(2)}) copy-start(f32[256,256]{1,0:T(8,128)} %copy.216) | copy-start | bytes 786436
  477.9 14.1 %copy-start.52 = (f32[256,256]{1,0:T(8,128)S(1)}, f32[256,256]{1,0:T(8,128)}, u32[]{:S(2)}) copy-start(f32[256,256]{1,0:T(8,128)} %copy.215) | copy-start | bytes 786436
  477.9 14.1 %copy-start.53 = (f32[256,256]{1,0:T(8,128)S(1)}, f32[256,256]{1,0:T(8,128)}, u32[]{:S(2)}) copy-start(f32[256,256]{1,0:T(8,128)} %copy.214) | copy-start | bytes 786436
  480.2 13.8 %collective-permute-start.8 = (f32[2,32,2048]{2,1,0:T(8,128)S(1)}, f32[2,32,2048]{2,1,0:T(8,128)S(1)}, u32[]{:S(2)}, u32[]{:S(2)}) collective-permute-start(f32[2,32,2048]{2,1,0:T(8,128)S(1)} %dynamic-slice_bitcast_fusion), channel_id=1, source_target_pairs={{0,1},{1,0},{2,3},{3,2},{4,5},{5,4},{6,7},{7,6},{8,9},{9,8},{10,11... | collective-permute-start | bytes 1572872 | tf_op jit(solution)/shard_map/ppermute | solution.py:254
  492.4 7.9 %copy-start.58 = (f32[2048]{0:T(1024)S(1)}, f32[2048]{0:T(1024)}, u32[]{:S(2)}) copy-start(f32[2048]{0:T(1024)} %param.27) | copy-start | bytes 24580
  492.4 12.1 %copy-start.28 = (f32[128,2048]{1,0:T(8,128)S(1)}, f32[128,2048]{1,0:T(8,128)}, u32[]{:S(2)}) copy-start(f32[128,2048]{1,0:T(8,128)} %array_ref.2) | copy-start | bytes 3145732
  492.4 12.3 %copy-start.47 = (f32[1024,256]{1,0:T(8,128)S(1)}, f32[1024,256]{1,0:T(8,128)}, u32[]{:S(2)}) copy-start(f32[1024,256]{1,0:T(8,128)} %copy-done.46) | copy-start | bytes 3145732
  494.0 1.2 collective-permute-start.17
  495.2 3.7 collective-permute-start.18
  496.3 8.1 %collective-permute-start.9 = (f32[32,2048]{1,0:T(8,128)S(1)}, f32[32,2048]{1,0:T(8,128)S(1)}, u32[]{:S(2)}, u32[]{:S(2)}) collective-permute-start(f32[32,2048]{1,0:T(8,128)S(1)} %dynamic-slice_bitcast_fusion.2), channel_id=1, source_target_pairs={{0,2},{1,3},{2,0},{3,1},{4,6},{5,7},{6,4},{7,5},{8,10},{9,11},{10,... | collective-permute-start | bytes 786440 | tf_op jit(solution)/shard_map/ppermute | solution.py:258
  504.6 9.3 %copy-start.32 = (f32[256,1408]{1,0:T(8,128)S(1)}, f32[256,1408]{1,0:T(8,128)}, u32[]{:S(2)}) copy-start(f32[256,1408]{1,0:T(8,128)} %get-tuple-element.161) | copy-start | bytes 4325380
  505.8 9.3 %copy-start.30 = (f32[256,1408]{1,0:T(8,128)S(1)}, f32[256,1408]{1,0:T(8,128)}, u32[]{:S(2)}) copy-start(f32[256,1408]{1,0:T(8,128)} %get-tuple-element.162) | copy-start | bytes 4325380
  505.9 10.3 %copy-start.48 = (f32[1408,256]{1,0:T(8,128)S(1)}, f32[1408,256]{1,0:T(8,128)}, u32[]{:S(2)}) copy-start(f32[1408,256]{1,0:T(8,128)} %get-tuple-element.163) | copy-start | bytes 4325380
  505.9 7.3 %collective-permute-start.16 = (f32[256,256]{1,0:T(8,128)S(1)}, f32[256,256]{1,0:T(8,128)S(1)}, u32[]{:S(2)}, u32[]{:S(2)}) collective-permute-start(f32[256,256]{1,0:T(8,128)S(1)} %get-tuple-element.98), channel_id=1, source_target_pairs={{0,4},{4,0},{8,12},{12,8},{16,20},{20,16},{24,28},{28,24},{1,5},{5... | collective-permute-start | bytes 786440 | tf_op jit(solution)/shard_map/ppermute | solution.py:250
  (50 other events, 149.8 us)

commit v3 on v2

--- a/solution.py
+++ b/solution.py
@@ -346,63 +346,96 @@
 
     def scratch(block):
         return [
-            pltpu.SemaphoreType.DMA((26,)),
-            pltpu.SemaphoreType.DMA((26,)),
+            pltpu.SemaphoreType.DMA((78,)),
+            pltpu.SemaphoreType.DMA((78,)),
             pltpu.SemaphoreType.DMA((1,)),
         ]
 
     def __init__(self, block_ref, out_ref, send, recv, local):
         self.block, self.out, self.sems_here, self.local = block_ref, out_ref, (send, recv), local
         self.z, self.x, self.y, self.core = where_am_i()
-        self.rows, self.half = block_ref.shape[0], block_ref.shape[1] // 2
-
-    def device(self, z, x, core):
-        return (z * X + x, self.y * 2 + core)
-
-    def region(self, z, x, core):
+        self.rows = block_ref.shape[0]
+        self.tile = block_ref.shape[1] // 16
+
+    def device(self, z, x, y, core):
+        return (z * X + x, y * 2 + core)
+
+    def columns(self, part, y, core):
+        if part == 0:
+            return pl.ds(pl.multiple_of((6 + 2 * core) * self.tile, self.tile), 2 * self.tile)
+        return pl.ds(pl.multiple_of((10 * y + 3 * core) * self.tile, self.tile), 3 * self.tile)
+
+    def region(self, z, x, part, y, core):
         return self.out.at[
             pl.ds(pl.multiple_of((z * X + x) * self.rows, self.rows), self.rows),
-            pl.ds(pl.multiple_of(core * self.half, self.half), self.half),
+            self.columns(part, y, core),
         ]
 
-    def own(self):
-        return self.block.at[:, pl.ds(pl.multiple_of(self.core * self.half, self.half), self.half)]
-
-    def along(self, way, step, arriving):
+    def own(self, part):
+        return self.block.at[:, self.columns(part, self.y, self.core)]
+
+    def here(self, z, x, part):
+        return self.region(z, x, part, self.y, self.core)
+
+    def along(self, way, step, part, arriving):
         source = self.z - way * (step if arriving else step - 1)
-        src = self.own() if step == 1 and not arriving else self.region(source, self.x, self.core)
+        dst = self.here(source, self.x, part)
         return remote(
-            src,
-            self.region(source, self.x, self.core),
+            self.own(part) if step == 1 and not arriving else dst,
+            dst,
             self.sems_here,
-            (0 if way > 0 else 3) + step - 1,
-            self.device(self.z + way, self.x, self.core),
-        )
-
-    def across(self, way, step, arriving):
-        source = self.z - way * step
+            26 * part + (0 if way > 0 else 3) + step - 1,
+            self.device(self.z + way, self.x, self.y, self.core),
+        )
+
+    def across(self, way, step, part, arriving):
         x = 1 - self.x if arriving else self.x
-        src = self.own() if step == 0 and not arriving else self.region(source, x, self.core)
+        dst = self.here(self.z - way * step, x, part)
         return remote(
-            src,
-            self.region(source, x, self.core),
+            self.own(part) if step == 0 and not arriving else dst,
+            dst,
             self.sems_here,
-            6 + (0 if step == 0 else (0 if way > 0 else 3) + step),
-            self.device(self.z, 1 - self.x, self.core),
-        )
-
-    def inside(self, way, step, other_x, arriving):
-        source = self.z - way * step
+            26 * part + 6 + self.slot(way, step),
+            self.device(self.z, 1 - self.x, self.y, self.core),
+        )
+
+    def slot(self, way, step):
+        return 0 if step == 0 else (0 if way > 0 else 3) + step
+
+    def inside(self, way, step, other_x, part, arriving):
         x = 1 - self.x if other_x else self.x
         core = 1 - self.core if arriving else self.core
-        region = self.region(source, x, core)
-        index = (0 if way > 0 else 3) + step
+        region = self.region(self.z - way * step, x, part, self.y, core)
         return remote(
             region,
             region,
             self.sems_here,
-            13 + index if other_x else 13 + 6 + index,
-            self.device(self.z, self.x, 1 - self.core),
+            26 * part + 13 + self.slot(way, step) + (0 if other_x else 6),
+            self.device(self.z, self.x, self.y, 1 - self.core),
+        )
+
+    def over_y(self, way, step, other_x, arriving):
+        x = 1 - self.x if other_x else self.x
+        y = 1 - self.y if arriving else self.y
+        region = self.region(self.z - way * step, x, 1, y, self.core)
+        return remote(
+            region,
+            region,
+            self.sems_here,
+            52 + self.slot(way, step) + (0 if other_x else 6),
+            self.device(self.z, self.x, 1 - self.y, self.core),
+        )
+
+    def inside_y(self, way, step, other_x, arriving):
+        x = 1 - self.x if other_x else self.x
+        core = 1 - self.core if arriving else self.core
+        region = self.region(self.z - way * step, x, 1, 1 - self.y, core)
+        return remote(
+            region,
+            region,
+            self.sems_here,
+            65 + self.slot(way, step) + (0 if other_x else 6),
+            self.device(self.z, self.x, self.y, 1 - self.core),
         )
 
     def holds(self, way, step):
@@ -412,25 +445,36 @@
     def goes_on(self, way, step):
         return self.holds(way, step - 1) & (self.z + way >= 0) & (self.z + way < Z)
 
-    def when_holds(self, way, step, action):
+    def each(self, step, action):
         if step == 0:
-            action()
+            action(1)
         else:
-            pl.when(self.holds(way, step))(action)
-
-    def greet(self):
+            for way in (1, -1):
+                pl.when(self.holds(way, step))(lambda way=way: action(way))
+
+    def begin(self):
         barrier = pltpu.get_barrier_semaphore()
 
         def signal(device):
             pl.semaphore_signal(barrier, inc=1, device_id=device, device_id_type=MESH)
 
-        signal(self.device(self.z, 1 - self.x, self.core))
-        signal(self.device(self.z, self.x, 1 - self.core))
+        signal(self.device(self.z, 1 - self.x, self.y, self.core))
+        signal(self.device(self.z, self.x, 1 - self.y, self.core))
+        signal(self.device(self.z, self.x, self.y, 1 - self.core))
         for way in (1, -1):
             ahead = (self.z + way >= 0) & (self.z + way < Z)
-            pl.when(ahead)(lambda way=way: signal(self.device(self.z + way, self.x, self.core)))
+            pl.when(ahead)(
+                lambda way=way: signal(self.device(self.z + way, self.x, self.y, self.core))
+            )
         neighbours = jnp.where(self.z > 0, 1, 0) + jnp.where(self.z < Z - 1, 1, 0)
-        pl.semaphore_wait(barrier, 2 + neighbours)
+        pl.semaphore_wait(barrier, 3 + neighbours)
+        for part in (0, 1):
+            self.across(1, 0, part, False).start()
+            for way in (1, -1):
+                pl.when(self.goes_on(way, 1))(
+                    lambda way=way, part=part: self.along(way, 1, part, False).start()
+                )
+        self.own_copy().start()
 
     def own_copy(self):
         row = pl.multiple_of((self.z * X + self.x) * self.rows, self.rows)
@@ -438,68 +482,78 @@
             self.block, self.out.at[pl.ds(row, self.rows), :], self.local.at[0]
         )
 
-    def begin(self):
-        self.greet()
-        self.own_copy().start()
-        for way in (1, -1):
-            pl.when(self.goes_on(way, 1))(lambda way=way: self.along(way, 1, False).start())
-        self.across(1, 0, False).start()
-
     def arrive_along(self, step):
-        for way in (1, -1):
-
-            def action(way=way):
-                self.along(way, step, True).wait_recv()
+        def action(way):
+            for part in (1, 0):
+                self.along(way, step, part, True).wait_recv()
                 if step < Z - 1:
                     pl.when(self.goes_on(way, step + 1))(
-                        lambda: self.along(way, step + 1, False).start()
+                        lambda: self.along(way, step + 1, part, False).start()
                     )
-                self.across(way, step, False).start()
-                self.inside(way, step, False, False).start()
-
-            self.when_holds(way, step, action)
+                self.across(way, step, part, False).start()
+                if part == 1:
+                    self.over_y(way, step, False, False).start()
+                self.inside(way, step, False, part, False).start()
+
+        self.each(step, action)
 
     def arrive_across(self, step):
-        for way in (1, -1) if step else (1,):
-
-            def action(way=way):
-                self.across(way, step, True).wait_recv()
-                self.inside(way, step, True, False).start()
-
-            self.when_holds(way, step, action)
+        def action(way):
+            for part in (1, 0):
+                self.across(way, step, part, True).wait_recv()
+                if part == 1:
+                    self.over_y(way, step, True, False).start()
+                self.inside(way, step, True, part, False).start()
+
+        self.each(step, action)
+
+    def arrive_y(self, step, other_x):
+        def action(way):
+            self.over_y(way, step, other_x, True).wait_recv()
+            self.inside_y(way, step, other_x, False).start()
+
+        self.each(step, action)
 
     def finish(self):
         self.own_copy().wait()
         for way in (1, -1):
             for step in range(1, Z):
-                pl.when(self.goes_on(way, step))(
-                    lambda way=way, step=step: self.along(way, step, False).wait_send()
-                )
+                for part in (0, 1):
+                    pl.when(self.goes_on(way, step))(
+                        lambda way=way, step=step, part=part: self.along(
+                            way, step, part, False
+                        ).wait_send()
+                    )
         for step in range(Z):
-            for way in (1, -1) if step else (1,):
-
-                def action(way=way, step=step):
-                    self.across(way, step, False).wait_send()
-                    self.inside(way, step, True, False).wait_send()
-                    self.inside(way, step, True, True).wait_recv()
-                    if step:
-                        self.inside(way, step, False, False).wait_send()
-                        self.inside(way, step, False, True).wait_recv()
-
-                self.when_holds(way, step, action)
+
+            def action(way, step=step):
+                for other_x in (False, True) if step else (True,):
+                    for part in (0, 1):
+                        self.inside(way, step, other_x, part, False).wait_send()
+                        self.inside(way, step, other_x, part, True).wait_recv()
+                    self.over_y(way, step, other_x, False).wait_send()
+                    self.inside_y(way, step, other_x, False).wait_send()
+                    self.inside_y(way, step, other_x, True).wait_recv()
+                for part in (0, 1):
+                    self.across(way, step, part, False).wait_send()
+
+            self.each(step, action)
 
     def events(self):
         def round_of(step):
             def event():
-                self.arrive_along(step)
-                self.arrive_across(step - 1)
+                if step < Z:
+                    self.arrive_along(step)
+                if step <= Z:
+                    self.arrive_across(step - 1)
+                if 1 <= step - 1 < Z:
+                    self.arrive_y(step - 1, False)
+                if 0 <= step - 2 < Z:
+                    self.arrive_y(step - 2, True)
 
             return event
 
-        return [round_of(step) for step in range(1, Z)] + [
-            lambda: self.arrive_across(Z - 1),
-            self.finish,
-        ]
+        return [round_of(step) for step in range(1, Z + 2)] + [self.finish]
 
 
 def move_only(kind, array, collective_id):
@@ -520,7 +574,7 @@
     )(array)
 
 
-def load_halves(src_ref, high_ref, low_ref, stage_ref, sem):
+def load_halves(src_ref, high_ref, low_ref, stage_ref, sem, change=None):
     rows = stage_ref.shape[1]
     count = src_ref.shape[0] // rows
 
@@ -534,6 +588,8 @@
         if index + 1 < count:
             fetch(index + 1).start()
         fetch(index).wait()
+        if change is not None:
+            change(index)
         high, low = halves(stage_ref[index % 2])
         high_ref[index * rows : (index + 1) * rows, :] = high
         low_ref[index * rows : (index + 1) * rows, :] = low
@@ -545,79 +601,192 @@
         pl.when(step == when)(event)
 
 
-def beside_product(kind, array, left, weights, by_rows, collective_id, steps):
+def kernel_params(collective_id):
+    return pltpu.CompilerParams(
+        collective_id=collective_id, has_side_effects=True, vmem_limit_bytes=VMEM_BYTES
+    )
+
+
+def halves_scratch(rows, inner):
+    return [
+        pltpu.VMEM((rows, inner), BF16),
+        pltpu.VMEM((rows, inner), BF16),
+        pltpu.VMEM((2, 128, inner), F32),
+        pltpu.SemaphoreType.DMA((2,)),
+    ]
+
+
+def project_beside(kind, array, tokens, gain, weights, collective_id, steps):
+    rows, inner = tokens.shape
+    count = len(weights)
+    wide = inner // Z
+
+    def kernel(array_ref, tokens_ref, gain_ref, *refs):
+        weight_refs, refs = refs[:count], refs[count:]
+        out_ref, product_ref, cols_ref, high_ref, low_ref, stage_ref, stage_sem, *refs = refs
+        weight_buf, weight_sem, *scratch = refs
+        move = kind(array_ref, out_ref, *scratch)
+        place = lax.axis_index("seq")
+        start = pl.multiple_of((place % X) * TILE, TILE)
+        first_col = pl.multiple_of((place // X) * wide, wide)
+        step = pl.program_id(0)
+
+        def fetch(index):
+            return pltpu.make_async_copy(
+                weight_refs[index].at[:, pl.ds(start, TILE)],
+                weight_buf.at[index % 2],
+                weight_sem.at[index % 2],
+            )
+
+        def normalize(index):
+            entries = stage_ref[index % 2]
+            stage_ref[index % 2] = entries * rms(entries) * gain_ref[...]
+            cols_ref[index * 128 : (index + 1) * 128, :] = stage_ref[
+                index % 2, :, pl.ds(first_col, wide)
+            ]
+
+        @pl.when(step == 0)
+        def _():
+            move.begin()
+            fetch(0).start()
+            load_halves(tokens_ref, high_ref, low_ref, stage_ref, stage_sem, normalize)
+
+        for index in range(count - 1):
+            pl.when(step == index)(fetch(index + 1).start)
+        for index in range(count):
+            pl.when(step == index)(fetch(index).wait)
+        product_ref[...] = three_pass(
+            (high_ref[...], low_ref[...]), halves(weight_buf[lax.rem(step, 2)]), 1, 0
+        )
+        at_steps(move.events(), steps)
+
+    return pl.pallas_call(
+        kernel,
+        grid=(count,),
+        out_shape=[
+            jax.ShapeDtypeStruct(kind.shape(array), F32),
+            jax.ShapeDtypeStruct((rows, count * TILE), F32),
+            jax.ShapeDtypeStruct((rows, wide), F32),
+        ],
+        in_specs=[kind.spec, ANY, pl.BlockSpec(memory_space=pltpu.VMEM)] + [ANY] * count,
+        out_specs=[
+            kind.spec,
+            pl.BlockSpec((rows, TILE), lambda tile: (0, tile)),
+            pl.BlockSpec(memory_space=pltpu.VMEM),
+        ],
+        scratch_shapes=[
+            *halves_scratch(rows, inner),
+            pltpu.VMEM((2, inner, TILE), F32),
+            pltpu.SemaphoreType.DMA((2,)),
+            *kind.scratch(array),
+        ],
+        compiler_params=kernel_params(collective_id),
+        cost_estimate=pl.CostEstimate(
+            flops=6 * rows * inner * count * TILE, bytes_accessed=48 << 20, transcendentals=0
+        ),
+    )(array, tokens, gain[None], *weights)
+
+
+def transposed_beside(kind, array, left, weight, collective_id, steps):
     rows, inner = left.shape
-    count = len(weights)
-    if count > 1:
-        tiles, columns = count, count * TILE
-    else:
-        columns = weights[0].shape[0 if by_rows else 1]
-        tiles = pl.cdiv(columns, TILE)
-
-    def kernel(array_ref, left_ref, *refs):
-        weight_refs, refs = refs[:count], refs[count:]
-        out_ref, product_ref, high_ref, low_ref, stage_ref, stage_sem, weight_buf, weight_sem, *scratch = refs
+    columns = weight.shape[0]
+
+    def kernel(array_ref, left_ref, weight_ref, out_ref, product_ref, *refs):
+        high_ref, low_ref, stage_ref, stage_sem, *scratch = refs
+        move = kind(array_ref, out_ref, *scratch)
+
+        @pl.when(pl.program_id(0) == 0)
+        def _():
+            move.begin()
+            load_halves(left_ref, high_ref, low_ref, stage_ref, stage_sem)
+
+        product_ref[...] = three_pass(
+            (high_ref[...], low_ref[...]), halves(weight_ref[...]), 1, 1
+        )
+        at_steps(move.events(), steps)
+
+    return pl.pallas_call(
+        kernel,
+        grid=(pl.cdiv(columns, TILE),),
+        out_shape=[
+            jax.ShapeDtypeStruct(kind.shape(array), F32),
+            jax.ShapeDtypeStruct((rows, columns), F32),
+        ],
+        in_specs=[kind.spec, ANY, pl.BlockSpec((TILE, inner), lambda tile: (tile, 0))],
+        out_specs=[kind.spec, pl.BlockSpec((rows, TILE), lambda tile: (0, tile))],
+        scratch_shapes=[*halves_scratch(rows, inner), *kind.scratch(array)],
+        compiler_params=kernel_params(collective_id),
+        cost_estimate=pl.CostEstimate(
+            flops=6 * rows * inner * columns, bytes_accessed=48 << 20, transcendentals=0
+        ),
+    )(array, left, weight)
+
+
+def few_rows(left, right, contract_right):
+    (left_high, left_low), (right_high, right_low) = left, right
+    rows = left_high.shape[0]
+    both = product(jnp.concatenate([left_high, left_low]), right_high, 1, contract_right)
+    return both[:rows] + (product(left_high, right_low, 1, contract_right) + both[rows:])
+
+
+def feed_forward_beside(kind, array, normed_two, grad_hidden, w_gate, w_up, w_down, collective_id, steps):
+    rows, inner = normed_two.shape
+    columns = w_gate.shape[1]
+    tiles = pl.cdiv(columns, TILE)
+
+    def kernel(array_ref, normed_ref, e_ref, gate_ref, up_ref, down_ref, out_ref, ffn_ref, grad_ref, *scratch):
         move = kind(array_ref, out_ref, *scratch)
         step = pl.program_id(0)
-        pl.when(step == 0)(move.begin)
-        if count > 1:
-            start = pl.multiple_of((lax.axis_index("seq") % X) * TILE, TILE)
-
-            def fetch(index):
-                return pltpu.make_async_copy(
-                    weight_refs[index].at[:, pl.ds(start, TILE)],
-                    weight_buf.at[index % 2],
-                    weight_sem.at[index % 2],
-                )
-
-            pl.when(step == 0)(fetch(0).start)
-            for index in range(count - 1):
-                pl.when(step == index)(fetch(index + 1).start)
-        pl.when(step == 0)(
-            lambda: load_halves(left_ref, high_ref, low_ref, stage_ref, stage_sem)
-        )
-        if count > 1:
-            for index in range(count):
-                pl.when(step == index)(fetch(index).wait)
-            weight = weight_buf[lax.rem(step, 2)]
-        else:
-            weight = weight_refs[0][...]
-        product_ref[...] = three_pass(
-            (high_ref[...], low_ref[...]), halves(weight), 1, 1 if by_rows else 0
-        )
+
+        @pl.when(step == 0)
+        def _():
+            move.begin()
+            ffn_ref[...] = jnp.zeros_like(ffn_ref)
+            grad_ref[...] = jnp.zeros_like(grad_ref)
+
+        def inside(shape, axis):
+            return step * TILE + lax.broadcasted_iota(jnp.int32, shape, axis) < columns
+
+        gate_weight = halves(jnp.where(inside((inner, TILE), 1), gate_ref[...], 0.0))
+        up_weight = halves(jnp.where(inside((inner, TILE), 1), up_ref[...], 0.0))
+        down_weight = halves(jnp.where(inside((TILE, inner), 0), down_ref[...], 0.0))
+        normed = halves(normed_ref[...])
+        a = few_rows(normed, gate_weight, 0)
+        b = few_rows(normed, up_weight, 0)
+        e = jnp.where(inside((rows, TILE), 1), e_ref[...], 0.0)
+        gate = jax.nn.sigmoid(a)
+        silu_a = a * gate
+        ffn_ref[...] += few_rows(halves(silu_a * b), down_weight, 0)
+        grad_ref[...] += few_rows(
+            halves(e * b * (gate * (1.0 + a * (1.0 - gate)))), gate_weight, 1
+        ) + few_rows(halves(e * silu_a), up_weight, 1)
         at_steps(move.events(), steps)
 
-    if count > 1:
-        weight_spec = ANY
-    elif by_rows:
-        weight_spec = pl.BlockSpec((TILE, inner), lambda tile: (tile, 0))
-    else:
-        weight_spec = pl.BlockSpec((inner, TILE), lambda tile: (0, tile))
+    whole = pl.BlockSpec(memory_space=pltpu.VMEM)
+    by_column = pl.BlockSpec((inner, TILE), lambda tile: (0, tile))
     return pl.pallas_call(
         kernel,
         grid=(tiles,),
         out_shape=[
             jax.ShapeDtypeStruct(kind.shape(array), F32),
-            jax.ShapeDtypeStruct((rows, columns), F32),
+            jax.ShapeDtypeStruct((rows, inner), F32),
+            jax.ShapeDtypeStruct((rows, inner), F32),
         ],
-        in_specs=[kind.spec, ANY] + [weight_spec] * count,
-        out_specs=[kind.spec, pl.BlockSpec((rows, TILE), lambda tile: (0, tile))],
-        scratch_shapes=[
-            pltpu.VMEM((rows, inner), BF16),
-            pltpu.VMEM((rows, inner), BF16),
-            pltpu.VMEM((2, 128, inner), F32),
-            pltpu.SemaphoreType.DMA((2,)),
-            pltpu.VMEM((2, inner, TILE) if count > 1 else (8, 128), F32),
-            pltpu.SemaphoreType.DMA((2,)),
-            *kind.scratch(array),
+        in_specs=[
+            kind.spec,
+            whole,
+            pl.BlockSpec((rows, TILE), lambda tile: (0, tile)),
+            by_column,
+            by_column,
+            pl.BlockSpec((TILE, inner), lambda tile: (tile, 0)),
         ],
-        compiler_params=pltpu.CompilerParams(
-            collective_id=collective_id, has_side_effects=True, vmem_limit_bytes=VMEM_BYTES
+        out_specs=[kind.spec, whole, whole],
+        scratch_shapes=kind.scratch(array),
+        compiler_params=kernel_params(collective_id),
+        cost_estimate=pl.CostEstimate(
+            flops=30 * rows * inner * columns, bytes_accessed=40 << 20, transcendentals=0
         ),
-        cost_estimate=pl.CostEstimate(
-            flops=6 * rows * inner * columns, bytes_accessed=48 << 20, transcendentals=0
-        ),
-    )(array, left, *weights)
+    )(array, normed_two, grad_hidden, w_gate, w_up, w_down)
 
 
 class Sum:
@@ -747,16 +916,8 @@
         out_specs=[
             whole, grad_spec, grad_spec, pl.BlockSpec((TILE, narrow), lambda tile: (tile, 0)),
         ],
-        scratch_shapes=[
-            pltpu.VMEM((rows, inner), BF16),
-            pltpu.VMEM((rows, inner), BF16),
-            pltpu.VMEM((2, 128, inner), F32),
-            pltpu.SemaphoreType.DMA((2,)),
-        ]
-        + Sum.scratch(part),
-        compiler_params=pltpu.CompilerParams(
-            collective_id=collective_id, has_side_effects=True, vmem_limit_bytes=VMEM_BYTES
-        ),
+        scratch_shapes=[*halves_scratch(rows, inner), *Sum.scratch(part)],
+        compiler_params=kernel_params(collective_id),
         cost_estimate=pl.CostEstimate(
             flops=15 * rows * inner * columns, bytes_accessed=48 << 20, transcendentals=0
         ),
@@ -797,14 +958,14 @@
 
     token_count = rows * Z * X
     positions = jnp.arange(token_count, dtype=jnp.int32)
-    offsets = jnp.cumsum(lengths) - lengths
+    order = jnp.arange(lengths.shape[0])
+    offsets = jnp.sum(jnp.where(order[:, None] < order[None, :], lengths[:, None], 0), 0)
     segment = jnp.sum((positions[:, None] >= offsets[None, :]).astype(jnp.int32), 1) - 1
 
     all_tokens = move_only(Gather, tokens_in, 1)
-    normed_one = all_tokens * rms(all_tokens) * first_gain
     in_weights = (query_weight, forget_weight, input_weight, gate_weight)
-    all_cotangent, projected = beside_product(
-        Gather, cotangent, normed_one, in_weights, False, 2, (1, 2, 3, 3, 3)
+    all_cotangent, projected, normed_one_cols = project_beside(
+        Gather, cotangent, all_tokens, first_gain, in_weights, 2, (1, 2, 3, 3, 3, 3)
     )
     mixer, mixer_back = jax.vjp(
         partial(mixer_all, lower_bound=cut(lower_bound, x, width, 0), segment=segment),
@@ -815,22 +976,23 @@
     mixer_part = dot(own(mixer, place), cut(out_weight, x, width, 0), 1, 0) + dot(
         mixer_other, cut(out_weight, 1 - x, width, 0), 1, 0
     )
-    mixer_sum, grad_hidden_all = beside_product(
-        Sum, mixer_part, all_cotangent, (swiglu_down,), True, 3, (0, 4, 5)
+    mixer_sum, grad_hidden_all = transposed_beside(
+        Sum, mixer_part, all_cotangent, swiglu_down, 3, (0, 3, 4)
     )
     residual = tokens_in + mixer_sum
     scale_two = rms(residual)
     normed_two = residual * scale_two * second_gain
-    all_normed_two = move_only(Gather, normed_two, 4)
-
-    a = dot(normed_two, swiglu_gate, 1, 0)
-    b = dot(normed_two, swiglu_up, 1, 0)
-    silu_a = jax.nn.silu(a)
-    e = own(grad_hidden_all, place)
-    normed_two_part = dot(e * b * silu_grad(a), swiglu_gate, 1, 1) + dot(
-        e * silu_a, swiglu_up, 1, 1
-    )
-    ffn_part = dot(silu_a * b, swiglu_down, 1, 0)
+    all_normed_two, ffn_part, normed_two_part = feed_forward_beside(
+        Gather,
+        normed_two,
+        normed_two,
+        own(grad_hidden_all, place),
+        swiglu_gate,
+        swiglu_up,
+        swiglu_down,
+        4,
+        (1, 2, 3, 4, 5, 5),
+    )
     grad_normed_two, grad_sgate, grad_sup, grad_sdown = hidden_and_sum(
         normed_two_part,
         all_normed_two,
@@ -896,7 +1058,6 @@
         - tokens_share * scale_one**3 * jnp.mean(pulled_one * tokens_share, -1, keepdims=True)
     )
 
-    normed_one_cols = cut(normed_one, z, wide, 1)
     blocks = [dot(normed_one_cols, part, 0, 0) for part in grad_rows]
     block_mine = jnp.stack([cut(block, x, narrow, 0) for block in blocks])
     block_other = x_swap(jnp.stack([cut(block, 1 - x, narrow, 0) for block in blocks]))

time: 524 us -> 462 us (0.88)
  matrix products: 85.2 us -> 44.6 us
  Pallas kernels: 259 us -> 247 us
  other arithmetic: 48.3 us -> 36.6 us
    pallas_call x2 -> x1, Pallas kernels: 105 us -> 43.9 us  [move_only(): pl.pallas_call(kernel, out_shape=jax.ShapeDtypeStruct(kind.shape(array),...]
    pallas_call x2 -> x3, Pallas kernels: 88.5 us -> 138 us  [the longest x1 52.8 us: project_beside(): pl.pallas_call(kernel, grid=(count,), out_shape=[jax.ShapeDtypeStruct(kin...]
    dot_general x17 -> x12, matrix products: 63.8 us -> 22 us  [dot(): lax.dot_general(left, right, (((contract_left,), (contract_right,)), ((),...]
    dynamic_slice x21 -> x22, local copies, waits for them, and re-layouts: 24.9 us -> 20.8 us  [cut(): return lax.dynamic_slice_in_dim(array, place * size, size, axis)]
    unnamed x193 -> x179, local copies, waits for them, and re-layouts: 8.91 us -> 12.1 us
  transfers between devices with their start and end apart: 20 -> 20, of which waited for: 10 -> 11; matrix products, arithmetic and copies ran while one was open for 17% -> 18% of each run, Pallas kernels for 0% -> 0%
where the time goes in v3:
time: 462 us; the launch traced here: 454 us
  Pallas kernels  247 us (53%)
  local copies, waits for them, and re-layouts  53.5 us (12%)
  waiting for transfers between devices  49.7 us (11%)
  matrix products  44.6 us (10%)
  other arithmetic  36.6 us (8%)
  starting transfers between devices  19.7 us (4%)
    pallas_call x1, Pallas kernels, hidden_and_sum(): pl.pallas_call(kernel, grid=(tiles,), out_shape=[jax.ShapeDtypeStruct(par...  65.7 us
    pallas_call x1, Pallas kernels, project_beside(): pl.pallas_call(kernel, grid=(count,), out_shape=[jax.ShapeDtypeStruct(kin...  52.8 us
    pallas_call x1, Pallas kernels, feed_forward_beside(): pl.pallas_call(kernel, grid=(tiles,), out_shape=[jax.ShapeDtypeStruct(kin...  50.8 us
    pallas_call x1, Pallas kernels, move_only(): pl.pallas_call(kernel, out_shape=jax.ShapeDtypeStruct(kind.shape(array),...  43.9 us
    pallas_call x1, Pallas kernels, transposed_beside(): pl.pallas_call(kernel, grid=(pl.cdiv(columns, TILE),), out_shape=[jax.Sha...  34 us
    dot_general x12, matrix products, dot(): lax.dot_general(left, right, (((contract_left,), (contract_right,)), ((),...  22 us
    dynamic_slice x22, local copies, waits for them, and re-layouts, cut(): return lax.dynamic_slice_in_dim(array, place * size, size, axis)  20.8 us
    ppermute x6, waiting for transfers between devices, z_shift(): return lax.ppermute(array, 'seq', steps)  20.4 us
  transfers between devices with their start and end apart: 20, of which 11 were waited for; matrix products, arithmetic and copies ran while one was open for 18% of the time, Pallas kernels for 0%

profile of v3, /device:TPU:8, one launch (start us, length us, event | category | flops | bytes accessed | tf_op | source)
XLA Modules:
  0.0 453.9 jit_solution(7545572795299239810)
XLA Ops:
  4.6 43.9 %shard_map.246.tokens_ref = f32[1024,2048]{1,0:T(8,128)} custom-call(f32[128,2048]{1,0:T(8,128)} %array_ref.2), custom_call_target="tpu_custom_call" | custom-call | bytes 16777216 | tf_op jit(solution)/shard_map/pallas_call | solution.py:566
  48.5 52.8 %shard_map.247 = (f32[1024,2048]{1,0:T(8,128)}, f32[1024,1024]{1,0:T(8,128)}, f32[1024,512]{1,0:T(8,128)}) custom-call(f32[128,2048]{1,0:T(8,128)} %array_ref.3, f32[1024,2048]{1,0:T(8,128)} %shard_map.246.tokens_ref, f32[1,2048]{1,0:T(1,128)} %bitcast.340, f32[2048,512]{1,0:T(8,128)} %refs_0_.1, f32[2048,512]{1,0:T(8,128)} %refs_1_.1, f32[2048,512]{1,0:T(8,128)} %refs_2_.1, ...), custom_call_target="tpu_custom_call" | custom-call | flops 12884901888 | bytes 50331648 | tf_op jit(solution)/shard_map/pallas_call | solution.py:663
  101.4 3.4 fusion.113
  105.3 2.1 reshape.291
  107.5 1.5 reshape.290
  108.9 2.3 copy_multiply_fusion
  111.5 1.3 fusion.45
  112.8 1.2 convolution_select_fusion.1
  115.9 1.4 multiply_reduce_fusion.4
  119.0 1.3 copy.190
  120.3 2.3 mul.645
  122.6 1.9 multiply_multiply_fusion.3
  125.6 1.5 collective-permute-start
  127.9 2.4 constant_dynamic-slice_fusion.18.cot_cols_ref
  130.3 2.4 fusion.7
  132.7 2.7 convolution_add_fusion.3.array_ref
  135.4 34.0 %shard_map.248 = (f32[128,2048]{1,0:T(8,128)}, f32[1024,1408]{1,0:T(8,128)}) custom-call(f32[128,2048]{1,0:T(8,128)} %convolution_add_fusion.3.array_ref, f32[1024,2048]{1,0:T(8,128)} %get-tuple-element.26.left_ref, f32[1408,2048]{1,0:T(8,128)} %down_ref.1), custom_call_target="tpu_custom_call" | custom-call | flops 17716740096 | bytes 50331648 | tf_op jit(solution)/shard_map/pallas_call | solution.py:708
  169.5 1.7 multiply_reduce_fusion.3
  171.2 2.0 constant_dynamic-slice_fusion.20.e_ref
  173.3 1.1 multiply_multiply_fusion.1.array_ref.normed_ref
  174.4 50.8 %shard_map.249 = (f32[1024,2048]{1,0:T(8,128)}, f32[128,2048]{1,0:T(8,128)}, f32[128,2048]{1,0:T(8,128)}) custom-call(f32[128,2048]{1,0:T(8,128)} %multiply_multiply_fusion.1.array_ref.normed_ref, f32[128,2048]{1,0:T(8,128)} %multiply_multiply_fusion.1.array_ref.normed_ref, f32[128,1408]{1,0:T(8,128)} %constant_dynamic-slice_fusion.20.e_ref, ...), custom_call_target="tpu_custom_call" | custom-call | flops 11072962560 | bytes 41943040 | tf_op jit(solution)/shard_map/pallas_call | solution.py:767
  225.2 2.3 constant_dynamic-slice_fusion.19.normed_cols_ref
  227.5 65.7 %shard_map.250 = (f32[128,2048]{1,0:T(8,128)}, f32[256,1408]{1,0:T(8,128)}, f32[256,1408]{1,0:T(8,128)}, f32[1408,256]{1,0:T(8,128)}) custom-call(f32[128,2048]{1,0:T(8,128)} %get-tuple-element.30.part_ref, f32[1024,2048]{1,0:T(8,128)} %get-tuple-element.31.normed_ref, f32[1024,1408]{1,0:T(8,128)} %get-tuple-element.28.e_ref, f32[2048,1408]{1,0:T(8,128)} %gate_ref.3, ...), custom_call_target="tpu_custom_call" | custom-call | flops 44291850240 | bytes 50331648 | tf_op jit(solution)/shard_map/pallas_call | solution.py:904
  293.2 1.6 multiply_reduce_fusion.2
  295.4 1.8 copy-done.9
  297.2 2.3 fusion.115
  301.2 1.4 collective-permute-start.13
  303.6 2.9 add_reduce_fusion
  306.6 2.9 collective-permute-start.5
  309.4 11.8 %collective-permute-done.11 = f32[128,256]{1,0:T(8,128)S(1)} collective-permute-done((f32[128,256]{1,0:T(8,128)S(1)}, f32[128,256]{1,0:T(8,128)S(1)}, u32[]{:S(2)}, u32[]{:S(2)}) %collective-permute-start.11) | collective-permute-done | bytes 131104 | tf_op jit(solution)/shard_map/ppermute | solution.py:246
  321.2 3.0 collective-permute-start.4
  325.5 1.6 collective-permute-start.14
  327.1 2.9 collective-permute-done.5
  330.0 5.6 %collective-permute-done.6 = f32[2,128,256]{2,1,0:T(8,128)S(1)} collective-permute-done((f32[2,128,256]{2,1,0:T(8,128)S(1)}, f32[2,128,256]{2,1,0:T(8,128)S(1)}, u32[]{:S(2)}, u32[]{:S(2)}) %collective-permute-start.6) | collective-permute-done | bytes 262176 | tf_op jit(solution)/shard_map/ppermute | solution.py:246
  337.4 3.9 multiply_reduce_fusion
  341.3 2.7 reshape.295
  344.0 2.2 copy.196
  346.3 1.8 multiply_reduce_fusion.1
  349.4 1.1 convolution_multiply_fusion.1
  354.0 1.3 fusion.57
  355.9 1.5 collective-permute-start.19
  357.4 2.0 convolution_bitcast_fusion.1
  359.7 2.1 exponential_multiply_fusion
  361.8 1.8 copy.202
  363.6 1.7 fusion.9
  365.3 2.5 copy.212
  367.9 4.7 %fusion.12 = f32[8,128,2,128]{3,1,2,0:T(8,128)S(1)} fusion(f32[8,128,2,128]{3,1,2,0:T(8,128)} %get-tuple-element.144, f32[8,1,2,128]{3,1,2,0:T(1,128)S(1)} %bitcast.347, f32[8,128,2,128]{3,1,2,0:T(8,128)} %convolution_bitcast_fusion.1, f32[8,128,2,128]{3,1,2,0:T(8,128)} %copy-done.45, f32[8,128,2,128]{3,2,1,0:T(2,128)} %reshape.290, ...), kind=kOutput, calls=%fused_computation.26 | convolution fusion | flops 408698880 | bytes 7356416 | tf_op jit(solution)/shard_map/transpose(jvp(ts,cshk->cthk))/dot_general | solution.py:60
  383.3 1.8 copy.216
  386.1 1.8 copy.220
  392.5 1.6 collective-permute-start.10
  397.5 1.3 maximum_select_fusion.3
  399.0 3.2 collective-permute-done.2
  402.9 3.8 collective-permute-done.7
  406.8 2.2 fusion.60
  409.0 2.5 convolution_add_fusion.2
  411.5 2.2 convolution_add_fusion.1
  413.8 2.2 convolution_add_fusion
  416.1 11.3 %collective-permute-done.10 = f32[4,256,256]{2,1,0:T(8,128)S(1)} collective-permute-done((f32[4,256,256]{2,1,0:T(8,128)S(1)}, f32[4,256,256]{2,1,0:T(8,128)S(1)}, u32[]{:S(2)}, u32[]{:S(2)}) %collective-permute-start.10) | collective-permute-done | bytes 1048608 | tf_op jit(solution)/shard_map/ppermute | solution.py:250
  427.8 1.5 multiply_reduce_fusion.5
  432.8 1.5 collective-permute-done.18
  434.3 1.3 dynamic-slice_divide_fusion
  436.3 3.6 collective-permute-done.9
  441.9 1.8 multiply_subtract_fusion.1
  443.6 4.9 %collective-permute-done.16 = f32[256,256]{1,0:T(8,128)S(1)} collective-permute-done((f32[256,256]{1,0:T(8,128)S(1)}, f32[256,256]{1,0:T(8,128)S(1)}, u32[]{:S(2)}, u32[]{:S(2)}) %collective-permute-start.16) | collective-permute-done | bytes 262176 | tf_op jit(solution)/shard_map/ppermute | solution.py:250
  (299 shorter events, 53.5 us)
Async XLA Ops:
  3.3 98.1 %copy-start.83 = (f32[256]{0:T(256)}, f32[256]{0:T(256)S(1)}, u32[]{:S(2)}) copy-start(f32[256]{0:T(256)S(1)} %dynamic-slice_subtract_fusion) | copy-start | bytes 3076
  4.1 118.5 %copy-start.79 = (f32[256]{0:T(256)}, f32[256]{0:T(256)S(1)}, u32[]{:S(2)}) copy-start(f32[256]{0:T(256)S(1)} %dynamic_slice.162) | copy-start | bytes 3076
  4.2 107.2 %copy-start.74 = (f32[8,128]{1,0:T(8,128)}, f32[8,128]{1,0:T(8,128)S(1)}, u32[]{:S(2)}) copy-start(f32[8,128]{1,0:T(8,128)S(1)} %get-tuple-element.133) | copy-start | bytes 12292
  4.4 106.9 %copy-start.85 = (f32[8]{0:T(128)}, f32[8]{0:T(128)S(1)}, u32[]{:S(2)}) copy-start(f32[8]{0:T(128)S(1)} %slice_reduce_fusion.1) | copy-start | bytes 100
  105.3 8.7 %copy-start.4 = (f32[8,128,2,128]{3,2,1,0:T(2,128)}, f32[8,128,2,128]{3,2,1,0:T(2,128)S(1)}, u32[]{:S(2)}) copy-start(f32[8,128,2,128]{3,2,1,0:T(2,128)S(1)} %reshape.289) | copy-start | bytes 3145732
  111.4 4.2 copy-start.66
  111.4 4.2 copy-start.72
  111.4 4.3 copy-start.63
  111.4 4.4 copy-start.68
  111.4 4.4 copy-start.70
  111.4 4.4 copy-start.77
  112.7 3.1 copy-start.11
  117.3 5.3 %copy-start.6 = (f32[8,128,2,128]{1,3,2,0:T(8,128)}, f32[8,128,2,128]{1,3,2,0:T(8,128)S(1)}, u32[]{:S(2)}) copy-start(f32[8,128,2,128]{1,3,2,0:T(8,128)S(1)} %get-tuple-element.143) | copy-start | bytes 3145732
  117.3 5.3 %copy-start.60 = (f32[8,128,2]{1,2,0:T(2,128)}, f32[8,128,2]{1,2,0:T(2,128)S(1)}, u32[]{:S(2)}) copy-start(f32[8,128,2]{1,2,0:T(2,128)S(1)} %get-tuple-element.142) | copy-start | bytes 24580
  122.6 4.5 copy-start.12
  125.6 7.1 %collective-permute-start = (f32[128,256]{1,0:T(8,128)}, f32[128,256]{1,0:T(8,128)}, u32[]{:S(2)}, u32[]{:S(2)}) collective-permute-start(f32[128,256]{1,0:T(8,128)} %constant_dynamic-slice_fusion.21), channel_id=1, source_target_pairs={{0,4},{4,0},{8,12},{12,8},{16,20},{20,16},{24,28},{28,24},{1,5},{5... | collective-permute-start | bytes 393224 | tf_op jit(solution)/shard_map/ppermute | solution.py:250
  127.9 4.8 %copy-start.8 = (f32[512,2048]{1,0:T(8,128)S(1)}, f32[512,2048]{1,0:T(8,128)}, u32[]{:S(2)}) copy-start(f32[512,2048]{1,0:T(8,128)} %param.23) | copy-start | bytes 12582916
  169.4 3.8 copy-start.59
  297.2 27.2 %copy-start.22 = (f32[128,2048]{1,0:T(8,128)}, f32[128,2048]{1,0:T(8,128)S(1)}, u32[]{:S(2)}) copy-start(f32[128,2048]{1,0:T(8,128)S(1)} %multiply_subtract_fusion) | copy-start | bytes 3145732
  297.2 5.6 %copy-start.51 = (f32[128,2048]{1,0:T(8,128)S(1)}, f32[128,2048]{1,0:T(8,128)}, u32[]{:S(2)}) copy-start(f32[128,2048]{1,0:T(8,128)} %get-tuple-element.29) | copy-start | bytes 3145732
  297.2 6.4 %copy-start.26 = (f32[256,1408]{1,0:T(8,128)S(1)}, f32[256,1408]{1,0:T(8,128)}, u32[]{:S(2)}) copy-start(f32[256,1408]{1,0:T(8,128)} %get-tuple-element.169) | copy-start | bytes 4325380
  299.5 4.1 copy-start.24
  299.6 7.0 %collective-permute-start.3 = (f32[128,256]{1,0:T(8,128)S(1)}, f32[128,256]{1,0:T(8,128)S(1)}, u32[]{:S(2)}, u32[]{:S(2)}) collective-permute-start(f32[128,256]{1,0:T(8,128)S(1)} %get-tuple-element.122), channel_id=1, source_target_pairs={{0,4},{4,0},{8,12},{12,8},{16,20},{20,16},{24,28},{28,24},{1,5},{5... | collective-permute-start | bytes 393224 | tf_op jit(solution)/shard_map/ppermute | solution.py:250
  300.6 20.7 %collective-permute-start.11 = (f32[128,256]{1,0:T(8,128)S(1)}, f32[128,256]{1,0:T(8,128)S(1)}, u32[]{:S(2)}, u32[]{:S(2)}) collective-permute-start(f32[128,256]{1,0:T(8,128)S(1)} %get-tuple-element.88), channel_id=1, source_target_pairs={{0,8},{4,12},{8,16},{12,20},{16,24},{20,28},{24,0},{28,4},{1,9},{5... | collective-permute-start | bytes 393224 | tf_op jit(solution)/shard_map/ppermute | solution.py:246
  301.2 20.0 %collective-permute-start.13 = (f32[128,256]{1,0:T(8,128)S(1)}, f32[128,256]{1,0:T(8,128)S(1)}, u32[]{:S(2)}, u32[]{:S(2)}) collective-permute-start(f32[128,256]{1,0:T(8,128)S(1)} %get-tuple-element.89), channel_id=1, source_target_pairs={{0,24},{4,28},{8,0},{12,4},{16,8},{20,12},{24,16},{28,20},{1,25},{... | collective-permute-start | bytes 393224 | tf_op jit(solution)/shard_map/ppermute | solution.py:246
  302.6 21.7 %collective-permute-start.12 = (f32[128,256]{1,0:T(8,128)S(1)}, f32[128,256]{1,0:T(8,128)S(1)}, u32[]{:S(2)}, u32[]{:S(2)}) collective-permute-start(f32[128,256]{1,0:T(8,128)S(1)} %get-tuple-element.90), channel_id=1, source_target_pairs={{0,16},{4,20},{8,24},{12,28},{16,0},{20,4},{24,8},{28,12},{1,17},{... | collective-permute-start | bytes 393224 | tf_op jit(solution)/shard_map/ppermute | solution.py:246
  306.5 87.5 %collective-permute-start.1 = (f32[2,32,2048]{2,1,0:T(8,128)}, f32[2,32,2048]{2,1,0:T(8,128)}, u32[]{:S(2)}, u32[]{:S(2)}) collective-permute-start(f32[2,32,2048]{2,1,0:T(8,128)} %dynamic-slice_bitcast_fusion.1), channel_id=1, source_target_pairs={{0,1},{1,0},{2,3},{3,2},{4,5},{5,4},{6,7},{7,6},{8,9},{9,8},{10,11... | collective-permute-start | bytes 1572872 | tf_op jit(solution)/shard_map/ppermute | solution.py:254
  306.6 23.4 %collective-permute-start.5 = (f32[2,128,256]{2,1,0:T(8,128)S(1)}, f32[2,128,256]{2,1,0:T(8,128)S(1)}, u32[]{:S(2)}, u32[]{:S(2)}) collective-permute-start(f32[2,128,256]{2,1,0:T(8,128)S(1)} %pad_maximum_fusion.4), channel_id=1, source_target_pairs={{0,16},{4,20},{8,24},{12,28},{16,0},{20,4},{24,8},{28,12},{1,17},{... | collective-permute-start | bytes 786440 | tf_op jit(solution)/shard_map/ppermute | solution.py:246
  321.2 14.4 %collective-permute-start.6 = (f32[2,128,256]{2,1,0:T(8,128)S(1)}, f32[2,128,256]{2,1,0:T(8,128)S(1)}, u32[]{:S(2)}, u32[]{:S(2)}) collective-permute-start(f32[2,128,256]{2,1,0:T(8,128)S(1)} %pad_maximum_fusion.4), channel_id=1, source_target_pairs={{0,24},{4,28},{8,0},{12,4},{16,8},{20,12},{24,16},{28,20},{1,25},{... | collective-permute-start | bytes 786440 | tf_op jit(solution)/shard_map/ppermute | solution.py:246
  321.2 14.4 %collective-permute-start.4 = (f32[2,128,256]{2,1,0:T(8,128)S(1)}, f32[2,128,256]{2,1,0:T(8,128)S(1)}, u32[]{:S(2)}, u32[]{:S(2)}) collective-permute-start(f32[2,128,256]{2,1,0:T(8,128)S(1)} %pad_maximum_fusion.4), channel_id=1, source_target_pairs={{0,8},{4,12},{8,16},{12,20},{16,24},{20,28},{24,0},{28,4},{1,9},{5... | collective-permute-start | bytes 786440 | tf_op jit(solution)/shard_map/ppermute | solution.py:246
  325.5 72.0 %collective-permute-start.14 = (f32[4,128,256]{2,1,0:T(8,128)}, f32[4,128,256]{2,1,0:T(8,128)}, u32[]{:S(2)}, u32[]{:S(2)}) collective-permute-start(f32[4,128,256]{2,1,0:T(8,128)} %get-tuple-element.108), channel_id=1, source_target_pairs={{0,4},{4,0},{8,12},{12,8},{16,20},{20,16},{24,28},{28,24},{1,5},{5... | collective-permute-start | bytes 1572872 | tf_op jit(solution)/shard_map/ppermute | solution.py:250
  353.9 5.7 %copy-start.45 = (f32[8,128,2,128]{3,1,2,0:T(8,128)}, f32[8,128,2,128]{3,1,2,0:T(8,128)S(1)}, u32[]{:S(2)}) copy-start(f32[8,128,2,128]{3,1,2,0:T(8,128)S(1)} %fusion.13) | copy-start | bytes 3145732
  355.3 4.2 copy-start.13
  355.3 4.2 copy-start.73
  355.9 40.3 %collective-permute-start.19 = (f32[512]{0:T(512)}, f32[512]{0:T(512)}, u32[]{:S(2)}, u32[]{:S(2)}) collective-permute-start(f32[512]{0:T(512)} %pad_select_fusion), channel_id=1, source_target_pairs={{0,4},{4,0},{8,12},{12,8},{16,20},{20,16},{24,28},{28,24},{1,5},{5... | collective-permute-start | bytes 6152 | tf_op jit(solution)/shard_map/ppermute | solution.py:250
  365.3 2.6 copy-start.3
  367.9 5.5 %copy-start.29 = (f32[1024,256]{1,0:T(8,128)S(1)}, f32[1024,256]{1,0:T(8,128)}, u32[]{:S(2)}) copy-start(f32[1024,256]{1,0:T(8,128)} %get-tuple-element.71) | copy-start | bytes 3145732
  367.9 7.4 %copy-start.10 = (f32[1024,1024]{1,0:T(8,128)S(1)}, f32[1024,1024]{1,0:T(8,128)}, u32[]{:S(2)}) copy-start(f32[1024,1024]{1,0:T(8,128)} %get-tuple-element.25) | copy-start | bytes 12582916
  382.3 6.4 %copy-start.56 = (f32[256,256]{0,1:T(8,128)S(1)}, f32[256,256]{0,1:T(8,128)}, u32[]{:S(2)}) copy-start(f32[256,256]{0,1:T(8,128)} %get-tuple-element.146) | copy-start | bytes 786436
  383.3 4.6 %copy-start.57 = (f32[256,256]{0,1:T(8,128)S(1)}, f32[256,256]{0,1:T(8,128)}, u32[]{:S(2)}) copy-start(f32[256,256]{0,1:T(8,128)} %get-tuple-element.145) | copy-start | bytes 786436
  386.1 6.3 %copy-start.53 = (f32[256,256]{1,0:T(8,128)S(1)}, f32[256,256]{1,0:T(8,128)}, u32[]{:S(2)}) copy-start(f32[256,256]{1,0:T(8,128)} %copy.217) | copy-start | bytes 786436
  389.6 2.8 copy-start.54
  389.6 2.8 copy-start.55
  390.6 3.4 copy-start.52
  391.8 14.9 %collective-permute-start.7 = (f32[4,128,256]{2,1,0:T(8,128)S(1)}, f32[4,128,256]{2,1,0:T(8,128)S(1)}, u32[]{:S(2)}, u32[]{:S(2)}) collective-permute-start(f32[4,128,256]{2,1,0:T(8,128)S(1)} %pad_maximum_fusion.2), channel_id=1, source_target_pairs={{0,4},{4,0},{8,12},{12,8},{16,20},{20,16},{24,28},{28,24},{1,5},{5... | collective-permute-start | bytes 1572872 | tf_op jit(solution)/shard_map/ppermute | solution.py:250
  392.4 3.8 copy-start.82
  392.4 5.1 %copy-start.40 = (f32[4,1,128,256]{3,2,0,1:T(8,128)S(1)}, f32[4,1,128,256]{3,2,0,1:T(8,128)}, u32[]{:S(2)}) copy-start(f32[4,1,128,256]{3,2,0,1:T(8,128)} %get-tuple-element.107) | copy-start | bytes 1572868
  392.5 34.9 %collective-permute-start.10 = (f32[4,256,256]{2,1,0:T(8,128)S(1)}, f32[4,256,256]{2,1,0:T(8,128)S(1)}, u32[]{:S(2)}, u32[]{:S(2)}) collective-permute-start(f32[4,256,256]{2,1,0:T(8,128)S(1)} %pad_maximum_fusion.1), channel_id=1, source_target_pairs={{0,4},{4,0},{8,12},{12,8},{16,20},{20,16},{24,28},{28,24},{1,5},{5... | collective-permute-start | bytes 3145736 | tf_op jit(solution)/shard_map/ppermute | solution.py:250
  395.2 7.0 %collective-permute-start.2 = (f32[32,2048]{1,0:T(8,128)S(1)}, f32[32,2048]{1,0:T(8,128)S(1)}, u32[]{:S(2)}, u32[]{:S(2)}) collective-permute-start(f32[32,2048]{1,0:T(8,128)S(1)} %dynamic-slice_bitcast_fusion.3), channel_id=1, source_target_pairs={{0,2},{1,3},{2,0},{3,1},{4,6},{5,7},{6,4},{7,5},{8,10},{9,11},{10,... | collective-permute-start | bytes 786440 | tf_op jit(solution)/shard_map/ppermute | solution.py:258
  398.8 8.0 %copy-start.28 = (f32[2048,512]{1,0:T(8,128)S(1)}, f32[2048,512]{1,0:T(8,128)}, u32[]{:S(2)}) copy-start(f32[2048,512]{1,0:T(8,128)} %refs_0_.1) | copy-start | bytes 12582916
  398.9 41.2 %collective-permute-start.15 = (f32[1024,256]{1,0:T(8,128)S(1)}, f32[1024,256]{1,0:T(8,128)S(1)}, u32[]{:S(2)}, u32[]{:S(2)}) collective-permute-start(f32[1024,256]{1,0:T(8,128)S(1)} %bitcast.326), channel_id=1, source_target_pairs={{0,1},{1,0},{2,3},{3,2},{4,5},{5,4},{6,7},{7,6},{8,9},{9,8},{10,11... | collective-permute-start | bytes 3145736 | tf_op jit(solution)/shard_map/ppermute | solution.py:254
  413.8 13.6 %copy-start.46 = (f32[256,256]{1,0:T(8,128)S(1)}, f32[256,256]{1,0:T(8,128)}, u32[]{:S(2)}) copy-start(f32[256,256]{1,0:T(8,128)} %copy.216) | copy-start | bytes 786436
  413.8 13.6 %copy-start.47 = (f32[256,256]{1,0:T(8,128)S(1)}, f32[256,256]{1,0:T(8,128)}, u32[]{:S(2)}) copy-start(f32[256,256]{1,0:T(8,128)} %copy.215) | copy-start | bytes 786436
  413.8 13.6 %copy-start.48 = (f32[256,256]{1,0:T(8,128)S(1)}, f32[256,256]{1,0:T(8,128)}, u32[]{:S(2)}) copy-start(f32[256,256]{1,0:T(8,128)} %copy.214) | copy-start | bytes 786436
  416.1 13.4 %collective-permute-start.8 = (f32[2,32,2048]{2,1,0:T(8,128)S(1)}, f32[2,32,2048]{2,1,0:T(8,128)S(1)}, u32[]{:S(2)}, u32[]{:S(2)}) collective-permute-start(f32[2,32,2048]{2,1,0:T(8,128)S(1)} %dynamic-slice_bitcast_fusion), channel_id=1, source_target_pairs={{0,1},{1,0},{2,3},{3,2},{4,5},{5,4},{6,7},{7,6},{8,9},{9,8},{10,11... | collective-permute-start | bytes 1572872 | tf_op jit(solution)/shard_map/ppermute | solution.py:254
  429.4 6.3 %copy-start.62 = (f32[2048]{0:T(1024)S(1)}, f32[2048]{0:T(1024)}, u32[]{:S(2)}) copy-start(f32[2048]{0:T(1024)} %param.27) | copy-start | bytes 24580
  429.4 10.5 %copy-start.23 = (f32[128,2048]{1,0:T(8,128)S(1)}, f32[128,2048]{1,0:T(8,128)}, u32[]{:S(2)}) copy-start(f32[128,2048]{1,0:T(8,128)} %array_ref.2) | copy-start | bytes 3145732
  429.4 10.7 %copy-start.42 = (f32[1024,256]{1,0:T(8,128)S(1)}, f32[1024,256]{1,0:T(8,128)}, u32[]{:S(2)}) copy-start(f32[1024,256]{1,0:T(8,128)} %copy-done.41) | copy-start | bytes 3145732
  429.4 1.2 collective-permute-start.17
  430.6 3.7 collective-permute-start.18
  431.7 8.1 %collective-permute-start.9 = (f32[32,2048]{1,0:T(8,128)S(1)}, f32[32,2048]{1,0:T(8,128)S(1)}, u32[]{:S(2)}, u32[]{:S(2)}) collective-permute-start(f32[32,2048]{1,0:T(8,128)S(1)} %dynamic-slice_bitcast_fusion.2), channel_id=1, source_target_pairs={{0,2},{1,3},{2,0},{3,1},{4,6},{5,7},{6,4},{7,5},{8,10},{9,11},{10,... | collective-permute-start | bytes 786440 | tf_op jit(solution)/shard_map/ppermute | solution.py:258
  441.2 8.2 %copy-start.27 = (f32[256,1408]{1,0:T(8,128)S(1)}, f32[256,1408]{1,0:T(8,128)}, u32[]{:S(2)}) copy-start(f32[256,1408]{1,0:T(8,128)} %get-tuple-element.169) | copy-start | bytes 4325380
  441.3 7.3 %collective-permute-start.16 = (f32[256,256]{1,0:T(8,128)S(1)}, f32[256,256]{1,0:T(8,128)S(1)}, u32[]{:S(2)}, u32[]{:S(2)}) collective-permute-start(f32[256,256]{1,0:T(8,128)S(1)} %get-tuple-element.106), channel_id=1, source_target_pairs={{0,4},{4,0},{8,12},{12,8},{16,20},{20,16},{24,28},{28,24},{1,5},{5... | collective-permute-start | bytes 786440 | tf_op jit(solution)/shard_map/ppermute | solution.py:250
  443.6 6.9 %copy-start.25 = (f32[256,1408]{1,0:T(8,128)S(1)}, f32[256,1408]{1,0:T(8,128)}, u32[]{:S(2)}) copy-start(f32[256,1408]{1,0:T(8,128)} %get-tuple-element.170) | copy-start | bytes 4325380
  (43 other events, 69.8 us)

commit v4 on v1

--- a/solution.py
+++ b/solution.py
@@ -3,6 +3,8 @@
 import jax
 import jax.numpy as jnp
 from jax import lax
+from jax.experimental import pallas as pl
+from jax.experimental.pallas import tpu as pltpu
 from jax.sharding import PartitionSpec as P
 
 HDIM = 128
@@ -236,6 +238,1740 @@
     )
 
 
+Z, X = 4, 2
+
+
+def x_swap(array):
+    return lax.ppermute(array, "seq", [(s, s ^ 1) for s in range(Z * X)])
+
+
+def cut(array, place, size, axis):
+    return lax.dynamic_slice_in_dim(array, place * size, size, axis)
+
+
+def in_order(first, mine, other, axis):
+    return jnp.where(
+        first, jnp.concatenate([mine, other], axis), jnp.concatenate([other, mine], axis)
+    )
+
+
+F32, BF16 = jnp.float32, jnp.bfloat16
+MESH = pl.DeviceIdType.MESH
+ANY = pl.BlockSpec(memory_space=pl.ANY)
+WHOLE = pl.BlockSpec(memory_space=pltpu.VMEM)
+TILE = 256
+VMEM_BYTES = 60 << 20
+
+
+def halves(entries):
+    high = entries.astype(BF16)
+    return high, (entries - high.astype(F32)).astype(BF16)
+
+
+def product(left, right, contract_left, contract_right):
+    return lax.dot_general(
+        left,
+        right,
+        (((contract_left,), (contract_right,)), ((), ())),
+        preferred_element_type=F32,
+    )
+
+
+def three_pass(left, right, contract_left, contract_right):
+    (left_high, left_low), (right_high, right_low) = left, right
+    return product(left_high, right_high, contract_left, contract_right) + (
+        product(left_high, right_low, contract_left, contract_right)
+        + product(left_low, right_high, contract_left, contract_right)
+    )
+
+
+def few_rows(left, right, contract_right):
+    (left_high, left_low), (right_high, right_low) = left, right
+    rows = left_high.shape[0]
+    both = product(jnp.concatenate([left_high, left_low]), right_high, 1, contract_right)
+    return both[:rows] + (product(left_high, right_low, 1, contract_right) + both[rows:])
+
+
+def remote(src, dst, sems, index, device):
+    return pltpu.make_async_remote_copy(
+        src_ref=src,
+        dst_ref=dst,
+        send_sem=sems[0].at[index],
+        recv_sem=sems[1].at[index],
+        device_id=device,
+        device_id_type=MESH,
+    )
+
+
+def dma_sems(count):
+    return [pltpu.SemaphoreType.DMA((count,)), pltpu.SemaphoreType.DMA((count,))]
+
+
+class Move:
+    def __init__(self, ins, outs, scratch):
+        self.ins, self.outs, self.scratch_refs = ins, outs, scratch
+        place, part = lax.axis_index("seq"), lax.axis_index("mp")
+        self.z, self.x, self.y, self.core = place // X, place % X, part // 2, part % 2
+        self.setup()
+
+    def setup(self):
+        pass
+
+    def device(self, z, x, y, core):
+        return (z * X + x, y * 2 + core)
+
+    def x_peer(self):
+        return self.device(self.z, 1 - self.x, self.y, self.core)
+
+    def y_peer(self):
+        return self.device(self.z, self.x, 1 - self.y, self.core)
+
+    def core_peer(self):
+        return self.device(self.z, self.x, self.y, 1 - self.core)
+
+    def holds(self, way, step):
+        source = self.z - way * step
+        return (source >= 0) & (source < Z)
+
+    def goes_on(self, way, step):
+        return self.holds(way, step - 1) & (self.z + way >= 0) & (self.z + way < Z)
+
+    def each(self, step, action):
+        if step == 0:
+            action(1)
+        else:
+            for way in (1, -1):
+                pl.when(self.holds(way, step))(lambda way=way: action(way))
+
+    def greet(self, far):
+        barrier = pltpu.get_barrier_semaphore()
+
+        def signal(device):
+            pl.semaphore_signal(barrier, inc=1, device_id=device, device_id_type=MESH)
+
+        signal(self.x_peer())
+        signal(self.y_peer())
+        signal(self.core_peer())
+        if far:
+            for distance in range(1, Z):
+                signal(self.device((self.z + distance) % Z, self.x, self.y, self.core))
+            pl.semaphore_wait(barrier, 3 + Z - 1)
+        else:
+            for way in (1, -1):
+                ahead = (self.z + way >= 0) & (self.z + way < Z)
+                pl.when(ahead)(
+                    lambda way=way: signal(self.device(self.z + way, self.x, self.y, self.core))
+                )
+            neighbours = jnp.where(self.z > 0, 1, 0) + jnp.where(self.z < Z - 1, 1, 0)
+            pl.semaphore_wait(barrier, 3 + neighbours)
+
+
+class Gather(Move):
+    PIECES = 2
+
+    def in_specs(arrays):
+        return [ANY]
+
+    def results(arrays):
+        return [((Z * X * arrays[0].shape[0], arrays[0].shape[1]), ANY)]
+
+    def scratch(arrays):
+        return [*dma_sems(52 * Gather.PIECES), pltpu.SemaphoreType.DMA((1,))]
+
+    def setup(self):
+        (self.block,), (self.out,) = self.ins, self.outs
+        self.sems, self.local = self.scratch_refs[:2], self.scratch_refs[2]
+        self.rows = self.block.shape[0]
+        self.size = self.rows // self.PIECES
+        self.tile = self.block.shape[1] // 16
+
+    def cols(self, first, count):
+        return pl.ds(pl.multiple_of(first * self.tile, self.tile), count * self.tile)
+
+    def columns(self, y, core):
+        return self.cols(6 * y + 5 * core, 5)
+
+    def y_columns(self, y, big):
+        return self.cols(11 * y, 5) if big else self.cols(5 + 5 * y, 1)
+
+    def region(self, z, x, piece, columns):
+        row = (z * X + x) * self.rows + piece * self.size
+        return self.out.at[pl.ds(pl.multiple_of(row, self.size), self.size), columns]
+
+    def fetched(self, z, x, piece):
+        return self.region(z, x, piece, self.columns(self.y, self.core))
+
+    def own(self, piece):
+        return self.block.at[
+            pl.ds(piece * self.size, self.size), self.columns(self.y, self.core)
+        ]
+
+    def slot(self, way, step):
+        return 0 if step == 0 else (0 if way > 0 else 3) + step
+
+    def along(self, way, step, piece, arriving):
+        dst = self.fetched(self.z - way * (step if arriving else step - 1), self.x, piece)
+        return remote(
+            self.own(piece) if step == 1 and not arriving else dst,
+            dst,
+            self.sems,
+            52 * piece + (0 if way > 0 else 3) + step - 1,
+            self.device(self.z + way, self.x, self.y, self.core),
+        )
+
+    def across(self, way, step, piece, arriving):
+        dst = self.fetched(self.z - way * step, 1 - self.x if arriving else self.x, piece)
+        return remote(
+            self.own(piece) if step == 0 and not arriving else dst,
+            dst,
+            self.sems,
+            52 * piece + 6 + self.slot(way, step),
+            self.x_peer(),
+        )
+
+    def inside(self, way, step, other_x, piece, arriving):
+        region = self.region(
+            self.z - way * step,
+            1 - self.x if other_x else self.x,
+            piece,
+            self.columns(self.y, 1 - self.core if arriving else self.core),
+        )
+        index = 52 * piece + 13 + self.slot(way, step) + (0 if other_x else 6)
+        return remote(region, region, self.sems, index, self.core_peer())
+
+    def over_y(self, way, step, other_x, piece, arriving, big):
+        region = self.region(
+            self.z - way * step,
+            1 - self.x if other_x else self.x,
+            piece,
+            self.y_columns(1 - self.y if arriving else self.y, big),
+        )
+        index = 52 * piece + 26 + self.slot(way, step) + (0 if other_x else 6)
+        return remote(region, region, self.sems, index, self.y_peer())
+
+    def inside_y(self, way, step, other_x, piece, big):
+        region = self.region(
+            self.z - way * step,
+            1 - self.x if other_x else self.x,
+            piece,
+            self.y_columns(1 - self.y, big),
+        )
+        index = 52 * piece + 39 + self.slot(way, step) + (0 if other_x else 6)
+        return remote(region, region, self.sems, index, self.core_peer())
+
+    def sized(self, big, action):
+        pl.when(big)(lambda: action(True))
+        pl.when(jnp.logical_not(big))(lambda: action(False))
+
+    def pass_on(self, way, step, other_x, piece):
+        self.sized(
+            self.core == self.y,
+            lambda big: self.over_y(way, step, other_x, piece, False, big).start(),
+        )
+        self.inside(way, step, other_x, piece, False).start()
+
+    def begin(self):
+        for piece in range(self.PIECES):
+            self.across(1, 0, piece, False).start()
+            for way in (1, -1):
+                pl.when(self.goes_on(way, 1))(
+                    lambda way=way, piece=piece: self.along(way, 1, piece, False).start()
+                )
+        self.own_copy().start()
+
+    def own_copy(self):
+        row = pl.multiple_of((self.z * X + self.x) * self.rows, self.rows)
+        return pltpu.make_async_copy(
+            self.block, self.out.at[pl.ds(row, self.rows), :], self.local.at[0]
+        )
+
+    def arrive_along(self, step, piece):
+        def action(way):
+            self.along(way, step, piece, True).wait_recv()
+            if step < Z - 1:
+                pl.when(self.goes_on(way, step + 1))(
+                    lambda: self.along(way, step + 1, piece, False).start()
+                )
+            self.across(way, step, piece, False).start()
+            self.pass_on(way, step, False, piece)
+
+        self.each(step, action)
+
+    def arrive_across(self, step, piece):
+        def action(way):
+            self.across(way, step, piece, True).wait_recv()
+            self.pass_on(way, step, True, piece)
+
+        self.each(step, action)
+
+    def arrive_y(self, step, other_x, piece):
+        def action(way):
+            def sized(big):
+                self.over_y(way, step, other_x, piece, True, big).wait_recv()
+                self.inside_y(way, step, other_x, piece, big).start()
+
+            self.sized(self.core != self.y, sized)
+
+        self.each(step, action)
+
+    def finish(self):
+        self.own_copy().wait()
+        for piece in range(self.PIECES):
+            for way in (1, -1):
+                for step in range(1, Z):
+                    pl.when(self.goes_on(way, step))(
+                        lambda way=way, step=step, piece=piece: self.along(
+                            way, step, piece, False
+                        ).wait_send()
+                    )
+            for step in range(Z):
+
+                def action(way, step=step, piece=piece):
+                    self.across(way, step, piece, False).wait_send()
+                    for other_x in (False, True) if step else (True,):
+                        self.inside(way, step, other_x, piece, False).wait_send()
+                        self.inside(way, step, other_x, piece, True).wait_recv()
+
+                        def sized(big, other_x=other_x):
+                            self.over_y(way, step, other_x, piece, False, big).wait_send()
+                            self.inside_y(way, step, other_x, piece, not big).wait_send()
+                            self.inside_y(way, step, other_x, piece, big).wait_recv()
+
+                        self.sized(self.core == self.y, sized)
+
+                self.each(step, action)
+
+    def events(self):
+        def round_of(index):
+            step, piece = index // 2 + 1, index % 2
+
+            def event():
+                if step < Z:
+                    self.arrive_along(step, piece)
+                if step <= Z:
+                    self.arrive_across(step - 1, piece)
+                if 1 <= step - 1 < Z:
+                    self.arrive_y(step - 1, False, piece)
+                if 0 <= step - 2 < Z:
+                    self.arrive_y(step - 2, True, piece)
+
+            return event
+
+        return [round_of(index) for index in range(2 * (Z + 1))] + [self.finish]
+
+
+class Sum(Move):
+    def in_specs(arrays):
+        return [WHOLE]
+
+    def results(arrays):
+        return [(arrays[0].shape, WHOLE)]
+
+    def scratch(arrays):
+        rows, columns = arrays[0].shape
+        return [pltpu.VMEM((4, rows, columns // 2), F32), *dma_sems(3)]
+
+    def setup(self):
+        (self.part,), (self.out,) = self.ins, self.outs
+        self.landing, self.sems = self.scratch_refs[0], self.scratch_refs[1:]
+        self.half = self.part.shape[1] // 2
+
+    def columns(self, ref, core):
+        return ref.at[:, pl.ds(pl.multiple_of(core * self.half, self.half), self.half)]
+
+    def first(self):
+        return remote(
+            self.columns(self.part, 1 - self.core),
+            self.landing.at[0],
+            self.sems,
+            0,
+            self.core_peer(),
+        )
+
+    def second(self):
+        return remote(self.landing.at[1], self.landing.at[2], self.sems, 1, self.y_peer())
+
+    def third(self):
+        return remote(self.landing.at[1], self.landing.at[3], self.sems, 2, self.core_peer())
+
+    def begin(self):
+        self.first().start()
+
+    def to_y(self):
+        self.first().wait()
+        self.landing[1] = self.columns(self.part, self.core)[...] + self.landing[0]
+        self.second().start()
+
+    def back(self):
+        self.second().wait()
+        self.landing[1] = self.landing[1] + self.landing[2]
+        self.third().start()
+
+    def finish(self):
+        self.third().wait()
+        self.columns(self.out, self.core)[...] = self.landing[1]
+        self.columns(self.out, 1 - self.core)[...] = self.landing[3]
+
+    def events(self):
+        return [self.to_y, self.back, self.finish]
+
+
+class Scatter(Move):
+    def in_specs(arrays):
+        return [WHOLE]
+
+    def results(arrays):
+        rows, columns = arrays[0].shape
+        return [((rows // 4, columns), WHOLE)]
+
+    def scratch(arrays):
+        rows, columns = arrays[0].shape
+        return [pltpu.VMEM((5, rows // 4, columns), F32), *dma_sems(3)]
+
+    def setup(self):
+        (self.part,), (self.out,) = self.ins, self.outs
+        self.landing, self.sems = self.scratch_refs[0], self.scratch_refs[1:]
+        self.rows = self.part.shape[0] // 4
+
+    def block(self, y, core):
+        row = pl.multiple_of((y * 2 + core) * self.rows, self.rows)
+        return self.part.at[pl.ds(row, self.rows), :]
+
+    def to_core(self, y):
+        block = self.block(self.y if y == 0 else 1 - self.y, 1 - self.core)
+        return remote(block, self.landing.at[y], self.sems, y, self.core_peer())
+
+    def to_y(self):
+        return remote(self.landing.at[2], self.landing.at[3], self.sems, 2, self.y_peer())
+
+    def begin(self):
+        self.to_core(1).start()
+        self.to_core(0).start()
+
+    def middle(self):
+        self.to_core(1).wait()
+        self.landing[2] = self.block(1 - self.y, self.core)[...] + self.landing[1]
+        self.to_y().start()
+
+    def finish(self):
+        self.to_core(0).wait()
+        self.to_y().wait()
+        self.out[...] = (self.block(self.y, self.core)[...] + self.landing[0]) + self.landing[3]
+
+    def events(self):
+        return [self.middle, self.finish]
+
+
+class Heads(Move):
+    def in_specs(arrays):
+        return [ANY]
+
+    def results(arrays):
+        rows, columns = arrays[0].shape
+        return [((Z * X * rows, columns // X), ANY)]
+
+    def scratch(arrays):
+        return [*dma_sems(7), pltpu.SemaphoreType.DMA((1,))]
+
+    def setup(self):
+        (self.own,), (self.out,) = self.ins, self.outs
+        self.sems, self.local = self.scratch_refs[:2], self.scratch_refs[2]
+        self.rows, columns = self.own.shape
+        self.width = columns // X
+
+    def block(self, z, x):
+        row = pl.multiple_of((z * X + x) * self.rows, self.rows)
+        return self.out.at[pl.ds(row, self.rows), :]
+
+    def plane(self, z):
+        row = pl.multiple_of(z * X * self.rows, X * self.rows)
+        return self.out.at[pl.ds(row, X * self.rows), :]
+
+    def own_columns(self, x):
+        return self.own.at[:, pl.ds(pl.multiple_of(x * self.width, self.width), self.width)]
+
+    def swap(self):
+        return remote(
+            self.own_columns(1 - self.x), self.block(self.z, self.x), self.sems, 6, self.x_peer()
+        )
+
+    def keep(self):
+        return pltpu.make_async_copy(
+            self.own_columns(self.x), self.block(self.z, self.x), self.local.at[0]
+        )
+
+    def along(self, way, step, arriving):
+        plane = self.plane(self.z - way * (step if arriving else step - 1))
+        return remote(
+            plane,
+            plane,
+            self.sems,
+            (0 if way > 0 else 3) + step - 1,
+            self.device(self.z + way, self.x, self.y, self.core),
+        )
+
+    def begin(self):
+        self.swap().start()
+        self.keep().start()
+
+    def start_along(self, way, step):
+        pl.when(self.goes_on(way, step))(lambda: self.along(way, step, False).start())
+
+    def swapped(self):
+        self.swap().wait()
+        self.keep().wait()
+        for way in (1, -1):
+            self.start_along(way, 1)
+
+    def arrive(self, step):
+        def action(way):
+            self.along(way, step, True).wait_recv()
+            if step < Z - 1:
+                self.start_along(way, step + 1)
+
+        self.each(step, action)
+
+    def finish(self):
+        self.arrive(Z - 1)
+        for way in (1, -1):
+            for step in range(1, Z):
+                pl.when(self.goes_on(way, step))(
+                    lambda way=way, step=step: self.along(way, step, False).wait_send()
+                )
+
+    def events(self):
+        return [self.swapped, lambda: self.arrive(1), lambda: self.arrive(2), self.finish]
+
+
+class Columns(Move):
+    def in_specs(arrays):
+        return [ANY]
+
+    def results(arrays):
+        rows, columns = arrays[0].shape
+        return [((Z, X, rows, columns // Z), ANY)]
+
+    def scratch(arrays):
+        return [*dma_sems(Z + Z + 1), pltpu.SemaphoreType.DMA((1,))]
+
+    def setup(self):
+        (self.own,), (self.out,) = self.ins, self.outs
+        self.sems, self.local = self.scratch_refs[:2], self.scratch_refs[2]
+        self.half = self.own.shape[1] // (2 * Z)
+
+    def piece(self, z):
+        start = pl.multiple_of((z * 2 + self.core) * self.half, self.half)
+        return self.own.at[:, pl.ds(start, self.half)]
+
+    def landing(self, z, x, core):
+        start = pl.multiple_of(core * self.half, self.half)
+        return self.out.at[z, x, :, pl.ds(start, self.half)]
+
+    def along(self, distance):
+        z = (self.z + distance) % Z
+        return remote(
+            self.piece(z),
+            self.landing(self.z, self.x, self.core),
+            self.sems,
+            distance,
+            self.device(z, self.x, self.y, self.core),
+        )
+
+    def keep(self):
+        return pltpu.make_async_copy(
+            self.piece(self.z), self.landing(self.z, self.x, self.core), self.local.at[0]
+        )
+
+    def across(self, distance):
+        block = self.landing((self.z - distance) % Z, self.x, self.core)
+        return remote(block, block, self.sems, Z + distance, self.x_peer())
+
+    def inside(self):
+        start = pl.multiple_of(self.core * self.half, self.half)
+        part = self.out.at[:, :, :, pl.ds(start, self.half)]
+        return remote(part, part, self.sems, 2 * Z, self.core_peer())
+
+    def begin(self):
+        self.keep().start()
+        for distance in (1, 3, 2):
+            self.along(distance).start()
+
+    def arrived(self, distance):
+        if distance == 0:
+            self.keep().wait()
+        else:
+            self.along(distance).wait()
+        self.across(distance).start()
+
+    def all_here(self):
+        for distance in range(Z):
+            self.across(distance).wait()
+        self.inside().start()
+
+    def events(self):
+        return [
+            lambda: self.arrived(0),
+            lambda: self.arrived(1),
+            lambda: self.arrived(3),
+            lambda: self.arrived(2),
+            self.all_here,
+            lambda: self.inside().wait(),
+        ]
+
+
+class SwapX(Move):
+    def in_specs(arrays):
+        return [ANY] * len(arrays)
+
+    def results(arrays):
+        return [(array.shape, ANY) for array in arrays]
+
+    def scratch(arrays):
+        return dma_sems(len(arrays))
+
+    def setup(self):
+        pass
+
+    def copies(self):
+        return [
+            remote(src, dst, self.scratch_refs, index, self.x_peer())
+            for index, (src, dst) in enumerate(zip(self.ins, self.outs, strict=True))
+        ]
+
+    def begin(self):
+        for copy in self.copies():
+            copy.start()
+
+    def finish(self):
+        for copy in self.copies():
+            copy.wait()
+
+    def events(self):
+        return [self.finish]
+
+
+class SwapBlocks(Move):
+    def in_specs(arrays):
+        return [ANY] * len(arrays)
+
+    def results(arrays):
+        return [((X, array.shape[0] // X, array.shape[1]), ANY) for array in arrays]
+
+    def scratch(arrays):
+        return [*dma_sems(len(arrays)), pltpu.SemaphoreType.DMA((len(arrays),))]
+
+    def setup(self):
+        self.sems, self.local = self.scratch_refs[:2], self.scratch_refs[2]
+
+    def ends(self, index, x):
+        src, dst = self.ins[index], self.outs[index]
+        rows = src.shape[0] // X
+        return src.at[pl.ds(pl.multiple_of(x * rows, rows), rows), :], dst.at[self.x]
+
+    def send(self, index):
+        return remote(*self.ends(index, 1 - self.x), self.sems, index, self.x_peer())
+
+    def keep(self, index):
+        return pltpu.make_async_copy(*self.ends(index, self.x), self.local.at[index])
+
+    def begin(self):
+        for index in range(len(self.ins)):
+            self.send(index).start()
+            self.keep(index).start()
+
+    def finish(self):
+        for index in range(len(self.ins)):
+            self.send(index).wait()
+            self.keep(index).wait()
+
+    def events(self):
+        return [self.finish]
+
+
+class SumAll(Move):
+    def in_specs(arrays):
+        return [WHOLE]
+
+    def results(arrays):
+        rows, columns = arrays[0].shape
+        return [((rows // X, columns), WHOLE)]
+
+    def scratch(arrays):
+        rows, columns = arrays[0].shape
+        return [pltpu.VMEM((6, rows // X, columns), F32), *dma_sems(3)]
+
+    def setup(self):
+        (self.part,), (self.out,) = self.ins, self.outs
+        self.landing, self.sems = self.scratch_refs[0], self.scratch_refs[1:]
+        self.rows = self.part.shape[0] // X
+
+    def half(self, x):
+        return self.part.at[pl.ds(pl.multiple_of(x * self.rows, self.rows), self.rows), :]
+
+    def first(self):
+        return remote(self.half(1 - self.x), self.landing.at[0], self.sems, 0, self.x_peer())
+
+    def second(self):
+        return remote(self.landing.at[1], self.landing.at[2], self.sems, 1, self.core_peer())
+
+    def third(self):
+        return remote(self.landing.at[3], self.landing.at[4], self.sems, 2, self.y_peer())
+
+    def begin(self):
+        self.first().start()
+
+    def to_core(self):
+        self.first().wait()
+        self.landing[1] = self.half(self.x)[...] + self.landing[0]
+        self.second().start()
+
+    def to_y(self):
+        self.second().wait()
+        self.landing[3] = self.landing[1] + self.landing[2]
+        self.third().start()
+
+    def finish(self):
+        self.third().wait()
+        self.out[...] = self.landing[3] + self.landing[4]
+
+    def events(self):
+        return [self.to_core, self.to_y, self.finish]
+
+
+class Refs(dict):
+    __getattr__ = dict.__getitem__
+
+
+def fused(arrays, results, scratch, steps, body, collective_id, far=False, flops=0):
+    names = [*arrays, *results, *scratch]
+
+    def kernel(*refs):
+        refs = list(refs)
+        here = Refs(zip([*arrays, *results], refs, strict=False))
+        del refs[: len(arrays) + len(results)]
+        for name, needed in scratch.items():
+            here[name] = refs[: len(needed)]
+            del refs[: len(needed)]
+        step = pl.program_id(0)
+        if collective_id is not None:
+            pl.when(step == 0)(lambda: Move([], [], []).greet(far))
+        body(here, step)
+
+    outputs = pl.pallas_call(
+        kernel,
+        grid=(steps,),
+        out_shape=[jax.ShapeDtypeStruct(shape, F32) for shape, _ in results.values()],
+        in_specs=[spec for _, spec in arrays.values()],
+        out_specs=[spec for _, spec in results.values()],
+        scratch_shapes=[one for needed in scratch.values() for one in needed],
+        compiler_params=pltpu.CompilerParams(
+            has_side_effects=True,
+            vmem_limit_bytes=VMEM_BYTES,
+            **({} if collective_id is None else dict(collective_id=collective_id)),
+        ),
+        cost_estimate=pl.CostEstimate(flops=flops, bytes_accessed=32 << 20, transcendentals=0),
+    )(*(array for array, _ in arrays.values()))
+    return Refs(zip(results, outputs, strict=True))
+
+
+def at(now, when, *actions):
+    for action in actions:
+        pl.when(now == when)(action)
+
+
+def schedule(now, when, events):
+    for event, moment in zip(events, when, strict=True):
+        pl.when(now == moment)(event)
+
+
+def gather_tokens_fast(block, collective_id):
+    def body(refs, step):
+        move = Gather([refs.block], [refs.all], refs.move)
+        move.begin()
+        for event in move.events():
+            event()
+
+    return fused(
+        dict(block=(block, ANY)),
+        dict(all=Gather.results([block])[0]),
+        dict(move=Gather.scratch([block])),
+        1,
+        body,
+        collective_id,
+    ).all
+
+
+def halves_scratch(rows, inner):
+    return [
+        pltpu.VMEM((rows, inner), BF16),
+        pltpu.VMEM((rows, inner), BF16),
+        pltpu.VMEM((rows // 128, 128, inner), F32),
+        pltpu.SemaphoreType.DMA((rows // 128,)),
+    ]
+
+
+def load_halves(src_ref, high_ref, low_ref, stage_ref, sem, change=None):
+    count, rows, _ = stage_ref.shape
+
+    def spot(index):
+        return pl.ds(pl.multiple_of(index * rows, rows), rows)
+
+    def fetch(index):
+        return pltpu.make_async_copy(
+            src_ref.at[spot(index), :], stage_ref.at[index], sem.at[index]
+        )
+
+    for index in range(count):
+        fetch(index).start()
+
+    def split(index, carried):
+        fetch(index).wait()
+        if change is not None:
+            change(index)
+        high, low = halves(stage_ref[index])
+        high_ref[spot(index), :] = high
+        low_ref[spot(index), :] = low
+        return carried
+
+    lax.fori_loop(0, count, split, 0)
+
+
+STRIP = 256
+
+
+def strips(rows, action):
+    def one(index, carried):
+        action(index, pl.ds(pl.multiple_of(index * STRIP, STRIP), STRIP))
+        return carried
+
+    lax.fori_loop(0, rows // STRIP, one, 0)
+
+
+def block_fetch(src, buf, sem, index):
+    return pltpu.make_async_copy(src, buf.at[index], sem.at[index])
+
+
+def mixer_kernel(
+    all_tokens, tokens_in, cotangent, lengths, lower_bound, in_weights, out_weight, w_down,
+    first_gain, group_gain, second_gain, collective_id,
+):
+    rows, inner = all_tokens.shape
+    own_rows = tokens_in.shape[0]
+    count = len(in_weights)
+    wide = inner // Z
+    heads = TILE // HDIM
+    chunks = rows // CHUNK
+    columns = w_down.shape[0]
+    tiles = pl.cdiv(columns, TILE)
+    parts = rows // STRIP
+    middle = count + chunks
+    steps = middle + 1 + tiles
+
+    def body(refs, step):
+        place = lax.axis_index("seq")
+        x = place % X
+        here = pl.ds(pl.multiple_of(x * TILE, TILE), TILE)
+        there = pl.ds(pl.multiple_of((1 - x) * TILE, TILE), TILE)
+        first_col = pl.multiple_of((place // X) * wide, wide)
+        gather = Gather([refs.cotangent], [refs.all_cotangent], refs.gather)
+        part_ref, sum_ref, *sum_scratch = refs.sum
+        total = Sum([part_ref], [sum_ref], sum_scratch)
+        high_ref, low_ref, stage_ref, stage_sem = refs.halves
+        weight_buf, weight_sem, out_buf, out_sem, down_buf, down_sem = refs.weights
+        (state_ref,) = refs.state
+        other_ref, send, recv = refs.swap
+        weight_refs = [refs[f"weight_{index}"] for index in range(count)]
+        now = step * parts
+
+        def fetch(index):
+            return block_fetch(weight_refs[index].at[:, here], weight_buf, weight_sem, index % 2)
+
+        def fetch_out():
+            return pltpu.make_async_copy(refs.out_weight, out_buf, out_sem.at[0])
+
+        def fetch_down(tile, size=TILE):
+            return pltpu.make_async_copy(
+                refs.w_down.at[pl.ds(pl.multiple_of(tile * TILE, TILE), size), :],
+                down_buf.at[lax.rem(tile, 2), pl.ds(0, size), :],
+                down_sem.at[lax.rem(tile, 2)],
+            )
+
+        def sized(tile, action):
+            last = columns - (tiles - 1) * TILE
+            pl.when(tile < tiles - 1)(lambda: action(TILE))
+            pl.when(tile == tiles - 1)(lambda: action(last))
+
+        def swap():
+            peer = pl.multiple_of((place + 1 - 2 * x) * own_rows, own_rows)
+            return remote(
+                refs.mixer.at[pl.ds(peer, own_rows), :], other_ref, (send, recv), 0, gather.x_peer()
+            )
+
+        def pause(part):
+            schedule(now + part, (1, 3, 5, 7, 9, 11, 13, 15, 20, 24), gather.events()[:-1])
+            schedule(now + part, (4 * middle + 4, 4 * middle + 15, 4 * middle + 19), total.events())
+
+        def normalize(index):
+            entries = stage_ref[index]
+            stage_ref[index] = entries * rms(entries) * refs.first_gain[...]
+            refs.normed_cols[pl.ds(pl.multiple_of(index * 128, 128), 128), :] = stage_ref[
+                index, :, pl.ds(first_col, wide)
+            ]
+
+        @pl.when(step == 0)
+        def _():
+            gather.begin()
+            fetch(0).start()
+            fetch_out().start()
+            load_halves(refs.tokens, high_ref, low_ref, stage_ref, stage_sem, normalize)
+            state_ref[...] = jnp.zeros_like(state_ref)
+
+        for index in range(count):
+
+            @pl.when(step == index)
+            def _(index=index):
+                if index + 1 < count:
+                    fetch(index + 1).start()
+                fetch(index).wait()
+
+        @pl.when(step < count)
+        def _():
+            weight = halves(weight_buf[lax.rem(step, 2)])
+            target = pl.ds(pl.multiple_of(step * TILE, TILE), TILE)
+
+            def strip(index, spot):
+                refs.projected[spot, target] = three_pass(
+                    (high_ref[spot, :], low_ref[spot, :]), weight, 1, 0
+                )
+                pause(index)
+
+            strips(rows, strip)
+
+        @pl.when((step >= count) & (step < middle))
+        def _():
+            chunk = step - count
+            spot = pl.ds(pl.multiple_of(chunk * CHUNK, CHUNK), CHUNK)
+            forward_chunk(
+                chunk,
+                refs.lengths,
+                refs.projected.at[spot, :],
+                refs.lower_bound.at[:, here],
+                refs.group_gain.at[:, here],
+                refs.mixer.at[spot, :],
+                refs.raw.at[spot, :],
+                refs.states.at[pl.ds(chunk, 1)],
+                state_ref,
+            )
+            pause(0)
+
+        @pl.when(step == middle)
+        def _():
+            swap().start()
+            fetch_down(0).start()
+            fetch_out().wait()
+            own = refs.mixer[pl.ds(pl.multiple_of(place * own_rows, own_rows), own_rows), :]
+            part_ref[...] = few_rows(halves(own), halves(out_buf[here, :]), 0)
+            swap().wait()
+            part_ref[...] += few_rows(halves(other_ref[...]), halves(out_buf[there, :]), 0)
+            total.begin()
+            gather.finish()
+            load_halves(refs.all_cotangent, high_ref, low_ref, stage_ref, stage_sem)
+
+        @pl.when(step > middle)
+        def _():
+            tile = step - middle - 1
+            pl.when(tile < tiles - 1)(
+                lambda: sized(tile + 1, lambda size: fetch_down(tile + 1, size).start())
+            )
+            sized(tile, lambda size: fetch_down(tile, size).wait())
+            weight = halves(jnp.transpose(down_buf[lax.rem(tile, 2)]))
+
+            def strip(index, spot):
+                refs.grad_hidden[spot, :] = three_pass(
+                    (high_ref[spot, :], low_ref[spot, :]), weight, 1, 0
+                )
+                pause(index)
+
+            strips(rows, strip)
+
+        @pl.when(step == steps - 1)
+        def _():
+            residual = refs.tokens_in[...] + sum_ref[...]
+            refs.residual[...] = residual
+            refs.normed_two[...] = residual * rms(residual) * refs.second_gain[...]
+
+    own_shape = (own_rows, inner)
+    return fused(
+        dict(
+            lengths=(lengths, pl.BlockSpec(memory_space=pltpu.SMEM)),
+            tokens=(all_tokens, ANY),
+            tokens_in=(tokens_in, WHOLE),
+            cotangent=(cotangent, ANY),
+            lower_bound=(lower_bound[None], WHOLE),
+            first_gain=(first_gain[None], WHOLE),
+            group_gain=(group_gain[None], WHOLE),
+            second_gain=(second_gain[None], WHOLE),
+            out_weight=(out_weight, ANY),
+            w_down=(w_down, ANY),
+            **{f"weight_{index}": (weight, ANY) for index, weight in enumerate(in_weights)},
+        ),
+        dict(
+            all_cotangent=((rows, inner), ANY),
+            projected=((rows, count * TILE), WHOLE),
+            normed_cols=((rows, wide), WHOLE),
+            mixer=((rows, TILE), WHOLE),
+            raw=((rows, TILE), WHOLE),
+            states=((chunks, heads, HDIM, HDIM), WHOLE),
+            grad_hidden=(
+                (rows, columns),
+                pl.BlockSpec((rows, TILE), lambda step: (0, jnp.maximum(step - middle - 1, 0))),
+            ),
+            residual=(own_shape, WHOLE),
+            normed_two=(own_shape, WHOLE),
+        ),
+        dict(
+            halves=halves_scratch(rows, inner),
+            weights=[
+                pltpu.VMEM((2, inner, TILE), F32),
+                pltpu.SemaphoreType.DMA((2,)),
+                pltpu.VMEM(out_weight.shape, F32),
+                pltpu.SemaphoreType.DMA((1,)),
+                pltpu.VMEM((2, TILE, inner), F32),
+                pltpu.SemaphoreType.DMA((2,)),
+            ],
+            state=[pltpu.VMEM((heads, HDIM, HDIM), F32)],
+            swap=[pltpu.VMEM((own_rows, TILE), F32), *dma_sems(1)],
+            gather=Gather.scratch([cotangent]),
+            sum=[
+                pltpu.VMEM(own_shape, F32),
+                pltpu.VMEM(own_shape, F32),
+                *Sum.scratch([tokens_in]),
+            ],
+        ),
+        steps,
+        body,
+        collective_id,
+        flops=6 * rows * inner * (count * TILE + columns),
+    )
+
+
+def feed_forward_kernel(
+    normed_two, residual, cotangent, grad_hidden, w_gate, w_up, w_down, out_weight, second_gain, collective_id
+):
+    rows, inner = normed_two.shape
+    columns = w_gate.shape[1]
+    tiles = pl.cdiv(columns, TILE)
+
+    def body(refs, step):
+        gather = Gather([refs.normed_two], [refs.all_normed_two], refs.gather)
+        part_ref, sum_ref, *sum_scratch = refs.sum
+        total = Sum([part_ref], [sum_ref], sum_scratch)
+        out_buf, out_sem = refs.out
+        fetch_out = pltpu.make_async_copy(refs.out_weight, out_buf, out_sem.at[0])
+        events = gather.events()
+
+        def pause(part):
+            schedule(step * 2 + part, (0, 1, 2, 3, 4, 5, 7, 9), events[:8])
+
+        @pl.when(step == 0)
+        def _():
+            gather.begin()
+            fetch_out.start()
+            refs.ffn[...] = jnp.zeros_like(refs.ffn)
+            part_ref[...] = jnp.zeros_like(part_ref)
+
+        def inside(shape, axis):
+            return step * TILE + lax.broadcasted_iota(jnp.int32, shape, axis) < columns
+
+        gate_weight = halves(jnp.where(inside((inner, TILE), 1), refs.w_gate[...], 0.0))
+        up_weight = halves(jnp.where(inside((inner, TILE), 1), refs.w_up[...], 0.0))
+        normed = halves(refs.normed_two[...])
+        a = few_rows(normed, gate_weight, 0)
+        b = few_rows(normed, up_weight, 0)
+        pause(0)
+        e = jnp.where(inside((rows, TILE), 1), refs.grad_hidden[...], 0.0)
+        gate = jax.nn.sigmoid(a)
+        silu_a = a * gate
+        down_weight = halves(jnp.where(inside((TILE, inner), 0), refs.w_down[...], 0.0))
+        refs.ffn[...] += few_rows(halves(silu_a * b), down_weight, 0)
+        part_ref[...] += few_rows(
+            halves(e * b * (gate * (1.0 + a * (1.0 - gate)))), gate_weight, 1
+        ) + few_rows(halves(e * silu_a), up_weight, 1)
+        pause(1)
+
+        @pl.when(step == tiles - 1)
+        def _():
+            total.begin()
+            total.to_y()
+            events[8]()
+            events[9]()
+            total.back()
+            gather.finish()
+            total.finish()
+            residual_here = refs.residual[...]
+            scale = rms(residual_here)
+            summed = sum_ref[...]
+            pulled = summed * refs.second_gain[...]
+            grad_residual = (
+                refs.cotangent[...]
+                + scale * pulled
+                - residual_here
+                * (scale * scale * scale * jnp.mean(pulled * residual_here, -1, keepdims=True))
+            )
+            refs.grad_residual[...] = grad_residual
+            refs.second[...] = jnp.broadcast_to(
+                jnp.sum(summed * residual_here * scale, 0, keepdims=True), refs.second.shape
+            )
+            fetch_out.wait()
+            refs.grad_mixer[...] = few_rows(halves(grad_residual), halves(out_buf[...]), 1)
+
+    by_column = pl.BlockSpec((inner, TILE), lambda step: (0, step))
+    return fused(
+        dict(
+            normed_two=(normed_two, WHOLE),
+            residual=(residual, WHOLE),
+            cotangent=(cotangent, WHOLE),
+            grad_hidden=(
+                grad_hidden,
+                pl.BlockSpec((rows, TILE), lambda step: (lax.axis_index("seq"), step)),
+            ),
+            w_gate=(w_gate, by_column),
+            w_up=(w_up, by_column),
+            w_down=(w_down, pl.BlockSpec((TILE, inner), lambda step: (step, 0))),
+            out_weight=(out_weight, ANY),
+            second_gain=(second_gain[None], WHOLE),
+        ),
+        dict(
+            all_normed_two=Gather.results([normed_two])[0],
+            ffn=((rows, inner), WHOLE),
+            grad_residual=((rows, inner), WHOLE),
+            grad_mixer=((rows, out_weight.shape[0]), WHOLE),
+            second=((8, inner), WHOLE),
+        ),
+        dict(
+            gather=Gather.scratch([normed_two]),
+            sum=[
+                pltpu.VMEM((rows, inner), F32),
+                pltpu.VMEM((rows, inner), F32),
+                *Sum.scratch([normed_two]),
+            ],
+            out=[pltpu.VMEM(out_weight.shape, F32), pltpu.SemaphoreType.DMA((1,))],
+        ),
+        tiles,
+        body,
+        collective_id,
+        flops=30 * rows * inner * columns,
+    )
+
+
+def tile_strips(refs, step, first_step, pause):
+    high_ref, low_ref, stage_ref, stage_sem, cols_high_ref, cols_low_ref = refs.halves
+    grads = refs.grad_gate, refs.grad_up, refs.grad_down
+
+    @pl.when(step == first_step)
+    def _():
+        load_halves(refs.all_normed_two, high_ref, low_ref, stage_ref, stage_sem)
+        cols_high_ref[...], cols_low_ref[...] = halves(jnp.transpose(refs.normed_cols[...]))
+
+    gate_weight, up_weight = halves(refs.w_gate[...]), halves(refs.w_up[...])
+    for grad_ref in grads:
+        grad_ref[...] = jnp.zeros_like(grad_ref)
+
+    def strip(index, spot):
+        normed = high_ref[spot, :], low_ref[spot, :]
+        a = three_pass(normed, gate_weight, 1, 0)
+        b = three_pass(normed, up_weight, 1, 0)
+        gate = jax.nn.sigmoid(a)
+        silu_a = a * gate
+        e = refs.grad_hidden[spot, :]
+        cols = cols_high_ref[:, spot], cols_low_ref[:, spot]
+        grads[0][...] += three_pass(cols, halves(e * b * (gate * (1.0 + a * (1.0 - gate)))), 1, 0)
+        grads[1][...] += three_pass(cols, halves(e * silu_a), 1, 0)
+        grads[2][...] += three_pass(
+            halves(jnp.transpose(silu_a * b)), halves(refs.cot_cols[spot, :]), 1, 0
+        )
+        pause(index)
+
+    strips(refs.all_normed_two.shape[0], strip)
+
+
+def tile_parts(all_normed_two, all_cotangent, grad_hidden, w_gate, w_up, first, count, tile_of):
+    rows, inner = all_normed_two.shape
+    narrow = inner // (Z * X)
+    columns = min(count * TILE, w_gate.shape[1] - first * TILE)
+    own_columns = pl.BlockSpec((rows, narrow), lambda step: (0, lax.axis_index("seq")))
+    by_column = pl.BlockSpec((inner, TILE), lambda step: (0, first + tile_of(step)))
+    grad_spec = pl.BlockSpec((narrow, TILE), lambda step: (0, tile_of(step)))
+    arrays = dict(
+        all_normed_two=(all_normed_two, ANY),
+        grad_hidden=(
+            grad_hidden, pl.BlockSpec((rows, TILE), lambda step: (0, first + tile_of(step)))
+        ),
+        w_gate=(w_gate, by_column),
+        w_up=(w_up, by_column),
+        normed_cols=(all_normed_two, own_columns),
+        cot_cols=(all_cotangent, own_columns),
+    )
+    results = dict(
+        grad_gate=((narrow, columns), grad_spec),
+        grad_up=((narrow, columns), grad_spec),
+        grad_down=(
+            (columns, narrow), pl.BlockSpec((TILE, narrow), lambda step: (tile_of(step), 0))
+        ),
+    )
+    scratch = dict(
+        halves=[
+            *halves_scratch(rows, inner),
+            pltpu.VMEM((narrow, rows), BF16),
+            pltpu.VMEM((narrow, rows), BF16),
+        ]
+    )
+    return arrays, results, scratch
+
+
+def heads_kernel(grad_mixer, ffn, tiles, count, collective_id):
+    arrays, results, scratch = tiles(lambda step: step)
+    parts = arrays["all_normed_two"][0].shape[0] // STRIP
+
+    def body(refs, step):
+        heads = Heads([refs.grad_mixer], [refs.all_grad_mixer], refs.heads)
+        scatter = Scatter([refs.ffn], [refs.ffn_share], refs.scatter)
+
+        @pl.when(step == 0)
+        def _():
+            heads.begin()
+            scatter.begin()
+
+        def pause(part):
+            now = step * parts + part
+            schedule(now, (0, 2, 4, 6), heads.events())
+            schedule(now, (1, 5), scatter.events())
+
+        tile_strips(refs, step, 0, pause)
+
+    return fused(
+        dict(grad_mixer=(grad_mixer, ANY), ffn=(ffn, WHOLE), **arrays),
+        dict(
+            all_grad_mixer=Heads.results([grad_mixer])[0],
+            ffn_share=Scatter.results([ffn])[0],
+            **results,
+        ),
+        dict(heads=Heads.scratch([grad_mixer]), scatter=Scatter.scratch([ffn]), **scratch),
+        count,
+        body,
+        collective_id,
+    )
+
+
+def last_kernel(grads, group, blocks, first_part, in_weights, tiles, count, collective_id):
+    arrays, results, scratch = tiles(
+        lambda step: jnp.where(step == 0, 0, jnp.maximum(step - len(in_weights), 0))
+    )
+    rows, columns = grads.shape
+    own_rows = rows // (Z * X)
+    inner = in_weights[0].shape[0]
+    width = in_weights[0].shape[1]
+    half = width // X
+    matrices = len(in_weights)
+    parts = rows // STRIP
+    part_like = jax.ShapeDtypeStruct((own_rows, inner), F32)
+    swapped = [jax.ShapeDtypeStruct((own_rows, columns), F32), group]
+
+    def body(refs, step):
+        place = lax.axis_index("seq")
+        x = place % X
+        peer = pl.multiple_of((place + 1 - 2 * x) * own_rows, own_rows)
+        other_ref, *swap_scratch = refs.swap
+        part_ref, *scatter_scratch = refs.scatter
+        weight_buf, weight_sem = refs.weights
+        swap = SwapX(
+            [refs.grads.at[pl.ds(peer, own_rows), :], refs.group],
+            [other_ref, refs.other_group],
+            swap_scratch,
+        )
+        blocks_here = SwapBlocks(
+            [refs[f"block_{index}"] for index in range(len(blocks))],
+            [refs[f"swapped_{index}"] for index in range(len(blocks))],
+            refs.blocks,
+        )
+        scatter = Scatter([part_ref], [refs.share], scatter_scratch)
+        sums = SumAll([refs.first_part], [refs.first_sum], refs.sums)
+
+        def fetch(index):
+            return block_fetch(refs[f"weight_{index}"], weight_buf, weight_sem, index % 2)
+
+        @pl.when(step == 0)
+        def _():
+            swap.begin()
+            sums.begin()
+            part_ref[...] = jnp.zeros_like(part_ref)
+
+        def pause(part):
+            now = step * parts + part
+            schedule(now, (0, 1, 2), sums.events())
+            schedule(now, (4 * matrices + 4, 4 * matrices + 7), scatter.events())
+
+        @pl.when((step == 0) | (step > matrices))
+        def _():
+            tile_strips(refs, step, 0, pause)
+
+        for index in range(matrices):
+
+            @pl.when(step == index)
+            def _(index=index):
+                fetch(index).start()
+
+            @pl.when(step == index + 1)
+            def _(index=index):
+                if index == 0:
+                    swap.finish()
+                    blocks_here.begin()
+                fetch(index).wait()
+                weight = halves(weight_buf[index % 2])
+                own = refs.own_grads[:, index * half : (index + 1) * half]
+                other = other_ref[:, index * half : (index + 1) * half]
+                low_x, high_x = (jnp.where(x == place_x, own, other) for place_x in range(X))
+                part_ref[...] += few_rows(halves(jnp.concatenate([low_x, high_x], 1)), weight, 1)
+                if index == matrices - 1:
+                    scatter.begin()
+
+        pl.when(step == matrices + count - 1)(blocks_here.finish)
+
+    return fused(
+        dict(
+            grads=(grads, ANY),
+            own_grads=(
+                grads, pl.BlockSpec((own_rows, columns), lambda step: (lax.axis_index("seq"), 0))
+            ),
+            group=(group, ANY),
+            first_part=(first_part, WHOLE),
+            **{f"block_{index}": (block, ANY) for index, block in enumerate(blocks)},
+            **{f"weight_{index}": (weight, ANY) for index, weight in enumerate(in_weights)},
+            **arrays,
+        ),
+        dict(
+            other_group=(group.shape, ANY),
+            share=Scatter.results([part_like])[0],
+            first_sum=SumAll.results([first_part])[0],
+            **{
+                f"swapped_{index}": result for index, result in enumerate(SwapBlocks.results(blocks))
+            },
+            **results,
+        ),
+        dict(
+            swap=[pltpu.VMEM((own_rows, columns), F32), *SwapX.scratch(swapped)],
+            scatter=[pltpu.VMEM((own_rows, inner), F32), *Scatter.scratch([part_like])],
+            blocks=SwapBlocks.scratch(blocks),
+            sums=SumAll.scratch([first_part]),
+            weights=[pltpu.VMEM((2, inner, width), F32), pltpu.SemaphoreType.DMA((2,))],
+            **scratch,
+        ),
+        count + matrices,
+        body,
+        collective_id,
+    )
+
+
+def thin(left, right, contract_left, contract_right):
+    (left_high, left_low), (right_high, right_low) = left, right
+    return product(
+        jnp.concatenate([left_high, left_low], contract_left),
+        jnp.concatenate([right_high, right_high], contract_right),
+        contract_left,
+        contract_right,
+    ) + product(left_high, right_low, contract_left, contract_right)
+
+
+def join(first, second, axis):
+    return tuple(jnp.concatenate(pair, axis) for pair in zip(first, second, strict=True))
+
+
+def running_sum(triangle, entries):
+    high, low = halves(entries)
+    least = (entries - high.astype(F32) - low.astype(F32)).astype(BF16)
+    return product(
+        jnp.concatenate([triangle, triangle], 1), jnp.concatenate([high, low], 0), 1, 0
+    ) + product(triangle, least, 1, 0)
+
+
+def chunk_masks(lengths_ref, chunk):
+    shape = (CHUNK, CHUNK)
+    row = lax.broadcasted_iota(jnp.int32, shape, 0)
+    column = lax.broadcasted_iota(jnp.int32, shape, 1)
+    start = chunk * CHUNK
+
+    offsets = [0]
+    for index in range(lengths_ref.shape[0] - 1):
+        offsets.append(offsets[-1] + lengths_ref[index])
+
+    def segment(position):
+        return sum(jnp.where(position >= offset, 1, 0) for offset in offsets)
+
+    segment_row = segment(start + row)
+    before, last = segment(start - 1), segment(start + CHUNK - 1)
+    allowed = (row >= column) & (segment_row == segment(start + column))
+    carry = (segment_row == before).astype(F32)
+    in_last = (segment_row == last).astype(F32)
+    lower = (row >= column).astype(F32).astype(BF16)
+    return allowed, carry, in_last, (last == before).astype(F32), lower
+
+
+def head_terms(pre_query, pre_forget, lower_bound, lower):
+    query_gate = jax.nn.sigmoid(pre_query)
+    forget_gate = jax.nn.sigmoid(-pre_forget)
+    keys = (1.0 - lower_bound) * forget_gate
+    log_decay = running_sum(lower, jnp.log1p(-keys))
+    last = log_decay[CHUNK - 1 :, :]
+    growth, shrink, trail = jnp.exp(log_decay), jnp.exp(-log_decay), jnp.exp(last - log_decay)
+    return query_gate, forget_gate, keys, last, growth, shrink, trail
+
+
+def tall(row):
+    return jnp.transpose(jnp.broadcast_to(row, (HDIM, HDIM)))
+
+
+def forward_chunk(
+    chunk, lengths_ref, projected_ref, bound_ref, gain_ref, mixer_ref, raw_ref, states_ref, state_ref
+):
+    heads = state_ref.shape[0]
+    width = heads * HDIM
+    allowed, carry, in_last, carry_last, lower = chunk_masks(lengths_ref, chunk)
+    for head in range(heads):
+        at = slice(head * HDIM, (head + 1) * HDIM)
+        pre_query, pre_forget, values, gate_in = (
+            projected_ref[:, part * width + head * HDIM : part * width + (head + 1) * HDIM]
+            for part in range(4)
+        )
+        query_gate, _, keys, last, growth, shrink, trail = head_terms(
+            pre_query, pre_forget, bound_ref[:, at], lower
+        )
+        grown = pre_query * query_gate * growth
+        state = state_ref[head]
+        states_ref[0, head] = state
+        value_halves = halves(values)
+        scores = thin(halves(grown), halves(keys * shrink), 1, 1)
+        scores = jnp.where(allowed, scores, 0.0)
+        raw = three_pass(
+            join(halves(scores), halves(grown * carry), 1),
+            join(value_halves, halves(state), 0),
+            1,
+            0,
+        )
+        state_ref[head] = state * (tall(jnp.exp(last)) * carry_last) + thin(
+            halves(keys * trail * in_last), value_halves, 0, 0
+        )
+        raw_ref[:, at] = raw
+        scale = lax.rsqrt(jnp.mean(raw * raw, -1, keepdims=True) + group_eps)
+        mixer_ref[:, at] = raw * scale * gain_ref[:, at] * jax.nn.silu(gate_in)
+
+
+def backward_kernel(
+    projected, raw_rows, states, grad_mixer, normed_cols, grad_residual, second, weights,
+    lower_bound, group_gain, lengths, collective_id,
+):
+    rows, columns = projected.shape
+    count = len(weights)
+    width = columns // count
+    heads = width // HDIM
+    chunks = rows // CHUNK
+    wide = normed_cols.shape[1]
+
+    def body(refs, step):
+        lengths_ref, projected_ref, raw_ref, states_ref = refs.lengths, refs.projected, refs.raw, refs.states
+        grad_ref, grads_ref, group_ref = refs.grad_mixer, refs.grads, refs.group
+        later_ref, weight_buf, weight_sem = refs.work
+        chunk = chunks - 1 - step
+        place = lax.axis_index("seq")
+        here = pl.ds(pl.multiple_of((place % X) * width, width), width)
+        bound_ref, gain_ref = refs.lower_bound.at[:, here], refs.group_gain.at[:, here]
+        block_refs = [refs[f"block_{index}"] for index in range(count)]
+        move = Columns([refs.grad_residual], [refs.residual_cols], refs.columns)
+        small = Columns([refs.second], [refs.second_cols], refs.small)
+
+        def fetch(index):
+            return block_fetch(
+                refs[f"weight_{index}"].at[
+                    pl.ds(pl.multiple_of((place // X) * wide, wide), wide), here
+                ],
+                weight_buf,
+                weight_sem,
+                index,
+            )
+
+        @pl.when(step == 0)
+        def _():
+            move.begin()
+            small.begin()
+            later_ref[...] = jnp.zeros_like(later_ref)
+            group_ref[...] = jnp.zeros_like(group_ref)
+            for index in range(count):
+                fetch(index).start()
+                block_refs[index][...] = jnp.zeros_like(block_refs[index])
+
+        allowed, carry, in_last, carry_last, lower = chunk_masks(lengths_ref, chunk)
+        upper = jnp.transpose(lower.astype(F32)).astype(BF16)
+        for head in range(heads):
+            at = slice(head * HDIM, (head + 1) * HDIM)
+            spots = [
+                slice(part * width + head * HDIM, part * width + (head + 1) * HDIM)
+                for part in range(4)
+            ]
+            pre_query, pre_forget, values, gate_in = (projected_ref[:, spot] for spot in spots)
+            raw, grad, gain = raw_ref[:, at], grad_ref[:, at], gain_ref[:, at]
+            state, later = states_ref[0, head], later_ref[head]
+
+            scale = lax.rsqrt(jnp.mean(raw * raw, -1, keepdims=True) + group_eps)
+            normed = raw * scale
+            gate = jax.nn.sigmoid(gate_in)
+            silu_gate = gate_in * gate
+            weighted = grad * gain * silu_gate
+            group_ref[:, at] += jnp.sum(grad * normed * silu_gate, 0, keepdims=True)
+            grads_ref[:, spots[3]] = (
+                grad * gain * normed * (gate * (1.0 + gate_in * (1.0 - gate)))
+            )
+            grad_raw = scale * weighted - raw * (
+                scale * scale * scale * jnp.mean(weighted * raw, -1, keepdims=True)
+            )
+
+            query_gate, forget_gate, keys, last, growth, shrink, trail = head_terms(
+                pre_query, pre_forget, bound_ref[:, at], lower
+            )
+            grown = pre_query * query_gate * growth
+            shrunk = keys * shrink
+            trailing = trail * in_last
+            ends = keys * trailing
+            grown_halves, shrunk_halves = halves(grown), halves(shrunk)
+            raw_halves, value_halves, later_halves = halves(grad_raw), halves(values), halves(later)
+            scores = jnp.where(allowed, thin(grown_halves, shrunk_halves, 1, 1), 0.0)
+            grad_scores = jnp.where(allowed, thin(raw_halves, value_halves, 1, 1), 0.0)
+            score_halves = halves(grad_scores)
+            grads_ref[:, spots[2]] = three_pass(
+                join(halves(jnp.transpose(scores)), halves(ends), 1),
+                join(raw_halves, later_halves, 0),
+                1,
+                0,
+            )
+            grad_grown = three_pass(
+                join(score_halves, halves(grad_raw * carry), 1),
+                join(shrunk_halves, halves(jnp.transpose(state)), 0),
+                1,
+                0,
+            )
+            grad_shrunk = thin(score_halves, grown_halves, 0, 0)
+            grad_ends = thin(value_halves, later_halves, 1, 1)
+            through = tall(jnp.exp(last)) * carry_last
+            later_ref[head] = later * through + thin(
+                halves(grown * carry), raw_halves, 0, 0
+            )
+            grads_ref[:, spots[0]] = (
+                grad_grown * growth * (query_gate * (1.0 + pre_query * (1.0 - query_gate)))
+            )
+            from_ends = grad_ends * ends
+            grad_log = grad_grown * grown - grad_shrunk * shrunk - from_ends
+            pulled = jnp.transpose(later * state * through)
+            grad_last = jnp.sum(from_ends + pulled, 0, keepdims=True)
+            grad_log_forget = running_sum(upper, grad_log) + grad_last
+            grad_keys = (
+                grad_shrunk * shrink + grad_ends * trailing - grad_log_forget / (1.0 - keys)
+            )
+            grads_ref[:, spots[1]] = -grad_keys * keys * (1.0 - forget_gate)
+
+        cols = halves(jnp.transpose(refs.normed_cols[...]))
+        for index in range(count):
+            part = grads_ref[:, index * width : (index + 1) * width]
+            block_refs[index][...] += thin(cols, halves(part), 1, 0)
+
+        @pl.when(step == chunks - 1)
+        def _():
+            total = 0.0
+            for index in range(count):
+                fetch(index).wait()
+                total = total + weight_buf[index] * block_refs[index][...]
+            ones = jnp.ones((8, width), BF16)
+            high, low = halves(total)
+            refs.sums[...] = product(ones, high, 1, 1) + product(ones, low, 1, 1)
+
+        schedule(step, (0, 2, 4, 6, 7, 7), move.events())
+        schedule(step, (0, 2, 4, 6, 7, 7), small.events())
+
+    def by_chunk(size):
+        return pl.BlockSpec((CHUNK, size), lambda step: (chunks - 1 - step, 0))
+
+    return fused(
+        dict(
+            lengths=(lengths, pl.BlockSpec(memory_space=pltpu.SMEM)),
+            projected=(projected, by_chunk(columns)),
+            raw=(raw_rows, by_chunk(width)),
+            states=(
+                states,
+                pl.BlockSpec((1, heads, HDIM, HDIM), lambda step: (chunks - 1 - step, 0, 0, 0)),
+            ),
+            grad_mixer=(grad_mixer, by_chunk(width)),
+            normed_cols=(normed_cols, by_chunk(wide)),
+            lower_bound=(lower_bound[None], WHOLE),
+            group_gain=(group_gain[None], WHOLE),
+            grad_residual=(grad_residual, ANY),
+            second=(second, ANY),
+            **{f"weight_{index}": (weight, ANY) for index, weight in enumerate(weights)},
+        ),
+        dict(
+            grads=((rows, columns), by_chunk(columns)),
+            group=((1, width), WHOLE),
+            sums=((8, wide), WHOLE),
+            residual_cols=Columns.results([grad_residual])[0],
+            second_cols=Columns.results([second])[0],
+            **{f"block_{index}": ((wide, width), WHOLE) for index in range(count)},
+        ),
+        dict(
+            work=[
+                pltpu.VMEM((heads, HDIM, HDIM), F32),
+                pltpu.VMEM((count, wide, width), F32),
+                pltpu.SemaphoreType.DMA((count,)),
+            ],
+            columns=Columns.scratch([grad_residual]),
+            small=Columns.scratch([second]),
+        ),
+        chunks,
+        body,
+        collective_id,
+        far=True,
+        flops=60 * rows * HDIM * width + 6 * rows * wide * columns,
+    )
+
+
+def fast_shards(
+    tokens_in,
+    cotangent,
+    lengths,
+    lower_bound,
+    query_weight,
+    forget_weight,
+    input_weight,
+    gate_weight,
+    out_weight,
+    swiglu_gate,
+    swiglu_up,
+    swiglu_down,
+    first_gain,
+    group_gain,
+    second_gain,
+):
+    place = lax.axis_index("seq")
+    z, x = place // X, place % X
+    rows, model = tokens_in.shape
+    wide = model // Z
+    narrow = model // (Z * X)
+    width = query_weight.shape[1] // X
+    share_rows = rows // 4
+    token_count = rows * Z * X
+
+    def share(entries):
+        return cut(entries, lax.axis_index("mp"), share_rows, 0)
+
+    in_weights = (query_weight, forget_weight, input_weight, gate_weight)
+    all_tokens = gather_tokens_fast(tokens_in, 1)
+    mixed = mixer_kernel(
+        all_tokens,
+        tokens_in,
+        cotangent,
+        lengths,
+        lower_bound,
+        in_weights,
+        out_weight,
+        swiglu_down,
+        first_gain,
+        group_gain,
+        second_gain,
+        2,
+    )
+    fed = feed_forward_kernel(
+        mixed.normed_two,
+        mixed.residual,
+        cotangent,
+        mixed.grad_hidden,
+        swiglu_gate,
+        swiglu_up,
+        swiglu_down,
+        out_weight,
+        second_gain,
+        3,
+    )
+    grad_residual = fed.grad_residual
+
+    def tiles(first, count):
+        return partial(
+            tile_parts,
+            fed.all_normed_two,
+            mixed.all_cotangent,
+            mixed.grad_hidden,
+            swiglu_gate,
+            swiglu_up,
+            first,
+            count,
+        )
+
+    split = 3
+    left = pl.cdiv(swiglu_gate.shape[1], TILE) - split
+    sent = heads_kernel(fed.grad_mixer, fed.ffn, tiles(0, split), split, 4)
+    output = share(mixed.residual) + sent.ffn_share
+    back = backward_kernel(
+        mixed.projected,
+        mixed.raw,
+        mixed.states,
+        sent.all_grad_mixer,
+        mixed.normed_cols,
+        grad_residual,
+        fed.second,
+        in_weights,
+        lower_bound,
+        group_gain,
+        lengths,
+        5,
+    )
+    second_cols = jnp.sum(back.second_cols[:, :, 0], (0, 1))
+    out_block = dot(back.residual_cols.reshape(token_count, wide), mixed.mixer, 0, 0)
+    last = last_kernel(
+        back.grads,
+        jnp.broadcast_to(back.group, (8, width)),
+        [*(back[f"block_{index}"] for index in range(4)), out_block],
+        jnp.concatenate([back.sums[:, :narrow], back.sums[:, narrow:]]),
+        in_weights,
+        tiles(split, left),
+        left,
+        6,
+    )
+    grad_group = in_order(x == 0, back.group[0], last.other_group[0], 0)
+    *weight_grads, grad_outw = (
+        jnp.concatenate([last[f"swapped_{index}"][0], last[f"swapped_{index}"][1]], 1)
+        for index in range(5)
+    )
+    grad_normed_one, first_sum = last.share, last.first_sum
+    grad_sgate, grad_sup, grad_sdown = (
+        jnp.concatenate([sent[name], last[name]], axis)
+        for name, axis in (("grad_gate", 1), ("grad_up", 1), ("grad_down", 0))
+    )
+    tokens_share = share(tokens_in)
+    scale_one = rms(tokens_share)
+    pulled_one = grad_normed_one * first_gain
+    grad_tokens = (
+        share(grad_residual)
+        + scale_one * pulled_one
+        - tokens_share * scale_one**3 * jnp.mean(pulled_one * tokens_share, -1, keepdims=True)
+    )
+    return (
+        output,
+        grad_tokens,
+        *weight_grads,
+        jnp.transpose(grad_outw),
+        grad_sgate,
+        grad_sup,
+        grad_sdown,
+        first_sum[0] / cut(first_gain, place, narrow, 0),
+        cut(grad_group, place, group_gain.shape[0] // (Z * X), 0),
+        cut(second_cols, x, narrow, 0),
+    )
+
+
 def solution(mesh):
     in_specs = (
         P("seq", None),
@@ -269,4 +2005,6 @@
         P(("mp", "seq")),
         P("seq"),
     )
-    return jax.shard_map(shards, mesh=mesh, in_specs=in_specs, out_specs=out_specs, check_vma=False)
+    small = (mesh.shape["seq"], mesh.shape["mp"]) == (Z * X, 4)
+    body = fast_shards if small else shards
+    return jax.shard_map(body, mesh=mesh, in_specs=in_specs, out_specs=out_specs, check_vma=False)

time: 743 us -> 392 us (0.53)
  waiting for transfers between devices: 368 us -> 0 us
  Pallas kernels: 0 us -> 367 us
  matrix products: 259 us -> 4.21 us
  local copies, waits for them, and re-layouts: 47.7 us -> 4.63 us
  other arithmetic: 31.1 us -> 11.9 us
  between operations: 15.6 us -> 1.07 us
    pallas_call x0 -> x6, Pallas kernels: none -> 367 us  [fused(): pl.pallas_call(kernel, grid=(steps,), out_shape=[jax.ShapeDtypeStruct(sha...]
    all_gather x4 -> x0, waiting for transfers between devices: 296 us -> none  [gather_tokens(): return lax.all_gather(block, 'seq', axis=0, tiled=True)]
    dot_general x26 -> x1, matrix products: 227 us -> 4.21 us  [dot(): lax.dot_general(left, right, (((contract_left,), (contract_right,)), ((),...]
    psum x2 -> x0, waiting for transfers between devices: 49.1 us -> none  [the longest x1 36.5 us: shards(): lax.psum(dot(grad_a, swiglu_gate, 1, 1) + dot(grad_b, swiglu_up, 1, 1), '...]
    dot_general x14 -> x0, matrix products: 32.2 us -> none  [the longest x2 7.59 us: recurrence(): jnp.einsum('ts,cshk->cthk', lower, jnp.log1p(-keys), precision=HIGHEST)]
    all_to_all x1 -> x0, waiting for transfers between devices: 20.2 us -> none  [shards(): residual_cols = lax.all_to_all(grad_residual, 'seq', 1, 0, tiled=True)]
    unnamed x172 -> x35, local copies, waits for them, and re-layouts: 20.4 us -> 1.08 us
    reshape x5 -> x0, local copies, waits for them, and re-layouts: 13.4 us -> none  [the longest x3 7.21 us: split(): return entries.reshape(chunks, CHUNK, heads, HDIM)]
  transfers between devices with their start and end apart: 9 -> 0, of which waited for: 7 -> 0; matrix products, arithmetic and copies ran while one was open for 27% -> 0% of each run, Pallas kernels for 0% -> 0%
where the time goes in v4:
time: 392 us; the launch traced here: 388 us
  Pallas kernels  367 us (94%)
  other arithmetic  11.9 us (3%)
  local copies, waits for them, and re-layouts  4.63 us (1%)
  matrix products  4.21 us (1%)
    pallas_call x6, Pallas kernels, fused(): pl.pallas_call(kernel, grid=(steps,), out_shape=[jax.ShapeDtypeStruct(sha...  367 us

profile of v4, /device:TPU:8, one launch (start us, length us, event | category | flops | bytes accessed | tf_op | source)
XLA Modules:
  0.0 388.4 jit_solution(8375450807116353456)
XLA Ops:
  0.6 40.5 %shard_map.246.refs_1_ = f32[1024,2048]{1,0:T(8,128)} custom-call(f32[128,2048]{1,0:T(8,128)} %refs_2_.2), custom_call_target="tpu_custom_call" | custom-call | bytes 33554432 | tf_op jit(solution)/shard_map/pallas_call | solution.py:960
  41.1 98.4 %shard_map.247 = (f32[1024,2048]{1,0:T(8,128)}, f32[1024,1024]{1,0:T(8,128)}, f32[1024,512]{1,0:T(8,128)}, f32[1024,256]{1,0:T(8,128)}, f32[1024,256]{1,0:T(8,12...) custom-call(s32[4]{0:T(128)} %refs_0_.5, ...), custom_call_target="tpu_custom_call" | custom-call | flops 30601641984 | bytes 33554432 | tf_op jit(solution)/shard_map/pallas_call | solution.py:960
  139.6 73.4 %shard_map.248 = (f32[1024,2048]{1,0:T(8,128)}, f32[128,2048]{1,0:T(8,128)}, f32[128,2048]{1,0:T(8,128)}, f32[128,512]{1,0:T(8,128)}, f32[8,2048]{1,0:T(8,128)}) custom-call(f32[128,2048]{1,0:T(8,128)} %get-tuple-element.53.refs_0_, f32[128,2048]{1,0:T(8,128)} %get-tuple-element.52.refs_1_, f32[128,2048]{1,0:T(8,128)} %refs_2_.3, ...), custom_call_target="tpu_custom_call" | custom-call | flops 11072962560 | bytes 33554432 | tf_op jit(solution)/shard_map/pallas_call | solution.py:960
  213.0 49.4 %shard_map.249 = (f32[1024,256]{1,0:T(8,128)}, f32[32,2048]{1,0:T(8,128)}, f32[256,768]{1,0:T(8,128)}, f32[256,768]{1,0:T(8,128)}, f32[768,256]{1,0:T(8,128)}) custom-call(f32[128,512]{1,0:T(8,128)} %get-tuple-element.55.refs_0_, f32[128,2048]{1,0:T(8,128)} %get-tuple-element.56.refs_1_, f32[1024,2048]{1,0:T(8,128)} %get-tuple-element.57.refs_2_.refs_6_.refs_13_.refs_17_, ...), custom_call_target="tpu_custom_call" | custom-call | bytes 33554432 | tf_op jit(solution)/shard_map/pallas_call | solution.py:960
  262.4 0.0 copy-start.1
  262.4 34.7 %shard_map.250 = (f32[1024,1024]{1,0:T(8,128)}, f32[1,256]{1,0:T(1,128)}, f32[8,512]{1,0:T(8,128)}, f32[4,2,128,512]{3,2,1,0:T(8,128)}, f32[4,2,8,512]{3,2,1,0:T...) custom-call(s32[4]{0:T(128)} %refs_0_.5, ...), custom_call_target="tpu_custom_call" | custom-call | flops 5234491392 | bytes 33554432 | tf_op jit(solution)/shard_map/pallas_call | solution.py:960
  297.1 0.0 copy-start.15
  297.1 0.0 copy-start.16
  297.1 0.0 copy-done.1
  297.1 4.2 %fusion.1.refs_8_ = f32[512,256]{1,0:T(8,128)} fusion(f32[1024,512]{1,0:T(8,128)} %bitcast.32, f32[1024,256]{1,0:T(8,128)S(1)} %copy-done.1), kind=kOutput, calls=%fused_computation.30 | convolution fusion | flops 805306368 | bytes 3670016 | tf_op jit(solution)/shard_map/dot_general | solution.py:19
  301.4 0.0 copy-done.15
  301.4 0.6 pad_maximum_fusion.7.refs_3_
  302.0 0.0 copy-done.16
  302.0 0.6 broadcast_in_dim.30.refs_2_
  302.6 0.0 copy-start.3
  302.6 70.2 %shard_map.251 = (f32[8,256]{1,0:T(8,128)}, f32[32,2048]{1,0:T(8,128)}, f32[8,256]{1,0:T(8,128)}, f32[2,256,256]{2,1,0:T(8,128)}, f32[2,256,256]{2,1,0:T(8,128)}...) custom-call(f32[1024,1024]{1,0:T(8,128)} %get-tuple-element.67.refs_, ...), custom_call_target="tpu_custom_call" | custom-call | bytes 33554432 | tf_op jit(solution)/shard_map/pallas_call | solution.py:960
  372.8 0.0 copy-start.4
  372.8 0.0 copy-start.5
  372.8 0.0 copy-start.6
  372.8 0.8 slice.58
  373.7 0.0 copy-start.7
  373.7 0.6 dynamic_slice.22
  374.2 0.0 copy-done.3
  374.2 2.3 pad_maximum_fusion.2
  376.5 0.0 copy-done.4
  376.5 0.0 copy-done.5
  376.5 0.0 copy-done.6
  376.5 0.0 copy-done.7
  376.5 0.0 copy-start.11
  376.6 0.0 copy-start.12
  376.6 1.8 pad_maximum_fusion
  378.4 0.0 copy-done.11
  378.4 0.0 copy-done.12
  378.4 0.1 slice_bitcast_fusion.1
  378.5 0.0 copy-start.9
  378.5 0.0 copy-start.10
  378.5 0.1 maximum_bitcast_fusion
  378.6 1.0 copy.28
  379.6 0.9 pad_maximum_fusion.6
  380.4 0.0 copy-done.9
  380.4 0.0 copy-done.10
  380.5 0.0 copy-start.8
  380.5 0.1 slice_bitcast_fusion.5
  380.5 0.0 copy-start
  380.5 0.0 copy-start.2
  380.6 0.0 copy-start.14
  380.6 0.9 pad_maximum_fusion.5
  381.4 0.0 copy-start.13
  381.4 0.9 pad_maximum_fusion.4
  382.3 0.0 copy-done.8
  382.3 0.9 pad_maximum_fusion.3
  383.2 0.0 copy-done
  383.2 0.0 copy-done.2
  383.2 0.0 copy-done.14
  383.2 0.2 multiply_reduce_fusion.1
  383.4 0.0 copy-done.13
  383.4 1.9 multiply_subtract_fusion
  385.3 0.7 slice.57
  386.0 0.6 dynamic-slice_divide_fusion
  386.6 0.9 slice_reduce_fusion
  387.5 0.6 dynamic_slice.23
  (5 shorter events, 0.1 us)
Async XLA Ops:
  262.4 34.7 %copy-start.1 = (f32[1024,256]{1,0:T(8,128)S(1)}, f32[1024,256]{1,0:T(8,128)}, u32[]{:S(2)}) copy-start(f32[1024,256]{1,0:T(8,128)} %get-tuple-element.75) | copy-start | bytes 3145732
  297.1 4.2 %copy-start.15 = (f32[8,512]{1,0:T(8,128)S(1)}, f32[8,512]{1,0:T(8,128)}, u32[]{:S(2)}) copy-start(f32[8,512]{1,0:T(8,128)} %get-tuple-element.69) | copy-start | bytes 49156
  297.1 4.8 %copy-start.16 = (f32[1,256]{1,0:T(1,128)S(1)}, f32[1,256]{1,0:T(1,128)}, u32[]{:S(2)}) copy-start(f32[1,256]{1,0:T(1,128)} %get-tuple-element.68) | copy-start | bytes 3076
  302.6 71.7 %copy-start.3 = (f32[768,256]{1,0:T(8,128)S(1)}, f32[768,256]{1,0:T(8,128)}, u32[]{:S(2)}) copy-start(f32[768,256]{1,0:T(8,128)} %get-tuple-element.86) | copy-start | bytes 2359300
  372.8 3.8 copy-start.4
  372.8 3.8 copy-start.5
  372.8 3.7 copy-start.6
  373.7 2.9 copy-start.7
  376.5 1.9 copy-start.11
  376.6 1.9 copy-start.12
  378.5 2.0 copy-start.9
  378.5 1.9 copy-start.10
  380.5 1.8 copy-start.8
  380.5 2.7 copy-start
  380.5 2.7 copy-start.2
  380.6 2.6 copy-start.14
  381.4 2.0 copy-start.13

commit v5 on v4

--- a/solution.py
+++ b/solution.py
@@ -368,6 +368,7 @@
 
 class Gather(Move):
     PIECES = 2
+    OWN = 5
 
     def in_specs(arrays):
         return [ANY]
@@ -389,10 +390,16 @@
         return pl.ds(pl.multiple_of(first * self.tile, self.tile), count * self.tile)
 
     def columns(self, y, core):
-        return self.cols(6 * y + 5 * core, 5)
+        return self.cols((16 - 2 * self.OWN) * y + self.OWN * core, self.OWN)
+
+    def y_count(self, big):
+        most = min(16 - 2 * self.OWN, self.OWN)
+        return most if big else 16 - 2 * self.OWN - most
 
     def y_columns(self, y, big):
-        return self.cols(11 * y, 5) if big else self.cols(5 + 5 * y, 1)
+        count = self.y_count(big)
+        first = (16 - count) * y if big else self.OWN * (1 - y) + 2 * self.OWN * y
+        return self.cols(first, count)
 
     def region(self, z, x, piece, columns):
         row = (z * X + x) * self.rows + piece * self.size
@@ -460,8 +467,10 @@
         return remote(region, region, self.sems, index, self.core_peer())
 
     def sized(self, big, action):
-        pl.when(big)(lambda: action(True))
-        pl.when(jnp.logical_not(big))(lambda: action(False))
+        if self.y_count(True):
+            pl.when(big)(lambda: action(True))
+        if self.y_count(False):
+            pl.when(jnp.logical_not(big))(lambda: action(False))
 
     def pass_on(self, way, step, other_x, piece):
         self.sized(
@@ -532,12 +541,15 @@
                         self.inside(way, step, other_x, piece, False).wait_send()
                         self.inside(way, step, other_x, piece, True).wait_recv()
 
-                        def sized(big, other_x=other_x):
+                        def sent(big, other_x=other_x):
                             self.over_y(way, step, other_x, piece, False, big).wait_send()
-                            self.inside_y(way, step, other_x, piece, not big).wait_send()
                             self.inside_y(way, step, other_x, piece, big).wait_recv()
 
-                        self.sized(self.core == self.y, sized)
+                        def handed(big, other_x=other_x):
+                            self.inside_y(way, step, other_x, piece, big).wait_send()
+
+                        self.sized(self.core == self.y, sent)
+                        self.sized(self.core != self.y, handed)
 
                 self.each(step, action)
 
@@ -558,6 +570,10 @@
             return event
 
         return [round_of(index) for index in range(2 * (Z + 1))] + [self.finish]
+
+
+class Gather12(Gather):
+    OWN = 6
 
 
 class Sum(Move):
@@ -960,9 +976,12 @@
     outputs = pl.pallas_call(
         kernel,
         grid=(steps,),
-        out_shape=[jax.ShapeDtypeStruct(shape, F32) for shape, _ in results.values()],
+        out_shape=[
+            jax.ShapeDtypeStruct(result[0], result[2] if len(result) > 2 else F32)
+            for result in results.values()
+        ],
         in_specs=[spec for _, spec in arrays.values()],
-        out_specs=[spec for _, spec in results.values()],
+        out_specs=[result[1] for result in results.values()],
         scratch_shapes=[one for needed in scratch.values() for one in needed],
         compiler_params=pltpu.CompilerParams(
             has_side_effects=True,
@@ -984,21 +1003,71 @@
         pl.when(now == moment)(event)
 
 
-def gather_tokens_fast(block, collective_id):
+SPLIT_ROWS = 128
+
+
+def first_kernel(block, out_weight, w_gate, w_up, w_down, collective_id):
+    inner, columns = w_gate.shape
+    padded = pl.cdiv(columns, TILE) * TILE
+    steps = inner // SPLIT_ROWS
+    down_steps = padded // SPLIT_ROWS
+    out_rows = out_weight.shape[0] // steps
+
     def body(refs, step):
-        move = Gather([refs.block], [refs.all], refs.move)
-        move.begin()
-        for event in move.events():
-            event()
-
+        gather = Gather12([refs.block], [refs.all], refs.gather)
+        pl.when(step == 0)(gather.begin)
+
+        def store(name, entries, spot):
+            refs[f"{name}_high"][:, spot], refs[f"{name}_low"][:, spot] = halves(entries)
+
+        whole = slice(None)
+        store("out", refs.out[...], whole)
+        for name in ("gate", "up"):
+            store(name, refs[name][...], slice(0, columns))
+            for half in ("high", "low"):
+                refs[f"{name}_{half}"][:, columns:] = jnp.zeros(
+                    (SPLIT_ROWS, padded - columns), BF16
+                )
+        row = jnp.minimum(step, down_steps - 1) * SPLIT_ROWS + lax.broadcasted_iota(
+            jnp.int32, (SPLIT_ROWS, inner), 0
+        )
+        down = jnp.where(row < columns, refs.down[...], 0.0)
+        store("down", down, whole)
+        store("turned", jnp.transpose(down), whole)
+        schedule(step, (2, 3, 5, 6, 8, 10, 11, 13, 14, 15, 15), gather.events())
+
+    def by_rows(rows, columns, last=steps - 1):
+        return pl.BlockSpec((rows, columns), lambda step: (jnp.minimum(step, last), 0))
+
+    results = dict(all=Gather.results([block])[0])
+    for half in ("high", "low"):
+        for name in ("gate", "up"):
+            results[f"{name}_{half}"] = ((inner, padded), by_rows(SPLIT_ROWS, padded), BF16)
+        results[f"out_{half}"] = (out_weight.shape, by_rows(out_rows, inner), BF16)
+        results[f"down_{half}"] = (
+            (padded, inner), by_rows(SPLIT_ROWS, inner, down_steps - 1), BF16
+        )
+        results[f"turned_{half}"] = (
+            (inner, padded),
+            pl.BlockSpec(
+                (inner, SPLIT_ROWS), lambda step: (0, jnp.minimum(step, down_steps - 1))
+            ),
+            BF16,
+        )
     return fused(
-        dict(block=(block, ANY)),
-        dict(all=Gather.results([block])[0]),
-        dict(move=Gather.scratch([block])),
-        1,
+        dict(
+            block=(block, ANY),
+            gate=(w_gate, by_rows(SPLIT_ROWS, columns)),
+            up=(w_up, by_rows(SPLIT_ROWS, columns)),
+            down=(w_down, by_rows(SPLIT_ROWS, inner, pl.cdiv(columns, SPLIT_ROWS) - 1)),
+            out=(out_weight, by_rows(out_rows, inner)),
+        ),
+        results,
+        dict(gather=Gather.scratch([block])),
+        steps,
         body,
         collective_id,
-    ).all
+    )
 
 
 def halves_scratch(rows, inner):
@@ -1010,7 +1079,7 @@
     ]
 
 
-def load_halves(src_ref, high_ref, low_ref, stage_ref, sem, change=None):
+def load_halves(src_ref, high_ref, low_ref, stage_ref, sem, change=None, start=True, split=True):
     count, rows, _ = stage_ref.shape
 
     def spot(index):
@@ -1021,10 +1090,7 @@
             src_ref.at[spot(index), :], stage_ref.at[index], sem.at[index]
         )
 
-    for index in range(count):
-        fetch(index).start()
-
-    def split(index, carried):
+    def one(index, carried):
         fetch(index).wait()
         if change is not None:
             change(index)
@@ -1033,10 +1099,14 @@
         low_ref[spot(index), :] = low
         return carried
 
-    lax.fori_loop(0, count, split, 0)
-
-
-STRIP = 256
+    if start:
+        for index in range(count):
+            fetch(index).start()
+    if split:
+        lax.fori_loop(0, count, one, 0)
+
+
+STRIP = 512
 
 
 def strips(rows, action):
@@ -1051,18 +1121,21 @@
     return pltpu.make_async_copy(src, buf.at[index], sem.at[index])
 
 
+EARLY = 3
+
+
 def mixer_kernel(
-    all_tokens, tokens_in, cotangent, lengths, lower_bound, in_weights, out_weight, w_down,
-    first_gain, group_gain, second_gain, collective_id,
+    all_tokens, tokens_in, cotangent, lengths, lower_bound, in_weights, split, first_gain, group_gain,
+    second_gain, collective_id,
 ):
     rows, inner = all_tokens.shape
     own_rows = tokens_in.shape[0]
-    count = len(in_weights)
+    count = 4
     wide = inner // Z
     heads = TILE // HDIM
     chunks = rows // CHUNK
-    columns = w_down.shape[0]
-    tiles = pl.cdiv(columns, TILE)
+    tiles = EARLY
+    columns = tiles * TILE
     parts = rows // STRIP
     middle = count + chunks
     steps = middle + 1 + tiles
@@ -1077,29 +1150,43 @@
         part_ref, sum_ref, *sum_scratch = refs.sum
         total = Sum([part_ref], [sum_ref], sum_scratch)
         high_ref, low_ref, stage_ref, stage_sem = refs.halves
-        weight_buf, weight_sem, out_buf, out_sem, down_buf, down_sem = refs.weights
+        weight_buf, weight_sem, down_buf, down_sem, out_buf, out_sem, ready_ref = refs.weights
         (state_ref,) = refs.state
         other_ref, send, recv = refs.swap
-        weight_refs = [refs[f"weight_{index}"] for index in range(count)]
         now = step * parts
 
         def fetch(index):
-            return block_fetch(weight_refs[index].at[:, here], weight_buf, weight_sem, index % 2)
+            return [
+                pltpu.make_async_copy(
+                    refs[f"weight_{index}"].at[:, here],
+                    weight_buf.at[index % 2],
+                    weight_sem.at[index % 2],
+                )
+            ]
+
+        def fetch_down(tile):
+            slot = lax.rem(tile, 2)
+            spot = pl.ds(pl.multiple_of(tile * TILE, TILE), TILE)
+            return [
+                pltpu.make_async_copy(
+                    refs[f"turned_{half}"].at[:, spot], down_buf.at[slot, at], down_sem.at[slot, at]
+                )
+                for at, half in enumerate(("high", "low"))
+            ]
+
+        def start(copies):
+            for copy in copies:
+                copy.start()
+
+        def wait(copies):
+            for copy in copies:
+                copy.wait()
 
         def fetch_out():
-            return pltpu.make_async_copy(refs.out_weight, out_buf, out_sem.at[0])
-
-        def fetch_down(tile, size=TILE):
-            return pltpu.make_async_copy(
-                refs.w_down.at[pl.ds(pl.multiple_of(tile * TILE, TILE), size), :],
-                down_buf.at[lax.rem(tile, 2), pl.ds(0, size), :],
-                down_sem.at[lax.rem(tile, 2)],
-            )
-
-        def sized(tile, action):
-            last = columns - (tiles - 1) * TILE
-            pl.when(tile < tiles - 1)(lambda: action(TILE))
-            pl.when(tile == tiles - 1)(lambda: action(last))
+            return [
+                pltpu.make_async_copy(refs[f"out_{half}"], out_buf.at[at], out_sem.at[at])
+                for at, half in enumerate(("high", "low"))
+            ]
 
         def swap():
             peer = pl.multiple_of((place + 1 - 2 * x) * own_rows, own_rows)
@@ -1108,8 +1195,12 @@
             )
 
         def pause(part):
-            schedule(now + part, (1, 3, 5, 7, 9, 11, 13, 15, 20, 24), gather.events()[:-1])
-            schedule(now + part, (4 * middle + 4, 4 * middle + 15, 4 * middle + 19), total.events())
+            mixing = count * parts
+            schedule(
+                now + part,
+                (0, 1, 2, 3, 5, mixing, mixing + 2 * parts, mixing + 4 * parts, mixing + 7 * parts),
+                gather.events()[:9],
+            )
 
         def normalize(index):
             entries = stage_ref[index]
@@ -1121,8 +1212,8 @@
         @pl.when(step == 0)
         def _():
             gather.begin()
-            fetch(0).start()
-            fetch_out().start()
+            start(fetch(0))
+            start(fetch_out())
             load_halves(refs.tokens, high_ref, low_ref, stage_ref, stage_sem, normalize)
             state_ref[...] = jnp.zeros_like(state_ref)
 
@@ -1131,17 +1222,20 @@
             @pl.when(step == index)
             def _(index=index):
                 if index + 1 < count:
-                    fetch(index + 1).start()
-                fetch(index).wait()
+                    start(fetch(index + 1))
+                wait(fetch(index))
 
         @pl.when(step < count)
         def _():
-            weight = halves(weight_buf[lax.rem(step, 2)])
+            ready_ref[0], ready_ref[1] = halves(weight_buf[lax.rem(step, 2)])
             target = pl.ds(pl.multiple_of(step * TILE, TILE), TILE)
 
             def strip(index, spot):
                 refs.projected[spot, target] = three_pass(
-                    (high_ref[spot, :], low_ref[spot, :]), weight, 1, 0
+                    (high_ref[spot, :], low_ref[spot, :]),
+                    (ready_ref[0], ready_ref[1]),
+                    1,
+                    0,
                 )
                 pause(index)
 
@@ -1167,35 +1261,36 @@
         @pl.when(step == middle)
         def _():
             swap().start()
-            fetch_down(0).start()
-            fetch_out().wait()
+            start(fetch_down(0))
+            wait(fetch_out())
+
+            def out_rows(spot):
+                return out_buf[0, spot, :], out_buf[1, spot, :]
+
             own = refs.mixer[pl.ds(pl.multiple_of(place * own_rows, own_rows), own_rows), :]
-            part_ref[...] = few_rows(halves(own), halves(out_buf[here, :]), 0)
+            part_ref[...] = few_rows(halves(own), out_rows(here), 0)
             swap().wait()
-            part_ref[...] += few_rows(halves(other_ref[...]), halves(out_buf[there, :]), 0)
+            part_ref[...] += few_rows(halves(other_ref[...]), out_rows(there), 0)
             total.begin()
+            total.to_y()
+            gather.events()[9]()
             gather.finish()
             load_halves(refs.all_cotangent, high_ref, low_ref, stage_ref, stage_sem)
 
         @pl.when(step > middle)
         def _():
             tile = step - middle - 1
-            pl.when(tile < tiles - 1)(
-                lambda: sized(tile + 1, lambda size: fetch_down(tile + 1, size).start())
+            pl.when(tile < tiles - 1)(lambda: start(fetch_down(tile + 1)))
+            wait(fetch_down(tile))
+            slot = lax.rem(tile, 2)
+            refs.grad_hidden[...] = three_pass(
+                (high_ref[...], low_ref[...]), (down_buf[slot, 0], down_buf[slot, 1]), 1, 0
             )
-            sized(tile, lambda size: fetch_down(tile, size).wait())
-            weight = halves(jnp.transpose(down_buf[lax.rem(tile, 2)]))
-
-            def strip(index, spot):
-                refs.grad_hidden[spot, :] = three_pass(
-                    (high_ref[spot, :], low_ref[spot, :]), weight, 1, 0
-                )
-                pause(index)
-
-            strips(rows, strip)
 
         @pl.when(step == steps - 1)
         def _():
+            total.back()
+            total.finish()
             residual = refs.tokens_in[...] + sum_ref[...]
             refs.residual[...] = residual
             refs.normed_two[...] = residual * rms(residual) * refs.second_gain[...]
@@ -1211,9 +1306,12 @@
             first_gain=(first_gain[None], WHOLE),
             group_gain=(group_gain[None], WHOLE),
             second_gain=(second_gain[None], WHOLE),
-            out_weight=(out_weight, ANY),
-            w_down=(w_down, ANY),
             **{f"weight_{index}": (weight, ANY) for index, weight in enumerate(in_weights)},
+            **{
+                f"{name}_{half}": (split[f"{name}_{half}"], ANY)
+                for name in ("out", "turned")
+                for half in ("high", "low")
+            },
         ),
         dict(
             all_cotangent=((rows, inner), ANY),
@@ -1234,10 +1332,11 @@
             weights=[
                 pltpu.VMEM((2, inner, TILE), F32),
                 pltpu.SemaphoreType.DMA((2,)),
-                pltpu.VMEM(out_weight.shape, F32),
-                pltpu.SemaphoreType.DMA((1,)),
-                pltpu.VMEM((2, TILE, inner), F32),
+                pltpu.VMEM((2, 2, inner, TILE), BF16),
+                pltpu.SemaphoreType.DMA((2, 2)),
+                pltpu.VMEM((2, *split.out_high.shape), BF16),
                 pltpu.SemaphoreType.DMA((2,)),
+                pltpu.VMEM((2, inner, TILE), BF16),
             ],
             state=[pltpu.VMEM((heads, HDIM, HDIM), F32)],
             swap=[pltpu.VMEM((own_rows, TILE), F32), *dma_sems(1)],
@@ -1255,58 +1354,204 @@
     )
 
 
-def feed_forward_kernel(
-    normed_two, residual, cotangent, grad_hidden, w_gate, w_up, w_down, out_weight, second_gain, collective_id
-):
+def feed_forward_kernel(normed_two, all_cotangent, grad_hidden, split, collective_id):
     rows, inner = normed_two.shape
-    columns = w_gate.shape[1]
-    tiles = pl.cdiv(columns, TILE)
+    token_count = all_cotangent.shape[0]
+    columns = split.gate_high.shape[1]
+    tiles = columns // TILE
 
     def body(refs, step):
         gather = Gather([refs.normed_two], [refs.all_normed_two], refs.gather)
-        part_ref, sum_ref, *sum_scratch = refs.sum
-        total = Sum([part_ref], [sum_ref], sum_scratch)
-        out_buf, out_sem = refs.out
-        fetch_out = pltpu.make_async_copy(refs.out_weight, out_buf, out_sem.at[0])
-        events = gather.events()
-
-        def pause(part):
-            schedule(step * 2 + part, (0, 1, 2, 3, 4, 5, 7, 9), events[:8])
+        high_ref, low_ref, stage_ref, stage_sem = refs.halves
+        (e_ref,) = refs.e
+        load = partial(load_halves, refs.all_cotangent, high_ref, low_ref, stage_ref, stage_sem)
 
         @pl.when(step == 0)
         def _():
             gather.begin()
-            fetch_out.start()
+            load(split=False)
             refs.ffn[...] = jnp.zeros_like(refs.ffn)
-            part_ref[...] = jnp.zeros_like(part_ref)
-
-        def inside(shape, axis):
-            return step * TILE + lax.broadcasted_iota(jnp.int32, shape, axis) < columns
-
-        gate_weight = halves(jnp.where(inside((inner, TILE), 1), refs.w_gate[...], 0.0))
-        up_weight = halves(jnp.where(inside((inner, TILE), 1), refs.w_up[...], 0.0))
+            refs.grad[...] = jnp.zeros_like(refs.grad)
+
+        pl.when(step == EARLY - 1)(lambda: load(start=False))
+
+        def both(name):
+            return refs[f"{name}_high"][...], refs[f"{name}_low"][...]
+
+        @pl.when(step < EARLY)
+        def _():
+            e_ref[...] = refs.early[...]
+
+        @pl.when(step >= EARLY)
+        def _():
+            refs.late[...] = three_pass((high_ref[...], low_ref[...]), both("turned"), 1, 0)
+            row = pl.multiple_of(lax.axis_index("seq") * rows, rows)
+            e_ref[...] = refs.late[pl.ds(row, rows), :]
+
+        moments = (1, 3, 4, 5, 6, 7, 7, 8, 9, 10, 11)
+        schedule(2 * step, moments, gather.events())
         normed = halves(refs.normed_two[...])
-        a = few_rows(normed, gate_weight, 0)
-        b = few_rows(normed, up_weight, 0)
-        pause(0)
-        e = jnp.where(inside((rows, TILE), 1), refs.grad_hidden[...], 0.0)
+        a = few_rows(normed, both("gate"), 0)
+        b = few_rows(normed, both("up"), 0)
+        e = e_ref[...]
         gate = jax.nn.sigmoid(a)
         silu_a = a * gate
-        down_weight = halves(jnp.where(inside((TILE, inner), 0), refs.w_down[...], 0.0))
-        refs.ffn[...] += few_rows(halves(silu_a * b), down_weight, 0)
-        part_ref[...] += few_rows(
-            halves(e * b * (gate * (1.0 + a * (1.0 - gate)))), gate_weight, 1
-        ) + few_rows(halves(e * silu_a), up_weight, 1)
-        pause(1)
-
-        @pl.when(step == tiles - 1)
-        def _():
-            total.begin()
-            total.to_y()
-            events[8]()
-            events[9]()
-            total.back()
-            gather.finish()
+        refs.ffn[...] += few_rows(halves(silu_a * b), both("down"), 0)
+        refs.grad[...] += few_rows(
+            halves(e * b * (gate * (1.0 + a * (1.0 - gate)))), both("gate"), 1
+        ) + few_rows(halves(e * silu_a), both("up"), 1)
+        schedule(2 * step + 1, moments, gather.events())
+
+    by_column = pl.BlockSpec((inner, TILE), lambda step: (0, step))
+    return fused(
+        dict(
+            normed_two=(normed_two, WHOLE),
+            all_cotangent=(all_cotangent, ANY),
+            early=(
+                grad_hidden,
+                pl.BlockSpec(
+                    (rows, TILE), lambda step: (lax.axis_index("seq"), jnp.minimum(step, EARLY - 1))
+                ),
+            ),
+            **{
+                f"{name}_{half}": (split[f"{name}_{half}"], spec)
+                for name, spec in (
+                    ("gate", by_column),
+                    ("up", by_column),
+                    ("down", pl.BlockSpec((TILE, inner), lambda step: (step, 0))),
+                    (
+                        "turned",
+                        pl.BlockSpec((inner, TILE), lambda step: (0, jnp.maximum(step, EARLY))),
+                    ),
+                )
+                for half in ("high", "low")
+            },
+        ),
+        dict(
+            all_normed_two=Gather.results([normed_two])[0],
+            ffn=((rows, inner), WHOLE),
+            grad=((rows, inner), WHOLE),
+            late=(
+                (token_count, columns - EARLY * TILE),
+                pl.BlockSpec((token_count, TILE), lambda step: (0, jnp.maximum(step - EARLY, 0))),
+            ),
+        ),
+        dict(
+            gather=Gather.scratch([normed_two]),
+            halves=halves_scratch(token_count, inner),
+            e=[pltpu.VMEM((rows, TILE), F32)],
+        ),
+        tiles,
+        body,
+        collective_id,
+        flops=30 * rows * inner * columns,
+    )
+
+
+SHARES = 2
+
+
+def tile_share(refs, share, tile):
+    high_ref, low_ref, cols_high_ref, cols_low_ref, cot_high_ref, cot_low_ref = refs.halves
+    size = high_ref.shape[0] // SHARES
+    spot = pl.ds(pl.multiple_of(share * size, size), size)
+    normed = high_ref[spot, :], low_ref[spot, :]
+    a = three_pass(normed, (refs.gate_high[...], refs.gate_low[...]), 1, 0)
+    b = three_pass(normed, (refs.up_high[...], refs.up_low[...]), 1, 0)
+    gate = jax.nn.sigmoid(a)
+    silu_a = a * gate
+    e = jnp.where(tile < EARLY, refs.early[spot, :], refs.late[spot, :])
+    cols = cols_high_ref[:, spot], cols_low_ref[:, spot]
+    cot = cot_high_ref[spot, :], cot_low_ref[spot, :]
+    grads = (
+        three_pass(cols, halves(e * b * (gate * (1.0 + a * (1.0 - gate)))), 1, 0),
+        three_pass(cols, halves(e * silu_a), 1, 0),
+        three_pass(halves(jnp.transpose(silu_a * b)), cot, 1, 0),
+    )
+    for ref, grad in zip((refs.grad_gate, refs.grad_up, refs.grad_down), grads, strict=True):
+        ref[...] = jnp.where(share == 0, 0.0, ref[...]) + grad
+
+
+def tile_columns(refs):
+    cols_high_ref, cols_low_ref, cot_high_ref, cot_low_ref = refs.halves[2:]
+    cols_high_ref[...], cols_low_ref[...] = halves(jnp.transpose(refs.normed_cols[...]))
+    cot_high_ref[...], cot_low_ref[...] = halves(refs.cot_cols[...])
+
+
+def tile_parts(all_normed_two, all_cotangent, early, late, split, first, count, tile_of):
+    rows, inner = all_normed_two.shape
+    narrow = inner // (Z * X)
+    columns = count * TILE
+    own_columns = pl.BlockSpec((rows, narrow), lambda step: (0, lax.axis_index("seq")))
+    by_column = pl.BlockSpec((inner, TILE), lambda step: (0, first + tile_of(step)))
+    grad_spec = pl.BlockSpec((narrow, TILE), lambda step: (0, tile_of(step)))
+    arrays = dict(
+        early=(
+            early,
+            pl.BlockSpec((rows, TILE), lambda step: (0, jnp.minimum(first + tile_of(step), EARLY - 1))),
+        ),
+        late=(
+            late,
+            pl.BlockSpec(
+                (rows, TILE), lambda step: (0, jnp.maximum(first + tile_of(step) - EARLY, 0))
+            ),
+        ),
+        **{
+            f"{name}_{half}": (split[f"{name}_{half}"], by_column)
+            for name in ("gate", "up")
+            for half in ("high", "low")
+        },
+        normed_cols=(all_normed_two, own_columns),
+        cot_cols=(all_cotangent, own_columns),
+    )
+    results = dict(
+        grad_gate=((narrow, columns), grad_spec),
+        grad_up=((narrow, columns), grad_spec),
+        grad_down=(
+            (columns, narrow), pl.BlockSpec((TILE, narrow), lambda step: (tile_of(step), 0))
+        ),
+    )
+    scratch = dict(
+        halves=[
+            pltpu.VMEM((rows, inner), BF16),
+            pltpu.VMEM((rows, inner), BF16),
+            pltpu.VMEM((narrow, rows), BF16),
+            pltpu.VMEM((narrow, rows), BF16),
+            pltpu.VMEM((rows, narrow), BF16),
+            pltpu.VMEM((rows, narrow), BF16),
+        ]
+    )
+    return arrays, results, scratch
+
+
+def residual_kernel(
+    part, ffn, residual, cotangent, second_gain, split, all_normed_two, tiles, count, collective_id
+):
+    arrays, results, scratch = tiles(lambda step: step // SHARES)
+    rows, inner = all_normed_two.shape
+    own_rows = part.shape[0]
+    out_shape = split.out_high.shape
+    grad_like = jax.ShapeDtypeStruct((own_rows, out_shape[0]), F32)
+
+    def body(refs, step):
+        sum_ref, *sum_scratch = refs.sum
+        grad_mixer_ref, *heads_scratch = refs.heads
+        total = Sum([refs.part], [sum_ref], sum_scratch)
+        heads = Heads([grad_mixer_ref], [refs.all_grad_mixer], heads_scratch)
+        scatter = Scatter([refs.ffn], [refs.ffn_share], refs.scatter)
+        high_ref, low_ref = refs.halves[:2]
+        stage_ref, stage_sem, out_sem = refs.stage
+        out_buf, out_buf_sem = refs.out
+        keep = [
+            pltpu.make_async_copy(high_ref, refs.normed_high, out_sem.at[0]),
+            pltpu.make_async_copy(low_ref, refs.normed_low, out_sem.at[1]),
+        ]
+        fetch_out = [
+            pltpu.make_async_copy(refs[f"out_{half}"], out_buf.at[at], out_buf_sem.at[at])
+            for at, half in enumerate(("high", "low"))
+        ]
+
+        def to_heads():
             total.finish()
             residual_here = refs.residual[...]
             scale = rms(residual_here)
@@ -1322,158 +1567,77 @@
             refs.second[...] = jnp.broadcast_to(
                 jnp.sum(summed * residual_here * scale, 0, keepdims=True), refs.second.shape
             )
-            fetch_out.wait()
-            refs.grad_mixer[...] = few_rows(halves(grad_residual), halves(out_buf[...]), 1)
-
-    by_column = pl.BlockSpec((inner, TILE), lambda step: (0, step))
+            for copy in fetch_out:
+                copy.wait()
+            grad_mixer_ref[...] = few_rows(halves(grad_residual), (out_buf[0], out_buf[1]), 1)
+            heads.begin()
+
+        @pl.when(step == 0)
+        def _():
+            total.begin()
+            for copy in fetch_out:
+                copy.start()
+            load_halves(refs.all_normed_two, high_ref, low_ref, stage_ref, stage_sem)
+            total.to_y()
+            for copy in keep:
+                copy.start()
+            tile_columns(refs)
+
+        tile_share(refs, lax.rem(step, SHARES), step // SHARES)
+        schedule(step, (1, 2, 3, 5, 6, 8), [total.back, to_heads, *heads.events()])
+        schedule(step, (3, 4, 6), [scatter.begin, *scatter.events()])
+
+        @pl.when(step == count * SHARES - 1)
+        def _():
+            for copy in keep:
+                copy.wait()
+
     return fused(
         dict(
-            normed_two=(normed_two, WHOLE),
+            part=(part, WHOLE),
+            ffn=(ffn, WHOLE),
             residual=(residual, WHOLE),
             cotangent=(cotangent, WHOLE),
-            grad_hidden=(
-                grad_hidden,
-                pl.BlockSpec((rows, TILE), lambda step: (lax.axis_index("seq"), step)),
-            ),
-            w_gate=(w_gate, by_column),
-            w_up=(w_up, by_column),
-            w_down=(w_down, pl.BlockSpec((TILE, inner), lambda step: (step, 0))),
-            out_weight=(out_weight, ANY),
             second_gain=(second_gain[None], WHOLE),
+            out_high=(split.out_high, ANY),
+            out_low=(split.out_low, ANY),
+            all_normed_two=(all_normed_two, ANY),
+            **arrays,
         ),
         dict(
-            all_normed_two=Gather.results([normed_two])[0],
-            ffn=((rows, inner), WHOLE),
-            grad_residual=((rows, inner), WHOLE),
-            grad_mixer=((rows, out_weight.shape[0]), WHOLE),
+            all_grad_mixer=Heads.results([grad_like])[0],
+            ffn_share=Scatter.results([ffn])[0],
+            grad_residual=((own_rows, inner), WHOLE),
             second=((8, inner), WHOLE),
+            normed_high=((rows, inner), ANY, BF16),
+            normed_low=((rows, inner), ANY, BF16),
+            **results,
         ),
         dict(
-            gather=Gather.scratch([normed_two]),
-            sum=[
-                pltpu.VMEM((rows, inner), F32),
-                pltpu.VMEM((rows, inner), F32),
-                *Sum.scratch([normed_two]),
-            ],
-            out=[pltpu.VMEM(out_weight.shape, F32), pltpu.SemaphoreType.DMA((1,))],
+            sum=[pltpu.VMEM((own_rows, inner), F32), *Sum.scratch([part])],
+            heads=[pltpu.VMEM(grad_like.shape, F32), *Heads.scratch([grad_like])],
+            scatter=Scatter.scratch([ffn]),
+            stage=[*halves_scratch(rows, inner)[2:], pltpu.SemaphoreType.DMA((2,))],
+            out=[pltpu.VMEM((2, *out_shape), BF16), pltpu.SemaphoreType.DMA((2,))],
+            **scratch,
         ),
-        tiles,
+        count * SHARES,
         body,
         collective_id,
-        flops=30 * rows * inner * columns,
-    )
-
-
-def tile_strips(refs, step, first_step, pause):
-    high_ref, low_ref, stage_ref, stage_sem, cols_high_ref, cols_low_ref = refs.halves
-    grads = refs.grad_gate, refs.grad_up, refs.grad_down
-
-    @pl.when(step == first_step)
-    def _():
-        load_halves(refs.all_normed_two, high_ref, low_ref, stage_ref, stage_sem)
-        cols_high_ref[...], cols_low_ref[...] = halves(jnp.transpose(refs.normed_cols[...]))
-
-    gate_weight, up_weight = halves(refs.w_gate[...]), halves(refs.w_up[...])
-    for grad_ref in grads:
-        grad_ref[...] = jnp.zeros_like(grad_ref)
-
-    def strip(index, spot):
-        normed = high_ref[spot, :], low_ref[spot, :]
-        a = three_pass(normed, gate_weight, 1, 0)
-        b = three_pass(normed, up_weight, 1, 0)
-        gate = jax.nn.sigmoid(a)
-        silu_a = a * gate
-        e = refs.grad_hidden[spot, :]
-        cols = cols_high_ref[:, spot], cols_low_ref[:, spot]
-        grads[0][...] += three_pass(cols, halves(e * b * (gate * (1.0 + a * (1.0 - gate)))), 1, 0)
-        grads[1][...] += three_pass(cols, halves(e * silu_a), 1, 0)
-        grads[2][...] += three_pass(
-            halves(jnp.transpose(silu_a * b)), halves(refs.cot_cols[spot, :]), 1, 0
-        )
-        pause(index)
-
-    strips(refs.all_normed_two.shape[0], strip)
-
-
-def tile_parts(all_normed_two, all_cotangent, grad_hidden, w_gate, w_up, first, count, tile_of):
-    rows, inner = all_normed_two.shape
-    narrow = inner // (Z * X)
-    columns = min(count * TILE, w_gate.shape[1] - first * TILE)
-    own_columns = pl.BlockSpec((rows, narrow), lambda step: (0, lax.axis_index("seq")))
-    by_column = pl.BlockSpec((inner, TILE), lambda step: (0, first + tile_of(step)))
-    grad_spec = pl.BlockSpec((narrow, TILE), lambda step: (0, tile_of(step)))
-    arrays = dict(
-        all_normed_two=(all_normed_two, ANY),
-        grad_hidden=(
-            grad_hidden, pl.BlockSpec((rows, TILE), lambda step: (0, first + tile_of(step)))
-        ),
-        w_gate=(w_gate, by_column),
-        w_up=(w_up, by_column),
-        normed_cols=(all_normed_two, own_columns),
-        cot_cols=(all_cotangent, own_columns),
-    )
-    results = dict(
-        grad_gate=((narrow, columns), grad_spec),
-        grad_up=((narrow, columns), grad_spec),
-        grad_down=(
-            (columns, narrow), pl.BlockSpec((TILE, narrow), lambda step: (tile_of(step), 0))
-        ),
-    )
-    scratch = dict(
-        halves=[
-            *halves_scratch(rows, inner),
-            pltpu.VMEM((narrow, rows), BF16),
-            pltpu.VMEM((narrow, rows), BF16),
-        ]
-    )
-    return arrays, results, scratch
-
-
-def heads_kernel(grad_mixer, ffn, tiles, count, collective_id):
-    arrays, results, scratch = tiles(lambda step: step)
-    parts = arrays["all_normed_two"][0].shape[0] // STRIP
-
-    def body(refs, step):
-        heads = Heads([refs.grad_mixer], [refs.all_grad_mixer], refs.heads)
-        scatter = Scatter([refs.ffn], [refs.ffn_share], refs.scatter)
-
-        @pl.when(step == 0)
-        def _():
-            heads.begin()
-            scatter.begin()
-
-        def pause(part):
-            now = step * parts + part
-            schedule(now, (0, 2, 4, 6), heads.events())
-            schedule(now, (1, 5), scatter.events())
-
-        tile_strips(refs, step, 0, pause)
-
-    return fused(
-        dict(grad_mixer=(grad_mixer, ANY), ffn=(ffn, WHOLE), **arrays),
-        dict(
-            all_grad_mixer=Heads.results([grad_mixer])[0],
-            ffn_share=Scatter.results([ffn])[0],
-            **results,
-        ),
-        dict(heads=Heads.scratch([grad_mixer]), scatter=Scatter.scratch([ffn]), **scratch),
-        count,
-        body,
-        collective_id,
-    )
-
-
-def last_kernel(grads, group, blocks, first_part, in_weights, tiles, count, collective_id):
+    )
+
+
+def last_kernel(
+    grads, group, blocks, first_part, in_weights, normed_high, normed_low, tiles, count, collective_id
+):
     arrays, results, scratch = tiles(
-        lambda step: jnp.where(step == 0, 0, jnp.maximum(step - len(in_weights), 0))
+        lambda step: jnp.where(step < SHARES, 0, jnp.maximum(step - 4, 0) // SHARES)
     )
     rows, columns = grads.shape
     own_rows = rows // (Z * X)
-    inner = in_weights[0].shape[0]
-    width = in_weights[0].shape[1]
+    inner, width = in_weights[0].shape
     half = width // X
-    matrices = len(in_weights)
-    parts = rows // STRIP
+    matrices = 4
     part_like = jax.ShapeDtypeStruct((own_rows, inner), F32)
     swapped = [jax.ShapeDtypeStruct((own_rows, columns), F32), group]
 
@@ -1483,7 +1647,7 @@
         peer = pl.multiple_of((place + 1 - 2 * x) * own_rows, own_rows)
         other_ref, *swap_scratch = refs.swap
         part_ref, *scatter_scratch = refs.scatter
-        weight_buf, weight_sem = refs.weights
+        weight_buf, weight_sem, load_sem = refs.weights
         swap = SwapX(
             [refs.grads.at[pl.ds(peer, own_rows), :], refs.group],
             [other_ref, refs.other_group],
@@ -1500,42 +1664,55 @@
         def fetch(index):
             return block_fetch(refs[f"weight_{index}"], weight_buf, weight_sem, index % 2)
 
+        load = [
+            pltpu.make_async_copy(refs[f"normed_{name}"], refs.halves[at], load_sem.at[at])
+            for at, name in enumerate(("high", "low"))
+        ]
+
         @pl.when(step == 0)
         def _():
+            for copy in load:
+                copy.start()
             swap.begin()
             sums.begin()
             part_ref[...] = jnp.zeros_like(part_ref)
-
-        def pause(part):
-            now = step * parts + part
-            schedule(now, (0, 1, 2), sums.events())
-            schedule(now, (4 * matrices + 4, 4 * matrices + 7), scatter.events())
-
-        @pl.when((step == 0) | (step > matrices))
+            for copy in load:
+                copy.wait()
+            for index in range(2):
+                fetch(index).start()
+
+        @pl.when(step == 1)
         def _():
-            tile_strips(refs, step, 0, pause)
-
+            swap.finish()
+            blocks_here.begin()
+
+        pl.when(step == 0)(lambda: tile_columns(refs))
+
+        @pl.when((step < SHARES) | (step >= matrices + SHARES))
+        def _():
+            tile_share(refs, lax.rem(step, SHARES), EARLY)
+
+        schedule(step, (0, 1, 2), sums.events())
         for index in range(matrices):
 
-            @pl.when(step == index)
+            @pl.when(step == index + SHARES)
             def _(index=index):
-                fetch(index).start()
-
-            @pl.when(step == index + 1)
-            def _(index=index):
-                if index == 0:
-                    swap.finish()
-                    blocks_here.begin()
                 fetch(index).wait()
                 weight = halves(weight_buf[index % 2])
+                if index + 2 < matrices:
+                    fetch(index + 2).start()
                 own = refs.own_grads[:, index * half : (index + 1) * half]
                 other = other_ref[:, index * half : (index + 1) * half]
                 low_x, high_x = (jnp.where(x == place_x, own, other) for place_x in range(X))
                 part_ref[...] += few_rows(halves(jnp.concatenate([low_x, high_x], 1)), weight, 1)
-                if index == matrices - 1:
-                    scatter.begin()
-
-        pl.when(step == matrices + count - 1)(blocks_here.finish)
+
+        @pl.when(step == matrices + count * SHARES - 1)
+        def _():
+            scatter.begin()
+            scatter.middle()
+            scatter.finish()
+            blocks_here.finish()
+
 
     return fused(
         dict(
@@ -1547,6 +1724,8 @@
             first_part=(first_part, WHOLE),
             **{f"block_{index}": (block, ANY) for index, block in enumerate(blocks)},
             **{f"weight_{index}": (weight, ANY) for index, weight in enumerate(in_weights)},
+            normed_high=(normed_high, ANY),
+            normed_low=(normed_low, ANY),
             **arrays,
         ),
         dict(
@@ -1563,10 +1742,14 @@
             scatter=[pltpu.VMEM((own_rows, inner), F32), *Scatter.scratch([part_like])],
             blocks=SwapBlocks.scratch(blocks),
             sums=SumAll.scratch([first_part]),
-            weights=[pltpu.VMEM((2, inner, width), F32), pltpu.SemaphoreType.DMA((2,))],
+            weights=[
+                pltpu.VMEM((2, inner, width), F32),
+                pltpu.SemaphoreType.DMA((2,)),
+                pltpu.SemaphoreType.DMA((2,)),
+            ],
             **scratch,
         ),
-        count + matrices,
+        count * SHARES + matrices,
         body,
         collective_id,
     )
@@ -1791,8 +1974,8 @@
             high, low = halves(total)
             refs.sums[...] = product(ones, high, 1, 1) + product(ones, low, 1, 1)
 
-        schedule(step, (0, 2, 4, 6, 7, 7), move.events())
-        schedule(step, (0, 2, 4, 6, 7, 7), small.events())
+        schedule(step, (0, 1, 2, 4, 6, 7), small.events())
+        schedule(step, (0, 2, 3, 5, 7, 7), move.events())
 
     def by_chunk(size):
         return pl.BlockSpec((CHUNK, size), lambda step: (chunks - 1 - step, 0))
@@ -1869,34 +2052,23 @@
         return cut(entries, lax.axis_index("mp"), share_rows, 0)
 
     in_weights = (query_weight, forget_weight, input_weight, gate_weight)
-    all_tokens = gather_tokens_fast(tokens_in, 1)
+    split = first_kernel(tokens_in, out_weight, swiglu_gate, swiglu_up, swiglu_down, 1)
     mixed = mixer_kernel(
-        all_tokens,
+        split.all,
         tokens_in,
         cotangent,
         lengths,
         lower_bound,
         in_weights,
-        out_weight,
-        swiglu_down,
+        split,
         first_gain,
         group_gain,
         second_gain,
         2,
     )
     fed = feed_forward_kernel(
-        mixed.normed_two,
-        mixed.residual,
-        cotangent,
-        mixed.grad_hidden,
-        swiglu_gate,
-        swiglu_up,
-        swiglu_down,
-        out_weight,
-        second_gain,
-        3,
-    )
-    grad_residual = fed.grad_residual
+        mixed.normed_two, mixed.all_cotangent, mixed.grad_hidden, split, 3
+    )
 
     def tiles(first, count):
         return partial(
@@ -1904,15 +2076,27 @@
             fed.all_normed_two,
             mixed.all_cotangent,
             mixed.grad_hidden,
-            swiglu_gate,
-            swiglu_up,
+            fed.late,
+            split,
             first,
             count,
         )
 
-    split = 3
-    left = pl.cdiv(swiglu_gate.shape[1], TILE) - split
-    sent = heads_kernel(fed.grad_mixer, fed.ffn, tiles(0, split), split, 4)
+    early = 5
+    late = pl.cdiv(swiglu_gate.shape[1], TILE) - early
+    sent = residual_kernel(
+        fed.grad,
+        fed.ffn,
+        mixed.residual,
+        cotangent,
+        second_gain,
+        split,
+        fed.all_normed_two,
+        tiles(0, early),
+        early,
+        4,
+    )
+    grad_residual = sent.grad_residual
     output = share(mixed.residual) + sent.ffn_share
     back = backward_kernel(
         mixed.projected,
@@ -1921,7 +2105,7 @@
         sent.all_grad_mixer,
         mixed.normed_cols,
         grad_residual,
-        fed.second,
+        sent.second,
         in_weights,
         lower_bound,
         group_gain,
@@ -1936,8 +2120,10 @@
         [*(back[f"block_{index}"] for index in range(4)), out_block],
         jnp.concatenate([back.sums[:, :narrow], back.sums[:, narrow:]]),
         in_weights,
-        tiles(split, left),
-        left,
+        sent.normed_high,
+        sent.normed_low,
+        tiles(early, late),
+        late,
         6,
     )
     grad_group = in_order(x == 0, back.group[0], last.other_group[0], 0)
@@ -1946,8 +2132,9 @@
         for index in range(5)
     )
     grad_normed_one, first_sum = last.share, last.first_sum
+    rest = swiglu_gate.shape[1] - early * TILE
     grad_sgate, grad_sup, grad_sdown = (
-        jnp.concatenate([sent[name], last[name]], axis)
+        jnp.concatenate([sent[name], lax.slice_in_dim(last[name], 0, rest, axis=axis)], axis)
         for name, axis in (("grad_gate", 1), ("grad_up", 1), ("grad_down", 0))
     )
     tokens_share = share(tokens_in)

time: 392 us -> 383 us (0.977)
  Pallas kernels: 367 us -> 356 us
    pallas_call x6, Pallas kernels: 367 us -> 356 us  [fused(): pl.pallas_call(kernel, grid=(steps,), out_shape=[jax.ShapeDtypeStruct(res...]
where the time goes in v5:
time: 383 us; the launch traced here: 377 us
  Pallas kernels  356 us (93%)
  other arithmetic  10.9 us (3%)
  local copies, waits for them, and re-layouts  5.56 us (1%)
  matrix products  4.21 us (1%)
    pallas_call x6, Pallas kernels, fused(): pl.pallas_call(kernel, grid=(steps,), out_shape=[jax.ShapeDtypeStruct(res...  356 us

profile of v5, /device:TPU:8, one launch (start us, length us, event | category | flops | bytes accessed | tf_op | source)
XLA Modules:
  0.0 377.5 jit_solution(15338244850531277564)
XLA Ops:
  0.6 53.5 %shard_map.246 = (f32[1024,2048]{1,0:T(8,128)}, bf16[2048,1536]{1,0:T(8,128)(2,1)}, bf16[2048,1536]{1,0:T(8,128)(2,1)}, bf16[512,2048]{1,0:T(8,128)(2,1)}, bf16[...) custom-call(f32[128,2048]{1,0:T(8,128)} %refs_2_.3, ...), custom_call_target="tpu_custom_call" | custom-call | bytes 33554432 | tf_op jit(solution)/shard_map/pallas_call | solution.py:976
  54.2 77.1 %shard_map.247 = (f32[1024,2048]{1,0:T(8,128)}, f32[1024,1024]{1,0:T(8,128)}, f32[1024,512]{1,0:T(8,128)}, f32[1024,256]{1,0:T(8,128)}, f32[1024,256]{1,0:T(8,12...) custom-call(s32[4]{0:T(128)} %refs_0_.5, ...), custom_call_target="tpu_custom_call" | custom-call | flops 22548578304 | bytes 33554432 | tf_op jit(solution)/shard_map/pallas_call | solution.py:976
  131.2 54.0 %shard_map.248 = (f32[1024,2048]{1,0:T(8,128)}, f32[128,2048]{1,0:T(8,128)}, f32[128,2048]{1,0:T(8,128)}, f32[1024,768]{1,0:T(8,128)}) custom-call(f32[128,2048]{1,0:T(8,128)} %get-tuple-element.72.refs_0_, f32[1024,2048]{1,0:T(8,128)} %get-tuple-element.73.refs_1_.refs_15_.refs_22_, f32[1024,768]{1,0:T(8,128)} %get-tuple-element.74.refs_2_.refs_8_.refs_15_, ...), custom_call_target="tpu_custom_call" | custom-call | flops 12079595520 | bytes 33554432 | tf_op jit(solution)/shard_map/pallas_call | solution.py:976
  185.2 74.5 %shard_map.249 = (f32[1024,256]{1,0:T(8,128)}, f32[32,2048]{1,0:T(8,128)}, f32[128,2048]{1,0:T(8,128)}, f32[8,2048]{1,0:T(8,128)}, bf16[1024,2048]{1,0:T(8,128)(...) custom-call(f32[128,2048]{1,0:T(8,128)} %get-tuple-element.81.refs_0_, ...), custom_call_target="tpu_custom_call" | custom-call | bytes 33554432 | tf_op jit(solution)/shard_map/pallas_call | solution.py:976
  259.7 0.0 copy-start.4
  259.7 35.1 %shard_map.250 = (f32[1024,1024]{1,0:T(8,128)}, f32[1,256]{1,0:T(1,128)}, f32[8,512]{1,0:T(8,128)}, f32[4,2,128,512]{3,2,1,0:T(8,128)}, f32[4,2,8,512]{3,2,1,0:T...) custom-call(s32[4]{0:T(128)} %refs_0_.5, ...), custom_call_target="tpu_custom_call" | custom-call | flops 5234491392 | bytes 33554432 | tf_op jit(solution)/shard_map/pallas_call | solution.py:976
  294.8 0.0 copy-start.15
  294.8 0.0 copy-start.16
  294.9 0.0 copy-done.4
  294.9 4.2 %fusion.1.refs_8_ = f32[512,256]{1,0:T(8,128)} fusion(f32[1024,512]{1,0:T(8,128)} %bitcast.32, f32[1024,256]{1,0:T(8,128)S(1)} %copy-done.4), kind=kOutput, calls=%fused_computation.30 | convolution fusion | flops 805306368 | bytes 3670016 | tf_op jit(solution)/shard_map/dot_general | solution.py:19
  299.1 0.0 copy-done.15
  299.1 0.6 pad_maximum_fusion.7.refs_3_
  299.7 0.0 copy-done.16
  299.7 0.6 broadcast_in_dim.30.refs_2_
  300.3 0.0 copy-start.1
  300.3 61.4 %shard_map.251 = (f32[8,256]{1,0:T(8,128)}, f32[32,2048]{1,0:T(8,128)}, f32[8,256]{1,0:T(8,128)}, f32[2,256,256]{2,1,0:T(8,128)}, f32[2,256,256]{2,1,0:T(8,128)}...) custom-call(f32[1024,1024]{1,0:T(8,128)} %get-tuple-element.93.refs_, ...), custom_call_target="tpu_custom_call" | custom-call | bytes 33554432 | tf_op jit(solution)/shard_map/pallas_call | solution.py:976
  361.7 0.0 copy-start.13
  361.7 0.0 copy-start.12
  361.7 0.0 copy-start.2
  361.7 0.8 slice.70
  362.6 0.0 copy-start.3
  362.6 0.6 dynamic_slice.22
  363.2 0.9 slice.68
  364.1 0.0 copy-done.1
  364.1 1.2 pad_maximum_fusion.2
  365.3 0.0 copy-done.13
  365.3 0.0 copy-start.9
  365.3 0.0 copy-start.10
  365.3 0.0 copy-done.12
  365.3 0.0 copy-done.2
  365.3 0.0 copy-done.3
  365.3 1.9 pad_maximum_fusion
  367.3 0.0 copy-start.7
  367.3 0.0 copy-start.8
  367.3 0.0 copy-done.9
  367.3 0.0 copy-done.10
  367.3 0.1 slice_bitcast_fusion.1
  367.4 0.1 maximum_bitcast_fusion
  367.4 0.0 copy-start.6
  367.5 1.0 copy.28
  368.5 0.9 pad_maximum_fusion.6
  369.3 0.0 copy-done.7
  369.3 0.0 copy-done.8
  369.3 0.0 copy-start
  369.3 0.0 copy-start.5
  369.3 0.0 copy-start.14
  369.3 0.0 copy-start.11
  369.4 0.1 slice_bitcast_fusion.5
  369.4 0.9 pad_maximum_fusion.5
  370.3 0.9 pad_maximum_fusion.4
  371.2 0.0 copy-done.6
  371.2 0.9 pad_maximum_fusion.3
  372.1 0.0 copy-done
  372.1 0.0 copy-done.5
  372.1 0.0 copy-done.14
  372.1 0.2 multiply_reduce_fusion.1
  372.2 0.0 copy-done.11
  372.3 1.9 multiply_subtract_fusion
  374.1 0.7 slice.69
  374.8 0.6 dynamic-slice_divide_fusion
  375.5 0.9 slice_reduce_fusion
  376.4 0.6 dynamic_slice.23
  (7 shorter events, 0.1 us)
Async XLA Ops:
  259.7 35.1 %copy-start.4 = (f32[1024,256]{1,0:T(8,128)S(1)}, f32[1024,256]{1,0:T(8,128)}, u32[]{:S(2)}) copy-start(f32[1024,256]{1,0:T(8,128)} %get-tuple-element.101) | copy-start | bytes 3145732
  294.8 4.2 %copy-start.15 = (f32[8,512]{1,0:T(8,128)S(1)}, f32[8,512]{1,0:T(8,128)}, u32[]{:S(2)}) copy-start(f32[8,512]{1,0:T(8,128)} %get-tuple-element.95) | copy-start | bytes 49156
  294.8 4.8 %copy-start.16 = (f32[1,256]{1,0:T(1,128)S(1)}, f32[1,256]{1,0:T(1,128)}, u32[]{:S(2)}) copy-start(f32[1,256]{1,0:T(1,128)} %get-tuple-element.94) | copy-start | bytes 3076
  300.3 63.8 %copy-start.1 = (f32[1280,256]{1,0:T(8,128)S(1)}, f32[1280,256]{1,0:T(8,128)}, u32[]{:S(2)}) copy-start(f32[1280,256]{1,0:T(8,128)} %get-tuple-element.114) | copy-start | bytes 3932164
  361.7 3.6 copy-start.13
  361.7 3.6 copy-start.12
  361.7 3.6 copy-start.2
  362.6 2.8 copy-start.3
  365.3 2.0 copy-start.9
  365.3 2.0 copy-start.10
  367.3 2.1 copy-start.7
  367.3 2.1 copy-start.8
  367.4 3.7 copy-start.6
  369.3 2.7 copy-start
  369.3 2.7 copy-start.5
  369.3 2.7 copy-start.14
  369.3 2.9 copy-start.11

commit v6 on v5

--- a/solution.py
+++ b/solution.py
@@ -871,34 +871,29 @@
         return [ANY] * len(arrays)
 
     def results(arrays):
-        return [((X, array.shape[0] // X, array.shape[1]), ANY) for array in arrays]
+        return [((array.shape[0] // X, array.shape[1]), ANY) for array in arrays]
 
     def scratch(arrays):
-        return [*dma_sems(len(arrays)), pltpu.SemaphoreType.DMA((len(arrays),))]
-
-    def setup(self):
-        self.sems, self.local = self.scratch_refs[:2], self.scratch_refs[2]
-
-    def ends(self, index, x):
-        src, dst = self.ins[index], self.outs[index]
+        return dma_sems(len(arrays))
+
+    def send(self, index):
+        src = self.ins[index]
         rows = src.shape[0] // X
-        return src.at[pl.ds(pl.multiple_of(x * rows, rows), rows), :], dst.at[self.x]
-
-    def send(self, index):
-        return remote(*self.ends(index, 1 - self.x), self.sems, index, self.x_peer())
-
-    def keep(self, index):
-        return pltpu.make_async_copy(*self.ends(index, self.x), self.local.at[index])
+        return remote(
+            src.at[pl.ds(pl.multiple_of((1 - self.x) * rows, rows), rows), :],
+            self.outs[index],
+            self.scratch_refs,
+            index,
+            self.x_peer(),
+        )
 
     def begin(self):
         for index in range(len(self.ins)):
             self.send(index).start()
-            self.keep(index).start()
 
     def finish(self):
         for index in range(len(self.ins)):
             self.send(index).wait()
-            self.keep(index).wait()
 
     def events(self):
         return [self.finish]
@@ -1056,7 +1051,7 @@
         )
     return fused(
         dict(
-            block=(block, ANY),
+            block=(block, WHOLE),
             gate=(w_gate, by_rows(SPLIT_ROWS, columns)),
             up=(w_up, by_rows(SPLIT_ROWS, columns)),
             down=(w_down, by_rows(SPLIT_ROWS, inner, pl.cdiv(columns, SPLIT_ROWS) - 1)),
@@ -1301,7 +1296,7 @@
             lengths=(lengths, pl.BlockSpec(memory_space=pltpu.SMEM)),
             tokens=(all_tokens, ANY),
             tokens_in=(tokens_in, WHOLE),
-            cotangent=(cotangent, ANY),
+            cotangent=(cotangent, WHOLE),
             lower_bound=(lower_bound[None], WHOLE),
             first_gain=(first_gain[None], WHOLE),
             group_gain=(group_gain[None], WHOLE),
@@ -1584,7 +1579,7 @@
             tile_columns(refs)
 
         tile_share(refs, lax.rem(step, SHARES), step // SHARES)
-        schedule(step, (1, 2, 3, 5, 6, 8), [total.back, to_heads, *heads.events()])
+        schedule(step, (1, 2, 3, 5, 6, 7), [total.back, to_heads, *heads.events()])
         schedule(step, (3, 4, 6), [scatter.begin, *scatter.events()])
 
         @pl.when(step == count * SHARES - 1)
@@ -1693,6 +1688,7 @@
             tile_share(refs, lax.rem(step, SHARES), EARLY)
 
         schedule(step, (0, 1, 2), sums.events())
+        pl.when(step == matrices + SHARES)(scatter.middle)
         for index in range(matrices):
 
             @pl.when(step == index + SHARES)
@@ -1705,11 +1701,11 @@
                 other = other_ref[:, index * half : (index + 1) * half]
                 low_x, high_x = (jnp.where(x == place_x, own, other) for place_x in range(X))
                 part_ref[...] += few_rows(halves(jnp.concatenate([low_x, high_x], 1)), weight, 1)
+                if index == matrices - 1:
+                    scatter.begin()
 
         @pl.when(step == matrices + count * SHARES - 1)
         def _():
-            scatter.begin()
-            scatter.middle()
             scatter.finish()
             blocks_here.finish()
 
@@ -1993,8 +1989,8 @@
             normed_cols=(normed_cols, by_chunk(wide)),
             lower_bound=(lower_bound[None], WHOLE),
             group_gain=(group_gain[None], WHOLE),
-            grad_residual=(grad_residual, ANY),
-            second=(second, ANY),
+            grad_residual=(grad_residual, WHOLE),
+            second=(second, WHOLE),
             **{f"weight_{index}": (weight, ANY) for index, weight in enumerate(weights)},
         ),
         dict(
@@ -2082,7 +2078,7 @@
             count,
         )
 
-    early = 5
+    early = 4
     late = pl.cdiv(swiglu_gate.shape[1], TILE) - early
     sent = residual_kernel(
         fed.grad,
@@ -2114,10 +2110,11 @@
     )
     second_cols = jnp.sum(back.second_cols[:, :, 0], (0, 1))
     out_block = dot(back.residual_cols.reshape(token_count, wide), mixed.mixer, 0, 0)
+    blocks = [*(back[f"block_{index}"] for index in range(4)), out_block]
     last = last_kernel(
         back.grads,
         jnp.broadcast_to(back.group, (8, width)),
-        [*(back[f"block_{index}"] for index in range(4)), out_block],
+        blocks,
         jnp.concatenate([back.sums[:, :narrow], back.sums[:, narrow:]]),
         in_weights,
         sent.normed_high,
@@ -2128,8 +2125,8 @@
     )
     grad_group = in_order(x == 0, back.group[0], last.other_group[0], 0)
     *weight_grads, grad_outw = (
-        jnp.concatenate([last[f"swapped_{index}"][0], last[f"swapped_{index}"][1]], 1)
-        for index in range(5)
+        in_order(x == 0, cut(block, x, narrow, 0), last[f"swapped_{index}"], 1)
+        for index, block in enumerate(blocks)
     )
     grad_normed_one, first_sum = last.share, last.first_sum
     rest = swiglu_gate.shape[1] - early * TILE

time: 383 us -> 371 us (0.969)
  Pallas kernels: 356 us -> 337 us
  other arithmetic: 10.9 us -> 15.2 us
    pallas_call x6, Pallas kernels: 356 us -> 337 us  [fused(): pl.pallas_call(kernel, grid=(steps,), out_shape=[jax.ShapeDtypeStruct(res...]
    select_n x1 -> x5, other arithmetic: 0.01 us -> 5.5 us  [in_order(): jnp.where(first, jnp.concatenate([mine, other], axis), jnp.concatenate([o...]
where the time goes in v6:
time: 371 us; the launch traced here: 367 us
  Pallas kernels  337 us (91%)
  other arithmetic  15.2 us (4%)
  local copies, waits for them, and re-layouts  9.02 us (2%)
  matrix products  4.21 us (1%)
    pallas_call x6, Pallas kernels, fused(): pl.pallas_call(kernel, grid=(steps,), out_shape=[jax.ShapeDtypeStruct(res...  337 us

profile of v6, /device:TPU:8, one launch (start us, length us, event | category | flops | bytes accessed | tf_op | source)
XLA Modules:
  0.0 366.7 jit_solution(8846079660561031063)
XLA Ops:
  0.6 54.1 %shard_map.246 = (f32[1024,2048]{1,0:T(8,128)}, bf16[2048,1536]{1,0:T(8,128)(2,1)}, bf16[2048,1536]{1,0:T(8,128)(2,1)}, bf16[512,2048]{1,0:T(8,128)(2,1)}, bf16[...) custom-call(f32[128,2048]{1,0:T(8,128)} %refs_2_.3, ...), custom_call_target="tpu_custom_call" | custom-call | bytes 33554432 | tf_op jit(solution)/shard_map/pallas_call | solution.py:971
  54.7 77.8 %shard_map.247 = (f32[1024,2048]{1,0:T(8,128)}, f32[1024,1024]{1,0:T(8,128)}, f32[1024,512]{1,0:T(8,128)}, f32[1024,256]{1,0:T(8,128)}, f32[1024,256]{1,0:T(8,12...) custom-call(s32[4]{0:T(128)} %refs_0_.5, ...), custom_call_target="tpu_custom_call" | custom-call | flops 22548578304 | bytes 33554432 | tf_op jit(solution)/shard_map/pallas_call | solution.py:971
  132.5 54.0 %shard_map.248 = (f32[1024,2048]{1,0:T(8,128)}, f32[128,2048]{1,0:T(8,128)}, f32[128,2048]{1,0:T(8,128)}, f32[1024,768]{1,0:T(8,128)}) custom-call(f32[128,2048]{1,0:T(8,128)} %get-tuple-element.72.refs_0_, f32[1024,2048]{1,0:T(8,128)} %get-tuple-element.73.refs_1_.refs_15_.refs_22_, f32[1024,768]{1,0:T(8,128)} %get-tuple-element.74.refs_2_.refs_8_.refs_15_, ...), custom_call_target="tpu_custom_call" | custom-call | flops 12079595520 | bytes 33554432 | tf_op jit(solution)/shard_map/pallas_call | solution.py:971
  186.5 64.4 %shard_map.249 = (f32[1024,256]{1,0:T(8,128)}, f32[32,2048]{1,0:T(8,128)}, f32[128,2048]{1,0:T(8,128)}, f32[8,2048]{1,0:T(8,128)}, bf16[1024,2048]{1,0:T(8,128)(...) custom-call(f32[128,2048]{1,0:T(8,128)} %get-tuple-element.81.refs_0_, ...), custom_call_target="tpu_custom_call" | custom-call | bytes 33554432 | tf_op jit(solution)/shard_map/pallas_call | solution.py:971
  250.9 0.0 copy-start.5
  250.9 35.3 %shard_map.250 = (f32[1024,1024]{1,0:T(8,128)}, f32[1,256]{1,0:T(1,128)}, f32[8,512]{1,0:T(8,128)}, f32[4,2,128,512]{3,2,1,0:T(8,128)}, f32[4,2,8,512]{3,2,1,0:T...) custom-call(s32[4]{0:T(128)} %refs_0_.5, ...), custom_call_target="tpu_custom_call" | custom-call | flops 5234491392 | bytes 33554432 | tf_op jit(solution)/shard_map/pallas_call | solution.py:971
  286.2 0.0 copy-done.5
  286.2 4.2 %fusion.2.refs_8_ = f32[512,256]{1,0:T(8,128)} fusion(f32[1024,512]{1,0:T(8,128)} %bitcast.12, f32[1024,256]{1,0:T(8,128)S(1)} %copy-done.5), kind=kOutput, calls=%fused_computation.26 | convolution fusion | flops 805306368 | bytes 3670016 | tf_op jit(solution)/shard_map/dot_general | solution.py:19
  290.5 0.7 fusion.1
  291.2 0.6 pad_maximum_fusion.3.refs_3_
  291.8 1.3 broadcast_in_dim.30.refs_2_
  293.0 0.0 copy-start.14
  293.1 0.0 copy-start.8
  293.1 51.5 %shard_map.251 = (f32[8,256]{1,0:T(8,128)}, f32[32,2048]{1,0:T(8,128)}, f32[8,256]{1,0:T(8,128)}, f32[256,256]{1,0:T(8,128)}, f32[256,256]{1,0:T(8,128)}, /*inde...) custom-call(f32[1024,1024]{1,0:T(8,128)} %get-tuple-element.93.refs_, ...), custom_call_target="tpu_custom_call" | custom-call | bytes 33554432 | tf_op jit(solution)/shard_map/pallas_call | solution.py:971
  344.5 0.0 copy-start.9
  344.5 0.0 copy-start.7
  344.5 0.8 slice.30
  345.4 0.0 copy-done.14
  345.4 0.6 dynamic_slice.42
  346.0 1.0 slice.28
  347.0 0.0 copy-done.8
  347.0 1.2 pad_maximum_fusion.2
  348.2 0.0 copy-start
  348.2 1.1 slice.26
  349.3 0.0 copy-done.9
  349.3 0.0 copy-done.7
  349.3 0.0 copy-start.4
  349.3 3.0 pad_maximum_fusion
  352.4 0.0 copy-start.2
  352.4 0.0 copy-start.3
  352.4 0.0 copy-done
  352.4 0.0 copy-start.1
  352.4 0.0 copy-start.6
  352.4 0.0 copy-start.13
  352.5 1.2 fusion
  353.7 1.0 copy.30
  354.7 0.0 copy-done.4
  354.7 0.0 copy-start.12
  354.7 0.0 copy-start.11
  354.7 1.0 constant_dynamic-slice_fusion.1
  355.8 0.0 copy-start.10
  355.8 1.9 maximum_select_fusion.3
  357.7 1.9 maximum_select_fusion.2
  359.6 0.0 copy-done.2
  359.6 0.0 copy-done.3
  359.6 0.0 copy-done.12
  359.6 0.8 maximum_select_fusion.1
  360.5 0.0 copy-done.11
  360.5 0.8 maximum_select_fusion
  361.3 0.0 copy-done.1
  361.3 0.0 copy-done.6
  361.3 0.0 copy-done.13
  361.3 0.2 multiply_reduce_fusion.1
  361.5 0.0 copy-done.10
  361.5 1.9 multiply_subtract_fusion
  363.4 0.7 slice.29
  364.1 0.6 dynamic-slice_divide_fusion
  364.7 0.9 slice_reduce_fusion
  365.7 0.6 dynamic_slice.43
  (6 shorter events, 0.1 us)
Async XLA Ops:
  250.9 35.4 %copy-start.5 = (f32[1024,256]{1,0:T(8,128)S(1)}, f32[1024,256]{1,0:T(8,128)}, u32[]{:S(2)}) copy-start(f32[1024,256]{1,0:T(8,128)} %get-tuple-element.101) | copy-start | bytes 3145732
  293.0 52.3 %copy-start.14 = (f32[1,256]{1,0:T(1,128)S(1)}, f32[1,256]{1,0:T(1,128)}, u32[]{:S(2)}) copy-start(f32[1,256]{1,0:T(1,128)} %get-tuple-element.94) | copy-start | bytes 3076
  293.1 53.9 %copy-start.8 = (f32[1024,256]{1,0:T(8,128)S(1)}, f32[1024,256]{1,0:T(8,128)}, u32[]{:S(2)}) copy-start(f32[1024,256]{1,0:T(8,128)} %get-tuple-element.114) | copy-start | bytes 3145732
  344.5 4.8 %copy-start.9 = (f32[256,512]{1,0:T(8,128)S(1)}, f32[256,512]{1,0:T(8,128)}, u32[]{:S(2)}) copy-start(f32[256,512]{1,0:T(8,128)} %get-tuple-element.113) | copy-start | bytes 1572868
  344.5 4.8 %copy-start.7 = (f32[256,1024]{1,0:T(8,128)S(1)}, f32[256,1024]{1,0:T(8,128)}, u32[]{:S(2)}) copy-start(f32[256,1024]{1,0:T(8,128)} %get-tuple-element.110) | copy-start | bytes 3145732
  348.2 4.2 %copy-start = (f32[512,256]{1,0:T(8,128)S(1)}, f32[512,256]{1,0:T(8,128)}, u32[]{:S(2)}) copy-start(f32[512,256]{1,0:T(8,128)} %fusion.2.refs_8_) | copy-start | bytes 1572868
  349.3 5.4 %copy-start.4 = (f32[512,256]{1,0:T(8,128)S(1)}, f32[512,256]{1,0:T(8,128)}, u32[]{:S(2)}) copy-start(f32[512,256]{1,0:T(8,128)} %get-tuple-element.98.refs_6_) | copy-start | bytes 1572868
  352.4 7.2 %copy-start.2 = (f32[512,256]{1,0:T(8,128)S(1)}, f32[512,256]{1,0:T(8,128)}, u32[]{:S(2)}) copy-start(f32[512,256]{1,0:T(8,128)} %get-tuple-element.96.refs_4_) | copy-start | bytes 1572868
  352.4 7.2 %copy-start.3 = (f32[512,256]{1,0:T(8,128)S(1)}, f32[512,256]{1,0:T(8,128)}, u32[]{:S(2)}) copy-start(f32[512,256]{1,0:T(8,128)} %get-tuple-element.97.refs_5_) | copy-start | bytes 1572868
  352.4 8.9 %copy-start.1 = (f32[128,2048]{1,0:T(8,128)S(1)}, f32[128,2048]{1,0:T(8,128)}, u32[]{:S(2)}) copy-start(f32[128,2048]{1,0:T(8,128)} %refs_2_.3) | copy-start | bytes 3145732
  352.4 8.9 %copy-start.6 = (f32[32,2048]{1,0:T(8,128)S(1)}, f32[32,2048]{1,0:T(8,128)}, u32[]{:S(2)}) copy-start(f32[32,2048]{1,0:T(8,128)} %get-tuple-element.104) | copy-start | bytes 786436
  352.4 8.9 %copy-start.13 = (f32[2048]{0:T(1024)S(1)}, f32[2048]{0:T(1024)}, u32[]{:S(2)}) copy-start(f32[2048]{0:T(1024)} %param.27) | copy-start | bytes 24580
  354.7 4.9 %copy-start.12 = (f32[256,256]{1,0:T(8,128)S(1)}, f32[256,256]{1,0:T(8,128)}, u32[]{:S(2)}) copy-start(f32[256,256]{1,0:T(8,128)} %get-tuple-element.106) | copy-start | bytes 786436
  354.7 5.8 %copy-start.11 = (f32[256,256]{1,0:T(8,128)S(1)}, f32[256,256]{1,0:T(8,128)}, u32[]{:S(2)}) copy-start(f32[256,256]{1,0:T(8,128)} %get-tuple-element.105) | copy-start | bytes 786436
  355.8 5.8 %copy-start.10 = (f32[32,2048]{1,0:T(8,128)S(1)}, f32[32,2048]{1,0:T(8,128)}, u32[]{:S(2)}) copy-start(f32[32,2048]{1,0:T(8,128)} %get-tuple-element.85) | copy-start | bytes 786436

commit v7 on v6

--- a/solution.py
+++ b/solution.py
@@ -1473,10 +1473,10 @@
     cot_high_ref[...], cot_low_ref[...] = halves(refs.cot_cols[...])
 
 
-def tile_parts(all_normed_two, all_cotangent, early, late, split, first, count, tile_of):
+def tile_parts(all_normed_two, all_cotangent, early, late, split, columns, first, count, tile_of):
     rows, inner = all_normed_two.shape
     narrow = inner // (Z * X)
-    columns = count * TILE
+    columns = min(count * TILE, columns - first * TILE)
     own_columns = pl.BlockSpec((rows, narrow), lambda step: (0, lax.axis_index("seq")))
     by_column = pl.BlockSpec((inner, TILE), lambda step: (0, first + tile_of(step)))
     grad_spec = pl.BlockSpec((narrow, TILE), lambda step: (0, tile_of(step)))
@@ -1968,7 +1968,11 @@
                 total = total + weight_buf[index] * block_refs[index][...]
             ones = jnp.ones((8, width), BF16)
             high, low = halves(total)
-            refs.sums[...] = product(ones, high, 1, 1) + product(ones, low, 1, 1)
+            sums = product(ones, high, 1, 1) + product(ones, low, 1, 1)
+            for index in range(X):
+                refs.sums[index * 8 : (index + 1) * 8, :] = sums[
+                    :, index * wide // X : (index + 1) * wide // X
+                ]
 
         schedule(step, (0, 1, 2, 4, 6, 7), small.events())
         schedule(step, (0, 2, 3, 5, 7, 7), move.events())
@@ -1995,8 +1999,8 @@
         ),
         dict(
             grads=((rows, columns), by_chunk(columns)),
-            group=((1, width), WHOLE),
-            sums=((8, wide), WHOLE),
+            group=((8, width), WHOLE),
+            sums=((X * 8, wide // X), WHOLE),
             residual_cols=Columns.results([grad_residual])[0],
             second_cols=Columns.results([second])[0],
             **{f"block_{index}": ((wide, width), WHOLE) for index in range(count)},
@@ -2074,6 +2078,7 @@
             mixed.grad_hidden,
             fed.late,
             split,
+            swiglu_gate.shape[1],
             first,
             count,
         )
@@ -2113,9 +2118,9 @@
     blocks = [*(back[f"block_{index}"] for index in range(4)), out_block]
     last = last_kernel(
         back.grads,
-        jnp.broadcast_to(back.group, (8, width)),
+        back.group,
         blocks,
-        jnp.concatenate([back.sums[:, :narrow], back.sums[:, narrow:]]),
+        back.sums,
         in_weights,
         sent.normed_high,
         sent.normed_low,
@@ -2129,9 +2134,8 @@
         for index, block in enumerate(blocks)
     )
     grad_normed_one, first_sum = last.share, last.first_sum
-    rest = swiglu_gate.shape[1] - early * TILE
     grad_sgate, grad_sup, grad_sdown = (
-        jnp.concatenate([sent[name], lax.slice_in_dim(last[name], 0, rest, axis=axis)], axis)
+        jnp.concatenate([sent[name], last[name]], axis)
         for name, axis in (("grad_gate", 1), ("grad_up", 1), ("grad_down", 0))
     )
     tokens_share = share(tokens_in)

time: 371 us -> 368 us (level)
  no operation moved by 1% of the time
where the time goes in v7:
time: 368 us; the launch traced here: 364 us
  Pallas kernels  337 us (92%)
  other arithmetic  15.9 us (4%)
  local copies, waits for them, and re-layouts  5.47 us (1%)
  matrix products  4.21 us (1%)
    pallas_call x6, Pallas kernels, fused(): pl.pallas_call(kernel, grid=(steps,), out_shape=[jax.ShapeDtypeStruct(res...  337 us

profile of v7, /device:TPU:8, one launch (start us, length us, event | category | flops | bytes accessed | tf_op | source)
XLA Modules:
  0.0 364.0 jit_solution(2705522605267193098)
XLA Ops:
  0.6 54.1 %shard_map.246 = (f32[1024,2048]{1,0:T(8,128)}, bf16[2048,1536]{1,0:T(8,128)(2,1)}, bf16[2048,1536]{1,0:T(8,128)(2,1)}, bf16[512,2048]{1,0:T(8,128)(2,1)}, bf16[...) custom-call(f32[128,2048]{1,0:T(8,128)} %refs_2_.3, ...), custom_call_target="tpu_custom_call" | custom-call | bytes 33554432 | tf_op jit(solution)/shard_map/pallas_call | solution.py:971
  54.7 77.8 %shard_map.247 = (f32[1024,2048]{1,0:T(8,128)}, f32[1024,1024]{1,0:T(8,128)}, f32[1024,512]{1,0:T(8,128)}, f32[1024,256]{1,0:T(8,128)}, f32[1024,256]{1,0:T(8,12...) custom-call(s32[4]{0:T(128)} %refs_0_.5, ...), custom_call_target="tpu_custom_call" | custom-call | flops 22548578304 | bytes 33554432 | tf_op jit(solution)/shard_map/pallas_call | solution.py:971
  132.5 54.0 %shard_map.248 = (f32[1024,2048]{1,0:T(8,128)}, f32[128,2048]{1,0:T(8,128)}, f32[128,2048]{1,0:T(8,128)}, f32[1024,768]{1,0:T(8,128)}) custom-call(f32[128,2048]{1,0:T(8,128)} %get-tuple-element.72.refs_0_, f32[1024,2048]{1,0:T(8,128)} %get-tuple-element.73.refs_1_.refs_15_.refs_22_, f32[1024,768]{1,0:T(8,128)} %get-tuple-element.74.refs_2_.refs_8_.refs_15_, ...), custom_call_target="tpu_custom_call" | custom-call | flops 12079595520 | bytes 33554432 | tf_op jit(solution)/shard_map/pallas_call | solution.py:971
  186.5 64.5 %shard_map.249 = (f32[1024,256]{1,0:T(8,128)}, f32[32,2048]{1,0:T(8,128)}, f32[128,2048]{1,0:T(8,128)}, f32[8,2048]{1,0:T(8,128)}, bf16[1024,2048]{1,0:T(8,128)(...) custom-call(f32[128,2048]{1,0:T(8,128)} %get-tuple-element.81.refs_0_, ...), custom_call_target="tpu_custom_call" | custom-call | bytes 33554432 | tf_op jit(solution)/shard_map/pallas_call | solution.py:971
  251.0 0.0 copy-start.5
  251.0 35.3 %shard_map.250 = (f32[1024,1024]{1,0:T(8,128)}, f32[8,256]{1,0:T(8,128)}, f32[16,256]{1,0:T(8,128)}, f32[4,2,128,512]{3,2,1,0:T(8,128)}, f32[4,2,8,512]{3,2,1,0:...) custom-call(s32[4]{0:T(128)} %refs_0_.5, ...), custom_call_target="tpu_custom_call" | custom-call | flops 5234491392 | bytes 33554432 | tf_op jit(solution)/shard_map/pallas_call | solution.py:971
  286.4 0.0 copy-done.5
  286.4 4.2 %fusion.1.refs_8_ = f32[512,256]{1,0:T(8,128)} fusion(f32[1024,512]{1,0:T(8,128)} %bitcast.12, f32[1024,256]{1,0:T(8,128)S(1)} %copy-done.5), kind=kOutput, calls=%fused_computation.24 | convolution fusion | flops 805306368 | bytes 3670016 | tf_op jit(solution)/shard_map/dot_general | solution.py:19
  290.6 0.0 copy-start.7
  290.6 0.0 copy-start.8
  290.6 51.5 %shard_map.251 = (f32[8,256]{1,0:T(8,128)}, f32[32,2048]{1,0:T(8,128)}, f32[8,256]{1,0:T(8,128)}, f32[256,256]{1,0:T(8,128)}, f32[256,256]{1,0:T(8,128)}, /*inde...) custom-call(f32[1024,1024]{1,0:T(8,128)} %get-tuple-element.93.refs_, ...), custom_call_target="tpu_custom_call" | custom-call | bytes 33554432 | tf_op jit(solution)/shard_map/pallas_call | solution.py:971
  342.0 0.7 slice.14
  342.7 0.7 slice.13
  343.5 0.6 dynamic_slice.42
  344.0 0.0 copy-start
  344.0 2.6 pad_maximum_fusion.2
  346.6 0.0 copy-done.7
  346.6 0.0 copy-done.8
  346.6 0.0 copy-start.4
  346.6 3.0 pad_maximum_fusion
  349.6 0.0 copy-start.2
  349.6 0.0 copy-start.3
  349.6 0.0 copy-done
  349.7 0.0 copy-start.1
  349.7 0.0 copy-start.6
  349.7 0.0 copy-start.12
  349.7 1.2 fusion
  350.9 1.0 copy.30
  351.9 0.0 copy-done.4
  351.9 0.0 copy-start.11
  351.9 0.0 copy-start.10
  351.9 1.0 constant_dynamic-slice_fusion.1
  353.0 0.0 copy-start.9
  353.0 1.9 maximum_select_fusion.3
  354.9 1.9 maximum_select_fusion.2
  356.8 0.0 copy-done.2
  356.8 0.0 copy-done.3
  356.9 0.0 copy-done.11
  356.9 0.8 maximum_select_fusion.1
  357.7 0.0 copy-done.10
  357.7 0.8 maximum_select_fusion
  358.5 0.0 copy-done.1
  358.5 0.0 copy-done.6
  358.6 0.0 copy-done.12
  358.6 0.2 multiply_reduce_fusion.1
  358.7 0.0 copy-done.9
  358.7 1.9 multiply_subtract_fusion
  360.6 0.7 slice.12
  361.3 0.6 dynamic-slice_divide_fusion
  362.0 0.9 slice_reduce_fusion
  362.9 0.6 dynamic_slice.43
  (5 shorter events, 0.1 us)
Async XLA Ops:
  251.0 35.3 %copy-start.5 = (f32[1024,256]{1,0:T(8,128)S(1)}, f32[1024,256]{1,0:T(8,128)}, u32[]{:S(2)}) copy-start(f32[1024,256]{1,0:T(8,128)} %get-tuple-element.101) | copy-start | bytes 3145732
  290.6 56.1 %copy-start.7 = (f32[256,1024]{1,0:T(8,128)S(1)}, f32[256,1024]{1,0:T(8,128)}, u32[]{:S(2)}) copy-start(f32[256,1024]{1,0:T(8,128)} %get-tuple-element.110) | copy-start | bytes 3145732
  290.6 56.1 %copy-start.8 = (f32[256,1024]{1,0:T(8,128)S(1)}, f32[256,1024]{1,0:T(8,128)}, u32[]{:S(2)}) copy-start(f32[256,1024]{1,0:T(8,128)} %get-tuple-element.112) | copy-start | bytes 3145732
  344.0 5.6 %copy-start = (f32[512,256]{1,0:T(8,128)S(1)}, f32[512,256]{1,0:T(8,128)}, u32[]{:S(2)}) copy-start(f32[512,256]{1,0:T(8,128)} %fusion.1.refs_8_) | copy-start | bytes 1572868
  346.6 5.3 %copy-start.4 = (f32[512,256]{1,0:T(8,128)S(1)}, f32[512,256]{1,0:T(8,128)}, u32[]{:S(2)}) copy-start(f32[512,256]{1,0:T(8,128)} %get-tuple-element.98.refs_6_) | copy-start | bytes 1572868
  349.6 7.2 %copy-start.2 = (f32[512,256]{1,0:T(8,128)S(1)}, f32[512,256]{1,0:T(8,128)}, u32[]{:S(2)}) copy-start(f32[512,256]{1,0:T(8,128)} %get-tuple-element.96.refs_4_) | copy-start | bytes 1572868
  349.6 7.2 %copy-start.3 = (f32[512,256]{1,0:T(8,128)S(1)}, f32[512,256]{1,0:T(8,128)}, u32[]{:S(2)}) copy-start(f32[512,256]{1,0:T(8,128)} %get-tuple-element.97.refs_5_) | copy-start | bytes 1572868
  349.7 8.9 %copy-start.1 = (f32[128,2048]{1,0:T(8,128)S(1)}, f32[128,2048]{1,0:T(8,128)}, u32[]{:S(2)}) copy-start(f32[128,2048]{1,0:T(8,128)} %refs_2_.3) | copy-start | bytes 3145732
  349.7 8.9 %copy-start.6 = (f32[32,2048]{1,0:T(8,128)S(1)}, f32[32,2048]{1,0:T(8,128)}, u32[]{:S(2)}) copy-start(f32[32,2048]{1,0:T(8,128)} %get-tuple-element.104) | copy-start | bytes 786436
  349.7 8.9 %copy-start.12 = (f32[2048]{0:T(1024)S(1)}, f32[2048]{0:T(1024)}, u32[]{:S(2)}) copy-start(f32[2048]{0:T(1024)} %param.27) | copy-start | bytes 24580
  351.9 4.9 %copy-start.11 = (f32[256,256]{1,0:T(8,128)S(1)}, f32[256,256]{1,0:T(8,128)}, u32[]{:S(2)}) copy-start(f32[256,256]{1,0:T(8,128)} %get-tuple-element.106) | copy-start | bytes 786436
  351.9 5.8 %copy-start.10 = (f32[256,256]{1,0:T(8,128)S(1)}, f32[256,256]{1,0:T(8,128)}, u32[]{:S(2)}) copy-start(f32[256,256]{1,0:T(8,128)} %get-tuple-element.105) | copy-start | bytes 786436
  353.0 5.8 %copy-start.9 = (f32[32,2048]{1,0:T(8,128)S(1)}, f32[32,2048]{1,0:T(8,128)}, u32[]{:S(2)}) copy-start(f32[32,2048]{1,0:T(8,128)} %get-tuple-element.85) | copy-start | bytes 786436
